TPU v7x, 1024 devices: a whole 4x4x32 slice. The times are simulated.
1024 devices in a mesh: lat: 64 (over z, y_hi), rad: 16 (over x, y_lo, core).
Axes of the slice: x: 4, y: 4 (y_hi: 2, y_lo: 2; y = y_hi * 2 + y_lo), z: 32, core: 2. Of those that a mesh axis runs over, the one named last changes fastest.
Arguments:
- rhs_force: float32 [16, 65536], P('rad', 'lat'), may hold values from -96 to 96
- viscosity: float32 [16, 65536], P('rad', 'lat'), may hold values from 0.1 to 10
- initial_guess: float32 [16, 65536], P('rad', 'lat'), may hold values from -3 to 3
- glue_tile: int32 [64, 4], replicated, may hold values from 0 to 63, as said below
- glue_side: int32 [64, 4], replicated, may hold values from 0 to 3
- glue_flip: int32 [64, 4], replicated, may hold values from 0 to 1
Outputs:
- velocity: float32 [16, 65536], P('rad', 'lat')
Inputs may be any that keep to these rules, and one draw needn't show every extreme that they name: `glue_tile`: every side of every tile is glued to exactly one other side: if side s of tile a meets side t of tile b, then side t of tile b meets side s of tile a with the same glue_flip code.
All inputs are finite; a program needn't handle non-finite values.
Results may differ from a plain program's by a relative error of at most 0.0003.
Values sent between devices are 32-bit elements; how exact they have to be, the bound alone decides.
No kernel may reach another device: no remote copies, remote signals or barrier semaphores. Data moves between devices by JAX's collectives and lax.ppermute only.
A program may use at most 32 MiB of HBM per device.

v0:
```python
import jax
import jax.numpy as jnp
from jax import lax
from jax.sharding import PartitionSpec as P

C = 32
NEWTON = 2
CG_ITERS = 4


cubic_weight = 8.0
radial_weight = 4.0
relax_factor = 0.8


def padded_2(block, sides, width):
    for axis, dim in sides:
        count = lax.axis_size(axis)
        forward = [(i, i + 1) for i in range(count - 1)]
        backward = [(target, source) for source, target in forward]
        low = lax.ppermute(
            lax.slice_in_dim(block, block.shape[dim] - width, None, axis=dim), axis, forward
        )
        high = lax.ppermute(lax.slice_in_dim(block, 0, width, axis=dim), axis, backward)
        block = jnp.concatenate([low, block, high], axis=dim)
    return block


def tile_sides(values, width):
    cell_total = width * width
    return jnp.stack(
        [
            values[..., :width],
            values[..., cell_total - width :],
            values[..., ::width],
            values[..., width - 1 :: width],
        ],
        axis=-2,
    )


def table_ghosts(sides_all, gluing):
    glue_tile, glue_side, glue_flip = gluing
    picked = sides_all[:, glue_tile, glue_side, :]
    return jnp.where(glue_flip[None, :, :, None] == 1, picked[..., ::-1], picked)


def lateral_beside(values, ghost_rows, width):
    column = jnp.arange(width * width) % width
    zero_col = jnp.zeros(values.shape[:-1] + (1,), values.dtype)
    up_row = jnp.concatenate([ghost_rows[0], values[..., :-width]], axis=-1)
    down_row = jnp.concatenate([values[..., width:], ghost_rows[1]], axis=-1)
    left_col = jnp.where(
        column == 0,
        jnp.repeat(ghost_rows[2], width, axis=-1),
        jnp.concatenate([zero_col, values[..., :-1]], axis=-1),
    )
    right_col = jnp.where(
        column == width - 1,
        jnp.repeat(ghost_rows[3], width, axis=-1),
        jnp.concatenate([values[..., 1:], zero_col], axis=-1),
    )
    return (up_row, down_row, left_col, right_col)


def restrict(values, width):
    half = width // 2
    shaped = values.reshape(values.shape[:-1] + (half, 2, half, 2))
    return jnp.sum(shaped, axis=(-3, -1)).reshape(values.shape[:-1] + (half * half,))


def prolong(values, half):
    shaped = values.reshape(values.shape[:-1] + (half, 1, half, 1))
    spread = jnp.broadcast_to(shaped, values.shape[:-1] + (half, 2, half, 2))
    return spread.reshape(values.shape[:-1] + (4 * half * half,))


def fine_rows(values, width, my_tile, gluing):
    glue_tile, glue_side, glue_flip = gluing
    layers = values.shape[0]
    tile_count = glue_tile.shape[0]
    cell_total = width * width
    own_rows = jnp.stack(
        [
            values[:, :width],
            values[:, cell_total - width :],
            values[:, ::width],
            values[:, width - 1 :: width],
        ],
        axis=0,
    )
    my_flips = glue_flip[my_tile]
    sending = jnp.where(my_flips[:, None, None] == 1, own_rows[..., ::-1], own_rows)
    target = (jnp.arange(tile_count)[:, None, None] == glue_tile[my_tile][None, None, :]) & (
        jnp.arange(4)[None, :, None] == glue_side[my_tile][None, None, :]
    )
    slot_buffer = jnp.einsum(
        "bti,ilk->btlk", target.astype(jnp.float32), sending, precision=lax.Precision.HIGHEST
    )
    received = lax.all_to_all(
        slot_buffer.reshape(tile_count, 4 * layers * width),
        "lat",
        split_axis=0,
        concat_axis=0,
        tiled=True,
    )
    arrived = jnp.sum(received, axis=0).reshape(4, layers, width)
    return (arrived[0], arrived[1], arrived[2], arrived[3])


def fine_beside(values, width, my_tile, gluing):
    ghost_rows = fine_rows(values, width, my_tile, gluing)
    padded = padded_2(values, (("rad", 0),), 1)
    return lateral_beside(values, ghost_rows, width) + (padded[2:], padded[:-2])


def fine_apply(values, conds, diagonal, width, my_tile, gluing):
    beside = fine_beside(values, width, my_tile, gluing)
    coupled = (
        conds[0] * beside[0]
        + conds[1] * beside[1]
        + conds[2] * beside[2]
        + conds[3] * beside[3]
        + conds[4] * beside[4]
        + conds[5] * beside[5]
    )
    return diagonal * values - coupled


def coarse_faces(conds, layers, half):

    def shaped(values):
        return values.reshape(layers, half, 2, half, 2)

    north = jnp.sum(shaped(conds[0])[:, :, 0], axis=-1)
    south = jnp.sum(shaped(conds[1])[:, :, 1], axis=-1)
    west = jnp.sum(shaped(conds[2])[..., 0], axis=2)
    east = jnp.sum(shaped(conds[3])[..., 1], axis=2)
    upward = jnp.sum(shaped(conds[4]), axis=(2, 4))
    downward = jnp.sum(shaped(conds[5]), axis=(2, 4))
    faces = [north, south, west, east, upward, downward]
    return jnp.stack([face.reshape(layers, half * half) for face in faces])


def coarse_apply(values, coeffs, diagonal, half, gluing):
    ghosts = table_ghosts(tile_sides(values, half), gluing)
    ghost_rows = (ghosts[..., 0, :], ghosts[..., 1, :], ghosts[..., 2, :], ghosts[..., 3, :])
    padded = padded_2(values, (("rad", 0),), 1)
    beside = lateral_beside(values, ghost_rows, half) + (padded[2:], padded[:-2])
    coupled = (
        coeffs[0] * beside[0]
        + coeffs[1] * beside[1]
        + coeffs[2] * beside[2]
        + coeffs[3] * beside[3]
        + coeffs[4] * beside[4]
        + coeffs[5] * beside[5]
    )
    return diagonal * values - coupled


def radial_squares(values):
    return lax.psum(jnp.sum(values * values), "rad")


def radial_inner(first_vec, second_vec):
    return lax.psum(jnp.sum(first_vec * second_vec), "rad")


def coarse_solve(coarse_rhs, operator):
    solution = jnp.zeros_like(coarse_rhs)
    residual_c = coarse_rhs
    direction = coarse_rhs
    norm_now = radial_squares(residual_c)
    for cg_step in range(CG_ITERS):
        image_dir = operator(direction)
        step_size = norm_now / radial_inner(direction, image_dir)
        solution = solution + step_size * direction
        residual_c = residual_c - step_size * image_dir
        if cg_step + 1 < CG_ITERS:
            norm_next = radial_squares(residual_c)
            direction = residual_c + norm_next / norm_now * direction
            norm_now = norm_next
    return solution


def on_device(rhs_force, viscosity, initial_guess, glue_tile, glue_side, glue_flip):
    gluing = (glue_tile, glue_side, glue_flip)
    layers = rhs_force.shape[0]
    width = C
    half = width // 2
    tile_count = lax.axis_size("lat")
    my_tile = lax.axis_index("lat")
    beside = fine_beside(viscosity, width, my_tile, gluing)
    conds = [0.5 * (viscosity + other) for other in beside[:4]] + [
        radial_weight * 0.5 * (viscosity + other) for other in beside[4:]
    ]
    cond_total = conds[0] + conds[1] + conds[2] + conds[3] + conds[4] + conds[5]
    local_faces = coarse_faces(conds, layers, half)
    faces = lax.all_gather(local_faces, "lat", axis=2, tiled=True)
    faces = faces.reshape(6, layers, tile_count, half * half)
    face_total = faces[0] + faces[1] + faces[2] + faces[3] + faces[4] + faces[5]
    velocity = initial_guess
    for newton_step in range(NEWTON):
        cubic_term = cubic_weight * velocity * velocity
        damping = 3.0 * cubic_term
        residual = rhs_force - fine_apply(
            velocity, conds, cond_total + cubic_term, width, my_tile, gluing
        )
        diag_j = cond_total + damping
        smoothed = relax_factor * residual / diag_j
        remain = residual - fine_apply(smoothed, conds, diag_j, width, my_tile, gluing)
        coarse_local = jnp.stack([restrict(remain, width), restrict(damping, width)])
        collected = lax.all_gather(coarse_local, "lat", axis=2, tiled=True)
        collected = collected.reshape(2, layers, tile_count, half * half)
        coarse_diag = face_total + collected[1]

        def operator(values, coarse_diag=coarse_diag):
            return coarse_apply(values, faces, coarse_diag, half, gluing)

        solution = coarse_solve(collected[0], operator)
        own_part = lax.dynamic_index_in_dim(solution, my_tile, axis=1, keepdims=False)
        velocity = velocity + smoothed + prolong(own_part, half)
    return velocity


def solution(mesh):
    return jax.shard_map(
        on_device,
        mesh=mesh,
        in_specs=(P("rad", "lat"), P("rad", "lat"), P("rad", "lat"), P(), P(), P()),
        out_specs=P("rad", "lat"),
        check_vma=False,
    )
```

profile of v0, /device:TPU:1, one launch (start us, length us, event | category | flops | bytes accessed | tf_op | source)
XLA Modules:
  0.0 1124.1 jit_solution(14511460676575143738)
XLA Ops:
  0.0 16.2 %collective-permute-start = (f32[1,1024]{1,0:T(1,128)}, f32[1,1024]{1,0:T(1,128)S(1)}, u32[]{:S(2)}, u32[]{:S(2)}) collective-permute-start(f32[1,1024]{1,0:T(1,128)} %param.7), channel_id=1, source_target_pairs={{1,0},{2,1},{3,2},{4,3},{5,4},{6,5},{7,6},{8,7},{9,8},{10,9},{11,1... | collective-permute-start | bytes 12296 | tf_op jit(solution)/shard_map/ppermute | solution.py:24
  20.5 3.2 collective-permute-start.3
  28.7 20.1 %all-to-all-start.1 = ((f32[64,1,128]{2,1,0:T(1,128)}), f32[64,1,128]{2,1,0:T(1,128)S(1)}, u32[]{:S(2)}, u32[]{:S(2)}) async-start(f32[64,1,128]{2,1,0:T(1,128)} %copy.203), calls=%async_computation.1 | async-start | bytes 65536 | tf_op jit(solution)/shard_map/all_to_all | solution.py:100
  49.9 23.5 %all-to-all-done.1 = f32[64,1,128]{2,1,0:T(1,128)S(1)} async-done(((f32[64,1,128]{2,1,0:T(1,128)}), f32[64,1,128]{2,1,0:T(1,128)S(1)}, u32[]{:S(2)}, u32[]{:S(2)}) %all-to-all-start.1) | async-done | bytes 32800 | tf_op jit(solution)/shard_map/all_to_all | solution.py:100
  73.5 4.6 all-to-all-start
  78.8 23.6 %all-to-all-done = f32[64,1,128]{2,1,0:T(1,128)S(1)} async-done(((f32[64,1,128]{2,1,0:T(1,128)}), f32[64,1,128]{2,1,0:T(1,128)S(1)}, u32[]{:S(2)}, u32[]{:S(2)}) %all-to-all-start) | async-done | bytes 32800 | tf_op jit(solution)/shard_map/all_to_all | solution.py:100
  104.4 3.5 collective-permute-start.4
  115.6 4.6 all-to-all-start.2
  122.9 121.0 %all_gather.10 = f32[6,1,16384]{2,1,0:T(1,128)S(1)} all-gather(f32[6,1,256]{2,1,0:T(1,128)S(1)} %constant_dynamic-update-slice_fusion), channel_id=1, replica_groups=mesh['lat'=64,'rad'=16] {'lat'}, dimensions={2}, use_global_device_ids=true | all-gather | bytes 399360 | tf_op jit(solution)/shard_map/all_gather | solution.py:199
  246.1 113.7 %all_gather.9 = f32[2,1,16384]{2,1,0:T(1,128)S(1)} all-gather(f32[2,1,256]{2,1,0:T(1,128)S(1)} %pad_maximum_fusion.13), channel_id=1, replica_groups=mesh['lat'=64,'rad'=16] {'lat'}, dimensions={2}, use_global_device_ids=true | all-gather | bytes 133120 | tf_op jit(solution)/shard_map/all_gather | solution.py:213
  361.3 56.3 %collective-permute-start.7 = (f32[1,64,256]{2,1,0:T(8,128)S(1)}, f32[1,64,256]{2,1,0:T(8,128)S(1)}, u32[]{:S(2)}, u32[]{:S(2)}) collective-permute-start(f32[1,64,256]{2,1,0:T(8,128)S(1)} %squeeze.81), channel_id=1, source_target_pairs={{0,1},{1,2},{2,3},{3,4},{4,5},{5,6},{6,7},{7,8},{8,9},{9,10},{10,1... | collective-permute-start | bytes 196616 | tf_op jit(solution)/shard_map/ppermute | solution.py:21
  424.0 25.1 %all-reduce.17 = (f32[]{:T(128)}, f32[]{:T(128)}) all-reduce(f32[]{:T(128)} %get-tuple-element.14, f32[]{:T(128)} %get-tuple-element.40), channel_id=1, replica_groups=mesh['lat'=64,'rad'=16] {'rad'}, use_global_device_ids=true, to_apply=%region_6.7 | all-reduce | flops 2 | bytes 16 | tf_op jit(solution)/shard_map/psum | solution.py:162
  451.1 30.5 %psum.114 = f32[]{:T(128)} all-reduce(f32[]{:T(128)} %multiply_reduce_fusion.11), channel_id=1, replica_groups=mesh['lat'=64,'rad'=16] {'rad'}, use_global_device_ids=true, to_apply=%region_16.17 | all-reduce | flops 1 | bytes 8 | tf_op jit(solution)/shard_map/psum | solution.py:162
  492.1 26.5 %psum.115 = f32[]{:T(128)} all-reduce(f32[]{:T(128)} %get-tuple-element.38), channel_id=1, replica_groups=mesh['lat'=64,'rad'=16] {'rad'}, use_global_device_ids=true, to_apply=%region_18.19 | all-reduce | flops 1 | bytes 8 | tf_op jit(solution)/shard_map/psum | solution.py:166
  520.6 28.8 %psum.116 = f32[]{:T(128)} all-reduce(f32[]{:T(128)} %get-tuple-element.36), channel_id=1, replica_groups=mesh['lat'=64,'rad'=16] {'rad'}, use_global_device_ids=true, to_apply=%region_20.21 | all-reduce | flops 1 | bytes 8 | tf_op jit(solution)/shard_map/psum | solution.py:162
  559.6 25.5 %psum.117 = f32[]{:T(128)} all-reduce(f32[]{:T(128)} %get-tuple-element.34), channel_id=1, replica_groups=mesh['lat'=64,'rad'=16] {'rad'}, use_global_device_ids=true, to_apply=%region_22.23 | all-reduce | flops 1 | bytes 8 | tf_op jit(solution)/shard_map/psum | solution.py:166
  587.1 29.9 %psum.118 = f32[]{:T(128)} all-reduce(f32[]{:T(128)} %multiply_reduce_fusion.7), channel_id=1, replica_groups=mesh['lat'=64,'rad'=16] {'rad'}, use_global_device_ids=true, to_apply=%region_24.25 | all-reduce | flops 1 | bytes 8 | tf_op jit(solution)/shard_map/psum | solution.py:162
  627.5 26.5 %psum.119 = f32[]{:T(128)} all-reduce(f32[]{:T(128)} %fusion.51), channel_id=1, replica_groups=mesh['lat'=64,'rad'=16] {'rad'}, use_global_device_ids=true, to_apply=%region_26.27 | all-reduce | flops 1 | bytes 8 | tf_op jit(solution)/shard_map/psum | solution.py:166
  657.2 22.9 %all-to-all-start.3 = ((f32[64,1,128]{2,1,0:T(1,128)}), f32[64,1,128]{2,1,0:T(1,128)S(1)}, u32[]{:S(2)}, u32[]{:S(2)}) async-start(f32[64,1,128]{2,1,0:T(1,128)} %copy.235), calls=%async_computation.3 | async-start | bytes 65536 | tf_op jit(solution)/shard_map/all_to_all | solution.py:100
  680.2 3.9 collective-permute-start.14
  686.5 17.5 %all-to-all-done.3 = f32[64,1,128]{2,1,0:T(1,128)S(1)} async-done(((f32[64,1,128]{2,1,0:T(1,128)}), f32[64,1,128]{2,1,0:T(1,128)S(1)}, u32[]{:S(2)}, u32[]{:S(2)}) %all-to-all-start.3) | async-done | bytes 32800 | tf_op jit(solution)/shard_map/all_to_all | solution.py:100
  706.1 7.0 all-to-all-start.4
  718.9 18.3 %all-to-all-done.4 = f32[64,1,128]{2,1,0:T(1,128)S(1)} async-done(((f32[64,1,128]{2,1,0:T(1,128)}), f32[64,1,128]{2,1,0:T(1,128)S(1)}, u32[]{:S(2)}, u32[]{:S(2)}) %all-to-all-start.4) | async-done | bytes 32800 | tf_op jit(solution)/shard_map/all_to_all | solution.py:100
  738.2 113.7 %all_gather.11 = f32[2,1,16384]{2,1,0:T(1,128)S(1)} all-gather(f32[2,1,256]{2,1,0:T(1,128)S(1)} %pad_maximum_fusion.16), channel_id=1, replica_groups=mesh['lat'=64,'rad'=16] {'lat'}, dimensions={2}, use_global_device_ids=true | all-gather | bytes 133120 | tf_op jit(solution)/shard_map/all_gather | solution.py:213
  853.4 32.2 %collective-permute-start.19 = (f32[1,64,256]{2,1,0:T(8,128)S(1)}, f32[1,64,256]{2,1,0:T(8,128)S(1)}, u32[]{:S(2)}, u32[]{:S(2)}) collective-permute-start(f32[1,64,256]{2,1,0:T(8,128)S(1)} %squeeze.101), channel_id=1, source_target_pairs={{0,1},{1,2},{2,3},{3,4},{4,5},{5,6},{6,7},{7,8},{8,9},{9,10},{10,1... | collective-permute-start | bytes 196616 | tf_op jit(solution)/shard_map/ppermute | solution.py:21
  892.0 24.7 %all-reduce.16 = (f32[]{:T(128)}, f32[]{:T(128)}) all-reduce(f32[]{:T(128)} %get-tuple-element.11, f32[]{:T(128)} %get-tuple-element.27), channel_id=1, replica_groups=mesh['lat'=64,'rad'=16] {'rad'}, use_global_device_ids=true, to_apply=%region_32.33 | all-reduce | flops 2 | bytes 16 | tf_op jit(solution)/shard_map/psum | solution.py:162
  918.6 30.8 %psum.122 = f32[]{:T(128)} all-reduce(f32[]{:T(128)} %multiply_reduce_fusion.4), channel_id=1, replica_groups=mesh['lat'=64,'rad'=16] {'rad'}, use_global_device_ids=true, to_apply=%region_36.37 | all-reduce | flops 1 | bytes 8 | tf_op jit(solution)/shard_map/psum | solution.py:162
  959.8 26.5 %psum.123 = f32[]{:T(128)} all-reduce(f32[]{:T(128)} %get-tuple-element.25), channel_id=1, replica_groups=mesh['lat'=64,'rad'=16] {'rad'}, use_global_device_ids=true, to_apply=%region_38.39 | all-reduce | flops 1 | bytes 8 | tf_op jit(solution)/shard_map/psum | solution.py:166
  988.3 28.8 %psum.124 = f32[]{:T(128)} all-reduce(f32[]{:T(128)} %get-tuple-element.23), channel_id=1, replica_groups=mesh['lat'=64,'rad'=16] {'rad'}, use_global_device_ids=true, to_apply=%region_40.41 | all-reduce | flops 1 | bytes 8 | tf_op jit(solution)/shard_map/psum | solution.py:162
  1027.3 25.5 %psum.125 = f32[]{:T(128)} all-reduce(f32[]{:T(128)} %get-tuple-element.21), channel_id=1, replica_groups=mesh['lat'=64,'rad'=16] {'rad'}, use_global_device_ids=true, to_apply=%region_42.43 | all-reduce | flops 1 | bytes 8 | tf_op jit(solution)/shard_map/psum | solution.py:166
  1054.8 29.9 %psum.126 = f32[]{:T(128)} all-reduce(f32[]{:T(128)} %multiply_reduce_fusion), channel_id=1, replica_groups=mesh['lat'=64,'rad'=16] {'rad'}, use_global_device_ids=true, to_apply=%region_44.45 | all-reduce | flops 1 | bytes 8 | tf_op jit(solution)/shard_map/psum | solution.py:162
  1095.2 26.5 %psum.127 = f32[]{:T(128)} all-reduce(f32[]{:T(128)} %fusion.50), channel_id=1, replica_groups=mesh['lat'=64,'rad'=16] {'rad'}, use_global_device_ids=true, to_apply=%region_46.47 | all-reduce | flops 1 | bytes 8 | tf_op jit(solution)/shard_map/psum | solution.py:166
  (378 shorter events, 112.1 us)
Async XLA Ops:
  0.0 25.4 %copy-start = (f32[1,1024]{1,0:T(1,128)S(1)}, f32[1,1024]{1,0:T(1,128)}, u32[]{:S(2)}) copy-start(f32[1,1024]{1,0:T(1,128)} %param.8) | copy-start | bytes 12292
  0.0 103.2 %collective-permute-start = (f32[1,1024]{1,0:T(1,128)}, f32[1,1024]{1,0:T(1,128)S(1)}, u32[]{:S(2)}, u32[]{:S(2)}) collective-permute-start(f32[1,1024]{1,0:T(1,128)} %param.7), channel_id=1, source_target_pairs={{1,0},{2,1},{3,2},{4,3},{5,4},{6,5},{7,6},{8,7},{9,8},{10,9},{11,1... | collective-permute-start | bytes 12296 | tf_op jit(solution)/shard_map/ppermute | solution.py:24
  16.2 87.0 %collective-permute-start.1 = (f32[1,1024]{1,0:T(1,128)}, f32[1,1024]{1,0:T(1,128)S(1)}, u32[]{:S(2)}, u32[]{:S(2)}) collective-permute-start(f32[1,1024]{1,0:T(1,128)} %param.7), channel_id=1, source_target_pairs={{0,1},{1,2},{2,3},{3,4},{4,5},{5,6},{6,7},{7,8},{8,9},{9,10},{10,1... | collective-permute-start | bytes 12296 | tf_op jit(solution)/shard_map/ppermute | solution.py:21
  18.1 85.1 %collective-permute-start.2 = (f32[1,1024]{1,0:T(1,128)}, f32[1,1024]{1,0:T(1,128)S(1)}, u32[]{:S(2)}, u32[]{:S(2)}) collective-permute-start(f32[1,1024]{1,0:T(1,128)} %param.8), channel_id=1, source_target_pairs={{1,0},{2,1},{3,2},{4,3},{5,4},{6,5},{7,6},{8,7},{9,8},{10,9},{11,1... | collective-permute-start | bytes 12296 | tf_op jit(solution)/shard_map/ppermute | solution.py:24
  20.5 82.7 %collective-permute-start.3 = (f32[1,1024]{1,0:T(1,128)}, f32[1,1024]{1,0:T(1,128)S(1)}, u32[]{:S(2)}, u32[]{:S(2)}) collective-permute-start(f32[1,1024]{1,0:T(1,128)} %param.8), channel_id=1, source_target_pairs={{0,1},{1,2},{2,3},{3,4},{4,5},{5,6},{6,7},{7,8},{8,9},{9,10},{10,1... | collective-permute-start | bytes 12296 | tf_op jit(solution)/shard_map/ppermute | solution.py:21
  28.7 44.8 %all-to-all-start.1 = ((f32[64,1,128]{2,1,0:T(1,128)}), f32[64,1,128]{2,1,0:T(1,128)S(1)}, u32[]{:S(2)}, u32[]{:S(2)}) async-start(f32[64,1,128]{2,1,0:T(1,128)} %copy.203), calls=%async_computation.1 | async-start | bytes 65536 | tf_op jit(solution)/shard_map/all_to_all | solution.py:100
  73.5 28.9 %all-to-all-start = ((f32[64,1,128]{2,1,0:T(1,128)}), f32[64,1,128]{2,1,0:T(1,128)S(1)}, u32[]{:S(2)}, u32[]{:S(2)}) async-start(f32[64,1,128]{2,1,0:T(1,128)} %copy.202), calls=%async_computation | async-start | bytes 65536 | tf_op jit(solution)/shard_map/all_to_all | solution.py:100
  104.4 141.2 %collective-permute-start.4 = (f32[1,1024]{1,0:T(1,128)S(1)}, f32[1,1024]{1,0:T(1,128)S(1)}, u32[]{:S(2)}, u32[]{:S(2)}) collective-permute-start(f32[1,1024]{1,0:T(1,128)S(1)} %get-tuple-element.44), channel_id=1, source_target_pairs={{1,0},{2,1},{3,2},{4,3},{5,4},{6,5},{7,6},{8,7},{9,8},{10,9},{11,1... | collective-permute-start | bytes 12296 | tf_op jit(solution)/shard_map/ppermute | solution.py:24
  107.9 137.7 %collective-permute-start.5 = (f32[1,1024]{1,0:T(1,128)S(1)}, f32[1,1024]{1,0:T(1,128)S(1)}, u32[]{:S(2)}, u32[]{:S(2)}) collective-permute-start(f32[1,1024]{1,0:T(1,128)S(1)} %get-tuple-element.44), channel_id=1, source_target_pairs={{0,1},{1,2},{2,3},{3,4},{4,5},{5,6},{6,7},{7,8},{8,9},{9,10},{10,1... | collective-permute-start | bytes 12296 | tf_op jit(solution)/shard_map/ppermute | solution.py:21
  115.6 129.5 %all-to-all-start.2 = ((f32[64,1,128]{2,1,0:T(1,128)}), f32[64,1,128]{2,1,0:T(1,128)S(1)}, u32[]{:S(2)}, u32[]{:S(2)}) async-start(f32[64,1,128]{2,1,0:T(1,128)} %copy.204), calls=%async_computation.2 | async-start | bytes 65536 | tf_op jit(solution)/shard_map/all_to_all | solution.py:100
  361.3 60.5 %collective-permute-start.7 = (f32[1,64,256]{2,1,0:T(8,128)S(1)}, f32[1,64,256]{2,1,0:T(8,128)S(1)}, u32[]{:S(2)}, u32[]{:S(2)}) collective-permute-start(f32[1,64,256]{2,1,0:T(8,128)S(1)} %squeeze.81), channel_id=1, source_target_pairs={{0,1},{1,2},{2,3},{3,4},{4,5},{5,6},{6,7},{7,8},{8,9},{9,10},{10,1... | collective-permute-start | bytes 196616 | tf_op jit(solution)/shard_map/ppermute | solution.py:21
  417.6 5.6 collective-permute-start.6
  483.5 7.8 collective-permute-start.8
  486.0 5.3 collective-permute-start.9
  551.3 6.5 collective-permute-start.11
  553.2 5.6 collective-permute-start.10
  618.9 7.8 collective-permute-start.12
  621.5 5.2 collective-permute-start.13
  657.2 46.9 %all-to-all-start.3 = ((f32[64,1,128]{2,1,0:T(1,128)}), f32[64,1,128]{2,1,0:T(1,128)S(1)}, u32[]{:S(2)}, u32[]{:S(2)}) async-start(f32[64,1,128]{2,1,0:T(1,128)} %copy.235), calls=%async_computation.3 | async-start | bytes 65536 | tf_op jit(solution)/shard_map/all_to_all | solution.py:100
  680.2 24.3 %collective-permute-start.14 = (f32[1,1024]{1,0:T(1,128)S(1)}, f32[1,1024]{1,0:T(1,128)S(1)}, u32[]{:S(2)}, u32[]{:S(2)}) collective-permute-start(f32[1,1024]{1,0:T(1,128)S(1)} %get-tuple-element.33), channel_id=1, source_target_pairs={{1,0},{2,1},{3,2},{4,3},{5,4},{6,5},{7,6},{8,7},{9,8},{10,9},{11,1... | collective-permute-start | bytes 12296 | tf_op jit(solution)/shard_map/ppermute | solution.py:24
  684.1 20.4 %collective-permute-start.15 = (f32[1,1024]{1,0:T(1,128)S(1)}, f32[1,1024]{1,0:T(1,128)S(1)}, u32[]{:S(2)}, u32[]{:S(2)}) collective-permute-start(f32[1,1024]{1,0:T(1,128)S(1)} %get-tuple-element.33), channel_id=1, source_target_pairs={{0,1},{1,2},{2,3},{3,4},{4,5},{5,6},{6,7},{7,8},{8,9},{9,10},{10,1... | collective-permute-start | bytes 12296 | tf_op jit(solution)/shard_map/ppermute | solution.py:21
  706.1 31.1 %all-to-all-start.4 = ((f32[64,1,128]{2,1,0:T(1,128)}), f32[64,1,128]{2,1,0:T(1,128)S(1)}, u32[]{:S(2)}, u32[]{:S(2)}) async-start(f32[64,1,128]{2,1,0:T(1,128)} %copy.236), calls=%async_computation.4 | async-start | bytes 65536 | tf_op jit(solution)/shard_map/all_to_all | solution.py:100
  713.2 24.4 %collective-permute-start.16 = (f32[1,1024]{1,0:T(1,128)S(1)}, f32[1,1024]{1,0:T(1,128)S(1)}, u32[]{:S(2)}, u32[]{:S(2)}) collective-permute-start(f32[1,1024]{1,0:T(1,128)S(1)} %get-tuple-element.30), channel_id=1, source_target_pairs={{1,0},{2,1},{3,2},{4,3},{5,4},{6,5},{7,6},{8,7},{9,8},{10,9},{11,1... | collective-permute-start | bytes 12296 | tf_op jit(solution)/shard_map/ppermute | solution.py:24
  715.8 21.9 %collective-permute-start.17 = (f32[1,1024]{1,0:T(1,128)S(1)}, f32[1,1024]{1,0:T(1,128)S(1)}, u32[]{:S(2)}, u32[]{:S(2)}) collective-permute-start(f32[1,1024]{1,0:T(1,128)S(1)} %get-tuple-element.30), channel_id=1, source_target_pairs={{0,1},{1,2},{2,3},{3,4},{4,5},{5,6},{6,7},{7,8},{8,9},{9,10},{10,1... | collective-permute-start | bytes 12296 | tf_op jit(solution)/shard_map/ppermute | solution.py:21
  853.4 36.6 %collective-permute-start.19 = (f32[1,64,256]{2,1,0:T(8,128)S(1)}, f32[1,64,256]{2,1,0:T(8,128)S(1)}, u32[]{:S(2)}, u32[]{:S(2)}) collective-permute-start(f32[1,64,256]{2,1,0:T(8,128)S(1)} %squeeze.101), channel_id=1, source_target_pairs={{0,1},{1,2},{2,3},{3,4},{4,5},{5,6},{6,7},{7,8},{8,9},{9,10},{10,1... | collective-permute-start | bytes 196616 | tf_op jit(solution)/shard_map/ppermute | solution.py:21
  885.6 5.6 collective-permute-start.18
  951.2 7.8 collective-permute-start.20
  953.8 5.2 collective-permute-start.21
  1019.0 6.5 collective-permute-start.23
  1021.0 5.6 collective-permute-start.22
  1086.6 7.8 collective-permute-start.24
  1089.2 5.2 collective-permute-start.25
  (5 other events, 4.9 us)
where the time goes:
time: 1130 us; the launch traced here: 1120 us
  blocking collectives  734 us (65%)
  starting transfers between devices  223 us (20%)
  waiting for transfers between devices  87.5 us (8%)
  local copies, waits for them, and re-layouts  36.5 us (3%)
  other arithmetic  21 us (2%)
  between operations  20.5 us (2%)
    psum x8, blocking collectives, radial_squares(): return lax.psum(jnp.sum(values * values), 'rad')  229 us
    all_gather x2, blocking collectives, on_device(): collected = lax.all_gather(coarse_local, 'lat', axis=2, tiled=True)  227 us
    psum x6, blocking collectives, radial_inner(): return lax.psum(jnp.sum(first_vec * second_vec), 'rad')  157 us
    all_gather x1, blocking collectives, on_device(): faces = lax.all_gather(local_faces, 'lat', axis=2, tiled=True)  121 us
    ppermute x13, starting transfers between devices, padded_2(): lax.ppermute(lax.slice_in_dim(block, block.shape[dim] - width, None, axis...  116 us
    all_to_all x5, waiting for transfers between devices, fine_rows(): lax.all_to_all(slot_buffer.reshape(tile_count, 4 * layers * width), 'lat'...  83 us
    all_to_all x5, starting transfers between devices, fine_rows(): lax.all_to_all(slot_buffer.reshape(tile_count, 4 * layers * width), 'lat'...  59.2 us
    ppermute x13, starting transfers between devices, padded_2(): lax.ppermute(lax.slice_in_dim(block, 0, width, axis=dim), axis, backward)  47.6 us
  transfers between devices with their start and end apart: 31, of which 8 were waited for; matrix products, arithmetic and copies ran while one was open for 3% of the time, Pallas kernels for 0%

commit v1 on v0

v1 whole, which is shorter than its diff:
```python
import functools

import jax
import jax.numpy as jnp
from jax import lax
from jax.experimental import pallas as pl
from jax.experimental.pallas import tpu as pltpu
from jax.sharding import PartitionSpec as P

C = 32
HALF = 16
TILES = 64
NR = 16
CELLS = C * C
COARSE = HALF * HALF
LANES = 128
CG_ITERS = 4

cubic_weight = 8.0
radial_weight = 4.0
relax_factor = 0.8


def low(x):
    return lax.broadcasted_iota(jnp.int32, x.shape, x.ndim - 1) < TILES


def swap(x):
    return pltpu.roll(x, TILES, x.ndim - 1)


def pack(a, b):
    return jnp.where(low(a), a, b)


def first_twin(x):
    return jnp.where(low(x), x, swap(x))


def second_twin(x):
    return jnp.where(low(x), swap(x), x)


def glued(values, gluing):
    rows = values.shape[0]
    high = values.astype(jnp.bfloat16)
    rest = values - high.astype(jnp.float32)
    middle = rest.astype(jnp.bfloat16)
    lowest = (rest - middle.astype(jnp.float32)).astype(jnp.bfloat16)
    moved = jnp.dot(
        jnp.concatenate([high, middle, lowest], axis=0), gluing, preferred_element_type=jnp.float32
    )
    return moved[:rows] + (moved[rows : 2 * rows] + moved[2 * rows :])


def fine_ghosts(pad_ref, west_ref, east_ref, gluing, flips):
    north, south = pad_ref[C : 2 * C], pad_ref[CELLS : CELLS + C]
    west, east = pad_ref[pl.ds(C, C, stride=C)], pad_ref[pl.ds(2 * C - 1, C, stride=C)]
    moved = glued(jnp.concatenate([pack(north, south), pack(west, east)], axis=1), gluing)
    mirror = lax.broadcasted_iota(jnp.int32, (C, C), 0) + lax.broadcasted_iota(jnp.int32, (C, C), 1) == C - 1
    mirrored = jnp.dot(
        mirror.astype(jnp.float32), moved, precision=lax.Precision.HIGHEST, preferred_element_type=jnp.float32
    )
    pairs = []
    for pair in range(2):
        lanes = slice(pair * LANES, (pair + 1) * LANES)
        flip = pack(flips[2 * pair : 2 * pair + 1], flips[2 * pair + 1 : 2 * pair + 2])
        pairs.append(jnp.where(flip > 0, mirrored[:, lanes], moved[:, lanes]))
    pad_ref[0:C] = first_twin(pairs[0])
    pad_ref[CELLS + C : CELLS + 2 * C] = second_twin(pairs[0])
    west_ref[...] = first_twin(pairs[1])
    east_ref[...] = second_twin(pairs[1])


def row_of(i):
    return pl.ds(pl.multiple_of(i * C, C), C)


def lateral(pad_ref, west_ref, east_ref, i):
    own = pad_ref[row_of(i + 1)]
    column = lax.broadcasted_iota(jnp.int32, own.shape, 0)
    west = jnp.where(column == 0, west_ref[pl.ds(i, 1)], pltpu.roll(own, 1, 0))
    east = jnp.where(column == C - 1, east_ref[pl.ds(i, 1)], pltpu.roll(own, C - 1, 0))
    return own, (pad_ref[row_of(i)], pad_ref[row_of(i + 2)], west, east)


def coupled(conds, beside):
    total = conds[0] * beside[0]
    for cond, value in zip(conds[1:], beside[1:]):
        total = total + cond * value
    return total


def smooth_row(i, force, conds, cond_total, own, beside, residual_ref, smoothed_ref):
    cubic = cubic_weight * own * own
    residual = force - ((cond_total + cubic) * own - coupled(conds, beside))
    residual_ref[row_of(i)] = residual
    smoothed_ref[row_of(i)] = relax_factor * residual / (cond_total + 3.0 * cubic)


def pack_halves(smoothed_ref, packed_ref):
    packed_ref[...] = pack(smoothed_ref[: CELLS // 2], smoothed_ref[CELLS // 2 :])


def unpack_row(packed_ref, i, upper):
    block = packed_ref[row_of(i)]
    return second_twin(block) if upper else first_twin(block)


def unpack_halves(packed_ref, target_ref):
    target_ref[: CELLS // 2] = first_twin(packed_ref[...])
    target_ref[CELLS // 2 :] = second_twin(packed_ref[...])


def every(ref, start, count):
    return ref[pl.ds(start, count, stride=2)]


def spread_kernel(arrived_ref, pair_ref, force_ref):
    for group in range(8):
        parts = [arrived_ref[pl.ds(8 * field + group, TILES, stride=24)] for field in range(3)]
        cells = slice(group * LANES, (group + 1) * LANES)
        pair_ref[cells] = jnp.concatenate(parts[:2], axis=0).T
        force_ref[cells] = jnp.concatenate([parts[2], parts[2]], axis=0).T


def first_kernel(
    pair_ref, force_ref, above_ref, below_ref, gluing_ref, flips_ref,
    conds_ref, total_ref, residual_ref, smoothed_ref, packed_ref, faces_ref, face_total_ref,
    viscous, viscous_west, viscous_east, velocity, west, east,
):
    gluing, flips = gluing_ref[...], flips_ref[...]
    viscous[C : C + CELLS] = first_twin(pair_ref[...])
    velocity[C : C + CELLS] = second_twin(pair_ref[...])
    fine_ghosts(viscous, viscous_west, viscous_east, gluing, flips)
    fine_ghosts(velocity, west, east, gluing, flips)

    @pl.loop(0, C)
    def _(i):
        above, below = above_ref[row_of(i)], below_ref[row_of(i)]
        own, beside = lateral(viscous, viscous_west, viscous_east, i)
        conds = [0.5 * (own + other) for other in beside]
        conds += [radial_weight * 0.5 * (own + other) for other in (first_twin(above), first_twin(below))]
        cond_total = conds[0]
        for cond in conds[1:]:
            cond_total = cond_total + cond
        for direction in range(6):
            conds_ref[direction, row_of(i)] = conds[direction]
        total_ref[row_of(i)] = cond_total
        own, beside = lateral(velocity, west, east, i)
        beside = beside + (second_twin(above), second_twin(below))
        smooth_row(i, force_ref[row_of(i)], conds, cond_total, own, beside, residual_ref, smoothed_ref)

    pack_halves(smoothed_ref, packed_ref)
    ups = []
    for big in range(HALF):
        upper, lower = big * 2 * C, big * 2 * C + C
        cells = slice(big * HALF, (big + 1) * HALF)

        def both(direction, start):
            return every(conds_ref.at[direction], start, HALF) + every(conds_ref.at[direction], start + 1, HALF)

        def column(direction, start):
            return every(conds_ref.at[direction], upper + start, HALF) + every(
                conds_ref.at[direction], lower + start, HALF
            )

        north, south = both(0, upper), both(1, lower)
        west_face, east_face = column(2, 0), column(3, 1)
        up, down = both(4, upper) + both(4, lower), both(5, upper) + both(5, lower)
        faces_ref[cells] = pack(south, east_face)
        if big == 0:
            faces_ref[COARSE + COARSE // 2 : COARSE + COARSE // 2 + HALF] = north
        viscous_west[big : big + 1] = west_face[0:1]
        ups.append(up)
        face_total_ref[cells] = north + south + west_face + east_face + up + down
    for big in range(HALF // 2):
        start = COARSE + big * HALF
        faces_ref[start : start + HALF] = pack(ups[big], ups[big + HALF // 2])
    start = COARSE + COARSE // 2
    faces_ref[start : start + HALF] = pack(faces_ref[start : start + HALF], viscous_west[0:HALF])


def remain_kernel(
    conds_ref, total_ref, velocity_ref, residual_ref, smoothed_ref, above_ref, below_ref, face_total_ref,
    gluing_ref, flips_ref, coarse_ref, pad, west, east, above, below, remain, damping, *, paired,
):
    pad[C : C + CELLS] = smoothed_ref[...]
    unpack_halves(above_ref, above)
    unpack_halves(below_ref, below)
    fine_ghosts(pad, west, east, gluing_ref[...], flips_ref[...])

    @pl.loop(0, C)
    def _(i):
        velocity = velocity_ref[row_of(i)]
        if paired:
            velocity = second_twin(velocity)
        damp = 3.0 * (cubic_weight * velocity * velocity)
        own, beside = lateral(pad, west, east, i)
        beside = beside + (above[row_of(i)], below[row_of(i)])
        conds = [conds_ref[direction, row_of(i)] for direction in range(6)]
        image = (total_ref[row_of(i)] + damp) * own - coupled(conds, beside)
        remain[row_of(i)] = residual_ref[row_of(i)] - image
        damping[row_of(i)] = damp

    for big in range(HALF):
        sums = []
        for ref in (remain, damping):
            start = big * 2 * C
            sums.append(
                every(ref, start, HALF)
                + every(ref, start + 1, HALF)
                + every(ref, start + C, HALF)
                + every(ref, start + C + 1, HALF)
            )
        cells = slice(big * HALF, (big + 1) * HALF)
        coarse_ref[cells] = pack(sums[0], face_total_ref[cells] + sums[1])


def layered(ref, layer_pair, start, count):
    return ref[2 * layer_pair, start : start + count], ref[2 * layer_pair + 1, start : start + count]


def faces_kernel(gathered_ref, rows_ref, columns_ref, up_ref, down_ref):
    middle, last = COARSE, COARSE + COARSE // 2
    for sub in range(8):
        a, b = layered(gathered_ref, sub, 0, COARSE)
        rows_ref[pl.ds(LANES + sub, COARSE, stride=8)] = pack(a, swap(b))
        east = pack(swap(a), b)
        for big in range(HALF):
            columns_ref[big, pl.ds(8 + sub, HALF, stride=8)] = east[big * HALF : (big + 1) * HALF]
        a, b = layered(gathered_ref, sub, middle, COARSE // 2)
        up_ref[pl.ds(sub, COARSE // 2, stride=8)] = pack(a, swap(b))
        up_ref[pl.ds(8 * COARSE // 2 + sub, COARSE // 2, stride=8)] = pack(swap(a), b)
        a, b = layered(gathered_ref, sub, last, HALF)
        rows_ref[pl.ds(sub, HALF, stride=8)] = pack(a, swap(b))
        west = pack(swap(a), b)
        for big in range(HALF):
            columns_ref[big, sub : sub + 1] = west[big : big + 1]
    row = lax.broadcasted_iota(jnp.int32, (8, LANES), 0)
    lane = lax.broadcasted_iota(jnp.int32, (8, LANES), 1)
    outside = (row == 7) & (lane >= TILES)

    @pl.loop(0, COARSE)
    def _(cell):
        here = pl.ds(pl.multiple_of(cell * 8, 8), 8)
        up = jnp.where(outside, 0.0, up_ref[here])
        up_ref[here] = up
        swapped = swap(up)
        down_ref[here] = jnp.where(lane < TILES, pltpu.roll(swapped, 1, 0), swapped)


def coarse_ghosts(pad, gluing, flips):
    side = HALF * 8
    inner = slice(8, 8 + side)
    north, south = pad[1, inner], pad[HALF, inner]
    west = pad[1 : HALF + 1, 8:16].reshape(side, LANES)
    east = pad[1 : HALF + 1, side : side + 8].reshape(side, LANES)
    first = jnp.concatenate([pack(north, swap(south)), pack(west, swap(east))], axis=1)
    second = jnp.concatenate([pack(swap(north), south), pack(swap(west), east)], axis=1)
    moved = glued(jnp.concatenate([first, second], axis=0), gluing)
    ghosts = []
    for pair in range(2):
        lanes = slice(pair * LANES, (pair + 1) * LANES)
        a, b = moved[:side, lanes], moved[side:, lanes]
        ghosts += [pack(a, swap(b)), pack(swap(a), b)]
    for number, ghost in enumerate(ghosts):
        flip = jnp.broadcast_to(flips[number : number + 1], (8, LANES)) > 0
        for k in range(HALF):
            other = HALF - 1 - k
            value = jnp.where(flip, ghost[8 * other : 8 * other + 8], ghost[8 * k : 8 * k + 8])
            if number < 2:
                pad[0 if number == 0 else HALF + 1, 8 + 8 * k : 16 + 8 * k] = value
            else:
                column = 0 if number == 2 else 8 + side
                pad[1 + k, column : column + 8] = value


def total_of(x):
    return jnp.sum(jnp.sum(x, axis=0, keepdims=True), axis=1, keepdims=True)


def folded(x):
    return jnp.sum(x.reshape(x.shape[0] // 8, 8, LANES), axis=0)


def solve_coarse(
    gathered_ref, rows_ref, columns_ref, up_ref, down_ref, gluing, flips, pad, diagonal, image, residual, solution
):
    side = HALF * 8
    inner = slice(8, 8 + side)
    chunk = 64
    for sub in range(8):
        a, b = layered(gathered_ref, sub, 0, COARSE)
        residual[pl.ds(sub, COARSE, stride=8)] = pack(a, swap(b))
        diagonal[pl.ds(sub, COARSE, stride=8)] = pack(swap(a), b)

    zero = jnp.zeros((8, LANES), jnp.float32)

    def start(big, norm):
        here = pl.ds(pl.multiple_of(big * side, side), side)
        values = residual[here]
        pad[big + 1, inner] = values
        solution[here] = jnp.zeros_like(values)
        return norm + folded(values * values)

    norm = total_of(lax.fori_loop(0, HALF, start, zero))

    def apply_row(big, total):
        for part in range(side // chunk):
            first = part * chunk
            here = pl.ds(pl.multiple_of(big * side + first, chunk), chunk)
            own = pad[big + 1, 8 + first : 8 + first + chunk]
            swapped = swap(own).reshape(chunk // 8, 8, LANES)
            before = pltpu.roll(swapped, 1, 1).reshape(chunk, LANES)
            after = pltpu.roll(swapped, 7, 1).reshape(chunk, LANES)
            swapped = swapped.reshape(chunk, LANES)
            below = pl.ds(pl.multiple_of((big + 1) * side + first, chunk), chunk)
            value = (
                rows_ref[here] * pad[big, 8 + first : 8 + first + chunk]
                + rows_ref[below] * pad[big + 2, 8 + first : 8 + first + chunk]
                + columns_ref[big, first : first + chunk] * pad[big + 1, first : first + chunk]
                + columns_ref[big, 8 + first : 8 + first + chunk] * pad[big + 1, 16 + first : 16 + first + chunk]
                + up_ref[here] * pack(swapped, after)
                + down_ref[here] * pack(before, swapped)
            )
            value = diagonal[here] * own - value
            image[here] = value
            total = total + folded(own * value)
        return total

    for step in range(CG_ITERS):
        coarse_ghosts(pad, gluing, flips)
        length = norm / total_of(lax.fori_loop(0, HALF, apply_row, zero))

        def advance(big, total, length=length):
            here = pl.ds(pl.multiple_of(big * side, side), side)
            solution[here] = solution[here] + length * pad[big + 1, inner]
            values = residual[here] - length * image[here]
            residual[here] = values
            return total + folded(values * values)

        following = total_of(lax.fori_loop(0, HALF, advance, zero))
        if step + 1 < CG_ITERS:
            ratio = following / norm
            norm = following

            def turn(big, carry, ratio=ratio):
                here = pl.ds(pl.multiple_of(big * side, side), side)
                pad[big + 1, inner] = residual[here] + ratio * pad[big + 1, inner]
                return carry

            lax.fori_loop(0, HALF, turn, 0)


def prolong_layer(solution, layer, target):
    inside = (layer >= 0) & (layer < NR)
    place = jnp.clip(layer, 0, NR - 1)
    values = solution[pl.ds(place // 2, COARSE, stride=8)]
    values = jnp.where(place % 2 == 0, first_twin(values), second_twin(values))
    values = jnp.where(inside, values, 0.0)
    for big in range(HALF):
        row = values[big * HALF : (big + 1) * HALF]
        for start in (0, 1, C, C + 1):
            target[pl.ds(big * 2 * C + start, HALF, stride=2)] = row


COARSE_SCRATCH = [
    pltpu.VMEM((HALF + 2, (HALF + 2) * 8, LANES), jnp.float32),
    *[pltpu.VMEM((COARSE * 8, LANES), jnp.float32) for _ in range(4)],
]


def step_kernel(
    place_ref, gathered_ref, rows_ref, columns_ref, up_ref, down_ref, gluing_ref, flips_ref,
    pair_ref, above_ref, below_ref, smoothed_ref, smoothed_above_ref, smoothed_below_ref, force_ref, conds_ref,
    total_ref, new_velocity_ref, new_residual_ref, new_smoothed_ref, packed_ref,
    pad, diagonal, image, residual, solution, velocity, west, east, above, below, spread,
):
    gluing, flips = gluing_ref[...], flips_ref[...]
    solve_coarse(
        gathered_ref, rows_ref, columns_ref, up_ref, down_ref, gluing, flips, pad, diagonal, image, residual, solution
    )
    layer = place_ref[0]
    prolong_layer(solution, layer, spread)
    velocity[C : C + CELLS] = second_twin(pair_ref[...]) + smoothed_ref[...] + spread[...]
    new_velocity_ref[...] = velocity[C : C + CELLS]
    for shift, pairs, smooth, target in (
        (1, above_ref, smoothed_above_ref, above),
        (-1, below_ref, smoothed_below_ref, below),
    ):
        prolong_layer(solution, layer + shift, spread)
        unpack_halves(smooth, target)
        target[...] = second_twin(pairs[...]) + target[...] + spread[...]
    fine_ghosts(velocity, west, east, gluing, flips)

    @pl.loop(0, C)
    def _(i):
        own, beside = lateral(velocity, west, east, i)
        beside = beside + (above[row_of(i)], below[row_of(i)])
        conds = [conds_ref[direction, row_of(i)] for direction in range(6)]
        smooth_row(
            i, force_ref[row_of(i)], conds, total_ref[row_of(i)], own, beside, new_residual_ref, new_smoothed_ref
        )

    pack_halves(new_smoothed_ref, packed_ref)


def last_kernel(
    place_ref, gathered_ref, rows_ref, columns_ref, up_ref, down_ref, gluing_ref, flips_ref, velocity_ref,
    smoothed_ref, out_ref, pad, diagonal, image, residual, solution, spread, turned,
):
    solve_coarse(
        gathered_ref, rows_ref, columns_ref, up_ref, down_ref, gluing_ref[...], flips_ref[...],
        pad, diagonal, image, residual, solution,
    )
    prolong_layer(solution, place_ref[0], spread)
    for group in range(8):
        cells = slice(group * LANES, (group + 1) * LANES)
        turned[cells] = (velocity_ref[cells] + smoothed_ref[cells] + spread[cells]).T
    for group in range(8):
        out_ref[group : group + 1] = turned[pl.ds(group * LANES + place_ref[1], 1)]


def call(kernel, outs, scratch, args, scalars=0):
    vmem = pl.BlockSpec(memory_space=pltpu.VMEM)
    shapes = [jax.ShapeDtypeStruct(shape, jnp.float32) for shape in outs]
    return pl.pallas_call(
        kernel,
        out_shape=shapes,
        in_specs=[pl.BlockSpec(memory_space=pltpu.SMEM)] * scalars + [vmem] * (len(args) - scalars),
        out_specs=[vmem] * len(outs),
        scratch_shapes=scratch,
        compiler_params=pltpu.CompilerParams(vmem_limit_bytes=44 << 20),
    )(*args)


PADDED = (CELLS + 2 * C, LANES)
FINE = (CELLS, LANES)
PACKED = (CELLS // 2, LANES)
EDGE = (C, LANES)
FACES = (COARSE + COARSE // 2 + HALF, LANES)


def buffers(*shapes):
    return [pltpu.VMEM(shape, jnp.float32) for shape in shapes]


def spread_layer(arrived):
    return call(spread_kernel, [FINE, FINE], [], [arrived])


def first_stage(pair, force, above, below, gluing, flips):
    outs = [(6,) + FINE, FINE, FINE, FINE, PACKED, FACES, (COARSE, LANES)]
    scratch = buffers(PADDED, EDGE, EDGE, PADDED, EDGE, EDGE)
    return call(first_kernel, outs, scratch, [pair, force, above, below, gluing, flips])


def remain_stage(paired, *args):
    scratch = buffers(PADDED, EDGE, EDGE, FINE, FINE, FINE, FINE)
    return call(functools.partial(remain_kernel, paired=paired), [(COARSE, LANES)], scratch, list(args))[0]


def faces_stage(gathered):
    outs = [((HALF + 1) * HALF * 8, LANES), (HALF, (HALF + 1) * 8, LANES)] + [(COARSE * 8, LANES)] * 2
    return call(faces_kernel, outs, [], [gathered])


def step_stage(*args):
    scratch = COARSE_SCRATCH + buffers(PADDED, EDGE, EDGE, FINE, FINE, FINE)
    return call(step_kernel, [FINE, FINE, FINE, PACKED], scratch, list(args), 1)


def last_stage(*args):
    scratch = COARSE_SCRATCH + buffers(FINE, FINE)
    return call(last_kernel, [(8, LANES)], scratch, list(args), 1)[0]


def gluing_tables(glue_tile, glue_side, glue_flip):
    source = (glue_side * TILES + glue_tile).T.reshape(1, 4 * TILES)
    gluing = (jnp.arange(4 * TILES)[:, None] == source).astype(jnp.bfloat16)
    flips = glue_flip.T.astype(jnp.float32)
    flips = jnp.concatenate([flips, flips], axis=1)
    return gluing, jnp.concatenate([flips, flips], axis=0)


def gather(values, axis):
    count = lax.axis_size(axis)
    return lax.all_to_all(
        jnp.broadcast_to(values[None], (count,) + values.shape), axis, split_axis=0, concat_axis=0, tiled=True
    )


def radial(values):
    backward = [(layer + 1, layer) for layer in range(NR - 1)]
    forward = [(layer, layer + 1) for layer in range(NR - 1)]
    return lax.ppermute(values, "rad", backward), lax.ppermute(values, "rad", forward)


def on_device(rhs_force, viscosity, initial_guess, glue_tile, glue_side, glue_flip):
    gluing, flips = gluing_tables(glue_tile, glue_side, glue_flip)
    place = jnp.stack([lax.axis_index("rad"), lax.axis_index("lat")]).astype(jnp.int32)
    own = jnp.concatenate([field.reshape(8, LANES) for field in (viscosity, initial_guess, rhs_force)], axis=0)
    pair, force = spread_layer(gather(own, "lat").reshape(TILES * 24, LANES))
    above, below = radial(pair)
    conds, total, residual, smoothed, packed, faces, face_total = first_stage(
        pair, force, above, below, gluing, flips
    )
    smoothed_above, smoothed_below = radial(packed)
    coefficients = faces_stage(gather(faces, "rad"))
    coarse = remain_stage(
        True, conds, total, pair, residual, smoothed, smoothed_above, smoothed_below, face_total, gluing, flips
    )
    velocity, residual, smoothed, packed = step_stage(
        place, gather(coarse, "rad"), *coefficients, gluing, flips, pair, above, below, smoothed, smoothed_above,
        smoothed_below, force, conds, total,
    )
    smoothed_above, smoothed_below = radial(packed)
    coarse = remain_stage(
        False, conds, total, velocity, residual, smoothed, smoothed_above, smoothed_below, face_total, gluing, flips
    )
    out = last_stage(place, gather(coarse, "rad"), *coefficients, gluing, flips, velocity, smoothed)
    return out.reshape(1, CELLS)


def solution(mesh):
    return jax.shard_map(
        on_device,
        mesh=mesh,
        in_specs=(P("rad", "lat"), P("rad", "lat"), P("rad", "lat"), P(), P(), P()),
        out_specs=P("rad", "lat"),
        check_vma=False,
    )
```

time: 1130 us -> 331 us (0.29)
  blocking collectives: 734 us -> 31.5 us
  starting transfers between devices: 223 us -> 70.7 us
  Pallas kernels: 0 us -> 60.7 us
  waiting for transfers between devices: 87.5 us -> 139 us
  between operations: 20.5 us -> 0.3 us
  other arithmetic: 21 us -> 0.95 us
    psum x14 -> x0, blocking collectives: 386 us -> none  [the longest x8 229 us: radial_squares(): return lax.psum(jnp.sum(values * values), 'rad')]
    all_gather x3 -> x0, blocking collectives: 348 us -> none  [the longest x2 227 us: on_device(): collected = lax.all_gather(coarse_local, 'lat', axis=2, tiled=True)]
    ppermute x26 -> x6, starting transfers between devices: 164 us -> 19.8 us  [the longest x3 9.92 us: radial(): lax.ppermute(values, 'rad', backward)]
    pallas_call x0 -> x7, Pallas kernels: none -> 60.7 us  [call(): pl.pallas_call(kernel, out_shape=shapes, in_specs=[pl.BlockSpec(memory_sp...]
    ppermute x26 -> x6, waiting for transfers between devices: 4.51 us -> 51.2 us  [the longest x3 42.1 us: radial(): lax.ppermute(values, 'rad', backward)]
    all_to_all x0 -> x1, blocking collectives: none -> 31.5 us  [gather(): lax.all_to_all(jnp.broadcast_to(values[None], (count,) + values.shape), a...]
    unnamed x17 -> x76, local copies, waits for them, and re-layouts: 1.91 us -> 20.8 us
    reduce_sum x31 -> x0, other arithmetic: 13.8 us -> none  [the longest x8 6.21 us: radial_inner(): return lax.psum(jnp.sum(first_vec * second_vec), 'rad')]
  transfers between devices with their start and end apart: 31 -> 9, of which waited for: 8 -> 7; matrix products, arithmetic and copies ran while one was open for 3% -> 0% of each run, Pallas kernels for 0% -> 7%
where the time goes in v1:
time: 331 us; the launch traced here: 330 us
  waiting for transfers between devices  139 us (42%)
  starting transfers between devices  70.7 us (21%)
  Pallas kernels  60.7 us (18%)
  blocking collectives  31.5 us (10%)
  local copies, waits for them, and re-layouts  26.5 us (8%)
    all_to_all x3, waiting for transfers between devices, gather(): lax.all_to_all(jnp.broadcast_to(values[None], (count,) + values.shape), a...  87.7 us
    pallas_call x7, Pallas kernels, call(): pl.pallas_call(kernel, out_shape=shapes, in_specs=[pl.BlockSpec(memory_sp...  60.7 us
    all_to_all x3, starting transfers between devices, gather(): lax.all_to_all(jnp.broadcast_to(values[None], (count,) + values.shape), a...  50.9 us
    ppermute x3, waiting for transfers between devices, radial(): lax.ppermute(values, 'rad', backward)  42.1 us
    all_to_all x1, blocking collectives, gather(): lax.all_to_all(jnp.broadcast_to(values[None], (count,) + values.shape), a...  31.5 us
    unnamed x76, local copies, waits for them, and re-layouts  20.8 us
    ppermute x3, starting transfers between devices, radial(): lax.ppermute(values, 'rad', backward)  9.92 us
    ppermute x3, starting transfers between devices, radial(): lax.ppermute(values, 'rad', forward)  9.87 us
  transfers between devices with their start and end apart: 9, of which 7 were waited for; matrix products, arithmetic and copies ran while one was open for 0% of the time, Pallas kernels for 7%

profile of v1, /device:TPU:1, one launch (start us, length us, event | category | flops | bytes accessed | tf_op | source)
XLA Modules:
  0.0 329.6 jit_solution(15193129196678560531)
XLA Ops:
  1.7 32.5 %all-to-all-start = ((f32[64,24,128]{2,1,0:T(8,128)}), f32[64,24,128]{2,1,0:T(8,128)S(1)}, u32[]{:S(2)}, u32[]{:S(2)}) async-start(f32[64,24,128]{2,1,0:T(8,128)} %broadcast_in_dim.8), calls=%async_computation | async-start | bytes 1572864 | tf_op jit(solution)/shard_map/all_to_all | solution.py:489
  34.4 85.1 %all-to-all-done = f32[64,24,128]{2,1,0:T(8,128)S(1)} async-done(((f32[64,24,128]{2,1,0:T(8,128)}), f32[64,24,128]{2,1,0:T(8,128)S(1)}, u32[]{:S(2)}, u32[]{:S(2)}) %all-to-all-start) | async-done | bytes 786464 | tf_op jit(solution)/shard_map/all_to_all | solution.py:489
  119.8 5.0 %collective-permute-start = (f32[1024,128]{1,0:T(8,128)S(1)}, f32[1024,128]{1,0:T(8,128)S(1)}, u32[]{:S(2)}, u32[]{:S(2)}) collective-permute-start(f32[1024,128]{1,0:T(8,128)S(1)} %get-tuple-element.22.pair_ref.velocity_ref), channel_id=1, source_target_pairs={{1,0},{2,1},{3,2},{4,3},{5,4},{6,5},{7,6},{8,7},{9,8},{10,9},{11,1... | collective-permute-start | bytes 1572872 | tf_op jit(solution)/shard_map/ppermute | solution.py:497
  124.9 2.2 collective-permute-start.1
  127.2 4.8 %collective-permute-done.above_ref = f32[1024,128]{1,0:T(8,128)S(1)} collective-permute-done((f32[1024,128]{1,0:T(8,128)S(1)}, f32[1024,128]{1,0:T(8,128)S(1)}, u32[]{:S(2)}, u32[]{:S(2)}) %collective-permute-start) | collective-permute-done | bytes 524320 | tf_op jit(solution)/shard_map/ppermute | solution.py:497
  132.0 5.7 %collective-permute-done.1.below_ref = f32[1024,128]{1,0:T(8,128)S(1)} collective-permute-done((f32[1024,128]{1,0:T(8,128)S(1)}, f32[1024,128]{1,0:T(8,128)S(1)}, u32[]{:S(2)}, u32[]{:S(2)}) %collective-permute-start.1) | collective-permute-done | bytes 524320 | tf_op jit(solution)/shard_map/ppermute | solution.py:497
  137.7 3.6 %shard_map.65 = (f32[6,1024,128]{2,1,0:T(8,128)S(1)}, f32[1024,128]{1,0:T(8,128)S(1)}, f32[1024,128]{1,0:T(8,128)S(1)}, f32[1024,128]{1,0:T(8,128)S(1)}, f32[512...) custom-call(f32[1024,128]{1,0:T(8,128)S(1)} %get-tuple-element.22.pair_ref.velocity_ref, ...), custom_call_target="tpu_custom_call" | custom-call | tf_op jit(solution)/shard_map/pallas_call | solution.py:428
  145.8 2.0 broadcast_in_dim.10
  147.9 6.3 %all-to-all-start.2 = ((f32[16,400,128]{2,1,0:T(8,128)}), f32[16,400,128]{2,1,0:T(8,128)}, u32[]{:S(2)}, u32[]{:S(2)}) async-start(f32[16,400,128]{2,1,0:T(8,128)} %broadcast_in_dim.10), calls=%async_computation.2 | async-start | bytes 6553600 | tf_op jit(solution)/shard_map/all_to_all | solution.py:489
  154.2 2.1 collective-permute-start.2
  156.3 3.5 %collective-permute-start.3 = (f32[512,128]{1,0:T(8,128)}, f32[512,128]{1,0:T(8,128)S(1)}, u32[]{:S(2)}, u32[]{:S(2)}) collective-permute-start(f32[512,128]{1,0:T(8,128)} %copy-done.34), channel_id=1, source_target_pairs={{0,1},{1,2},{2,3},{3,4},{4,5},{5,6},{6,7},{7,8},{8,9},{9,10},{10,1... | collective-permute-start | bytes 786440 | tf_op jit(solution)/shard_map/ppermute | solution.py:497
  159.8 35.2 %collective-permute-done.2.above_ref.smoothed_above_ref = f32[512,128]{1,0:T(8,128)S(1)} collective-permute-done((f32[512,128]{1,0:T(8,128)}, f32[512,128]{1,0:T(8,128)S(1)}, u32[]{:S(2)}, u32[]{:S(2)}) %collective-permute-start.2) | collective-permute-done | bytes 262176 | tf_op jit(solution)/shard_map/ppermute | solution.py:497
  196.0 1.0 copy-done.6
  198.1 1.0 copy-done.29
  200.0 3.1 shard_map.66
  204.4 2.4 broadcast_in_dim.9
  206.9 12.1 %all-to-all-start.1 = ((f32[16,256,128]{2,1,0:T(8,128)}), f32[16,256,128]{2,1,0:T(8,128)}, u32[]{:S(2)}, u32[]{:S(2)}) async-start(f32[16,256,128]{2,1,0:T(8,128)} %broadcast_in_dim.9), calls=%async_computation.1 | async-start | bytes 4194304 | tf_op jit(solution)/shard_map/all_to_all | solution.py:489
  219.1 21.3 %shard_map.67 = (f32[2176,128]{1,0:T(8,128)S(1)}, f32[16,136,128]{2,1,0:T(8,128)S(1)}, f32[2048,128]{1,0:T(8,128)S(1)}, f32[2048,128]{1,0:T(8,128)S(1)}) custom-call(f32[16,400,128]{2,1,0:T(8,128)} %all-to-all-done.2.gathered_ref), custom_call_target="tpu_custom_call" | custom-call | tf_op jit(solution)/shard_map/pallas_call | solution.py:428
  243.4 2.6 all-to-all-done.1.gathered_ref
  246.0 1.2 copy-done.9
  247.3 1.2 copy-done.12
  248.5 1.2 copy-done.15
  249.7 1.0 copy-done.20
  251.8 1.0 copy-done.25
  252.8 17.1 %shard_map.68 = (f32[1024,128]{1,0:T(8,128)S(1)}, f32[1024,128]{1,0:T(8,128)S(1)}, f32[1024,128]{1,0:T(8,128)S(1)}, f32[512,128]{1,0:T(8,128)S(1)}) custom-call(s32[2]{0:T(128)S(1)} %pad_add_fusion.place_ref, f32[16,256,128]{2,1,0:T(8,128)} %all-to-all-done.1.gathered_ref, f32[2176,128]{1,0:T(8,128)S(1)} %get-tuple-element.31.rows_ref, ...), custom_call_target="tpu_custom_call" | custom-call | tf_op jit(solution)/shard_map/pallas_call | solution.py:428
  270.0 2.8 collective-permute-start.4
  272.8 4.2 %collective-permute-start.5 = (f32[512,128]{1,0:T(8,128)S(1)}, f32[512,128]{1,0:T(8,128)S(1)}, u32[]{:S(2)}, u32[]{:S(2)}) collective-permute-start(f32[512,128]{1,0:T(8,128)S(1)} %get-tuple-element.38), channel_id=1, source_target_pairs={{0,1},{1,2},{2,3},{3,4},{4,5},{5,6},{6,7},{7,8},{8,9},{9,10},{10,1... | collective-permute-start | bytes 786440 | tf_op jit(solution)/shard_map/ppermute | solution.py:497
  277.0 2.1 collective-permute-done.4.above_ref
  279.1 3.4 %collective-permute-done.5.below_ref = f32[512,128]{1,0:T(8,128)S(1)} collective-permute-done((f32[512,128]{1,0:T(8,128)S(1)}, f32[512,128]{1,0:T(8,128)S(1)}, u32[]{:S(2)}, u32[]{:S(2)}) %collective-permute-start.5) | collective-permute-done | bytes 262176 | tf_op jit(solution)/shard_map/ppermute | solution.py:497
  282.5 1.1 shard_map.69
  283.9 31.5 %all_to_all.20.gathered_ref = f32[16,256,128]{2,1,0:T(8,128)S(1)} all-to-all(f32[16,256,128]{2,1,0:T(8,128)S(1)} %broadcast_in_dim.11), channel_id=1, replica_groups=mesh['lat'=64,'rad'=16] {'rad'}, dimensions={0} | all-to-all | bytes 4194304 | tf_op jit(solution)/shard_map/all_to_all | solution.py:489
  315.4 14.2 %shard_map.70 = f32[8,128]{1,0:T(8,128)} custom-call(s32[2]{0:T(128)S(1)} %pad_add_fusion.place_ref, f32[16,256,128]{2,1,0:T(8,128)S(1)} %all_to_all.20.gathered_ref, f32[2176,128]{1,0:T(8,128)S(1)} %get-tuple-element.31.rows_ref, f32[16,136,128]{2,1,0:T(8,128)S(1)} %copy-done.10, f32[2048,128]{1,0:T(8,128)S(1)} %copy-done.13, f32[2048,128]{1,0:T(8,128)S(1)} %copy-done.16, ...), custom_call_target="tpu_custom_call" | custom-call | tf_op jit(solution)/shard_map/pallas_call | solution.py:428
  (81 shorter events, 15.5 us)
Async XLA Ops:
  0.0 34.3 %copy-start.36 = (s32[64,4]{0,1:T(4,128)S(1)}, s32[64,4]{0,1:T(4,128)}, u32[]{:S(2)}) copy-start(s32[64,4]{0,1:T(4,128)} %param.10) | copy-start | bytes 3076
  0.0 34.3 %copy-start.35 = (s32[64,4]{0,1:T(4,128)S(1)}, s32[64,4]{0,1:T(4,128)}, u32[]{:S(2)}) copy-start(s32[64,4]{0,1:T(4,128)} %param.9) | copy-start | bytes 3076
  0.0 127.1 %copy-start.37 = (s32[64,4]{0,1:T(4,128)S(1)}, s32[64,4]{0,1:T(4,128)}, u32[]{:S(2)}) copy-start(s32[64,4]{0,1:T(4,128)} %param.11) | copy-start | bytes 3076
  1.7 117.7 %all-to-all-start = ((f32[64,24,128]{2,1,0:T(8,128)}), f32[64,24,128]{2,1,0:T(8,128)S(1)}, u32[]{:S(2)}, u32[]{:S(2)}) async-start(f32[64,24,128]{2,1,0:T(8,128)} %broadcast_in_dim.8), calls=%async_computation | async-start | bytes 1572864 | tf_op jit(solution)/shard_map/all_to_all | solution.py:489
  119.8 21.5 %copy-start.17 = (f32[1024,128]{1,0:T(8,128)}, f32[1024,128]{1,0:T(8,128)S(1)}, u32[]{:S(2)}) copy-start(f32[1024,128]{1,0:T(8,128)S(1)} %get-tuple-element.23.force_ref) | copy-start | bytes 1572868
  119.8 12.2 %collective-permute-start = (f32[1024,128]{1,0:T(8,128)S(1)}, f32[1024,128]{1,0:T(8,128)S(1)}, u32[]{:S(2)}, u32[]{:S(2)}) collective-permute-start(f32[1024,128]{1,0:T(8,128)S(1)} %get-tuple-element.22.pair_ref.velocity_ref), channel_id=1, source_target_pairs={{1,0},{2,1},{3,2},{4,3},{5,4},{6,5},{7,6},{8,7},{9,8},{10,9},{11,1... | collective-permute-start | bytes 1572872 | tf_op jit(solution)/shard_map/ppermute | solution.py:497
  124.9 12.8 %collective-permute-start.1 = (f32[1024,128]{1,0:T(8,128)S(1)}, f32[1024,128]{1,0:T(8,128)S(1)}, u32[]{:S(2)}, u32[]{:S(2)}) collective-permute-start(f32[1024,128]{1,0:T(8,128)S(1)} %get-tuple-element.22.pair_ref.velocity_ref), channel_id=1, source_target_pairs={{0,1},{1,2},{2,3},{3,4},{4,5},{5,6},{6,7},{7,8},{8,9},{9,10},{10,1... | collective-permute-start | bytes 1572872 | tf_op jit(solution)/shard_map/ppermute | solution.py:497
  132.0 13.9 %copy-start.19 = (f32[1024,128]{1,0:T(8,128)}, f32[1024,128]{1,0:T(8,128)S(1)}, u32[]{:S(2)}) copy-start(f32[1024,128]{1,0:T(8,128)S(1)} %collective-permute-done.above_ref) | copy-start | bytes 1572868
  137.7 8.2 %copy-start.21 = (f32[1024,128]{1,0:T(8,128)}, f32[1024,128]{1,0:T(8,128)S(1)}, u32[]{:S(2)}) copy-start(f32[1024,128]{1,0:T(8,128)S(1)} %collective-permute-done.1.below_ref) | copy-start | bytes 1572868
  145.8 49.1 %copy-start = (f32[6,1024,128]{2,1,0:T(8,128)}, f32[6,1024,128]{2,1,0:T(8,128)S(1)}, u32[]{:S(2)}) copy-start(f32[6,1024,128]{2,1,0:T(8,128)S(1)} %get-tuple-element.24.conds_ref) | copy-start | bytes 9437188
  147.9 56.6 %all-to-all-start.2 = ((f32[16,400,128]{2,1,0:T(8,128)}), f32[16,400,128]{2,1,0:T(8,128)}, u32[]{:S(2)}, u32[]{:S(2)}) async-start(f32[16,400,128]{2,1,0:T(8,128)} %broadcast_in_dim.10), calls=%async_computation.2 | async-start | bytes 6553600 | tf_op jit(solution)/shard_map/all_to_all | solution.py:489
  154.2 40.7 %collective-permute-start.2 = (f32[512,128]{1,0:T(8,128)}, f32[512,128]{1,0:T(8,128)S(1)}, u32[]{:S(2)}, u32[]{:S(2)}) collective-permute-start(f32[512,128]{1,0:T(8,128)} %copy-done.34), channel_id=1, source_target_pairs={{1,0},{2,1},{3,2},{4,3},{5,4},{6,5},{7,6},{8,7},{9,8},{10,9},{11,1... | collective-permute-start | bytes 786440 | tf_op jit(solution)/shard_map/ppermute | solution.py:497
  156.3 38.7 %collective-permute-start.3 = (f32[512,128]{1,0:T(8,128)}, f32[512,128]{1,0:T(8,128)S(1)}, u32[]{:S(2)}, u32[]{:S(2)}) collective-permute-start(f32[512,128]{1,0:T(8,128)} %copy-done.34), channel_id=1, source_target_pairs={{0,1},{1,2},{2,3},{3,4},{4,5},{5,6},{6,7},{7,8},{8,9},{9,10},{10,1... | collective-permute-start | bytes 786440 | tf_op jit(solution)/shard_map/ppermute | solution.py:497
  194.9 1.0 copy-start.3
  196.0 1.0 copy-start.6
  197.0 1.0 copy-start.24
  198.1 1.0 copy-start.29
  206.9 39.1 %all-to-all-start.1 = ((f32[16,256,128]{2,1,0:T(8,128)}), f32[16,256,128]{2,1,0:T(8,128)}, u32[]{:S(2)}, u32[]{:S(2)}) async-start(f32[16,256,128]{2,1,0:T(8,128)} %broadcast_in_dim.9), calls=%async_computation.1 | async-start | bytes 4194304 | tf_op jit(solution)/shard_map/all_to_all | solution.py:489
  218.9 27.0 %copy-start.4 = (f32[1024,128]{1,0:T(8,128)S(1)}, f32[1024,128]{1,0:T(8,128)}, u32[]{:S(2)}) copy-start(f32[1024,128]{1,0:T(8,128)} %copy-done.2) | copy-start | bytes 1572868
  219.0 27.0 %copy-start.7 = (f32[1024,128]{1,0:T(8,128)S(1)}, f32[1024,128]{1,0:T(8,128)}, u32[]{:S(2)}) copy-start(f32[1024,128]{1,0:T(8,128)} %copy-done.5) | copy-start | bytes 1572868
  219.0 27.0 %copy-start.18 = (f32[1024,128]{1,0:T(8,128)S(1)}, f32[1024,128]{1,0:T(8,128)}, u32[]{:S(2)}) copy-start(f32[1024,128]{1,0:T(8,128)} %copy-done.17) | copy-start | bytes 1572868
  219.0 27.0 %copy-start.27 = (f32[512,128]{1,0:T(8,128)S(1)}, f32[512,128]{1,0:T(8,128)}, u32[]{:S(2)}) copy-start(f32[512,128]{1,0:T(8,128)} %copy-done.26) | copy-start | bytes 786436
  246.0 1.2 copy-start.9
  247.3 1.2 copy-start.12
  248.5 1.2 copy-start.15
  252.8 29.7 %copy-start.1 = (f32[6,1024,128]{2,1,0:T(8,128)S(1)}, f32[6,1024,128]{2,1,0:T(8,128)}, u32[]{:S(2)}) copy-start(f32[6,1024,128]{2,1,0:T(8,128)} %copy-done) | copy-start | bytes 9437188
  252.8 29.7 %copy-start.33 = (f32[256,128]{1,0:T(8,128)S(1)}, f32[256,128]{1,0:T(8,128)}, u32[]{:S(2)}) copy-start(f32[256,128]{1,0:T(8,128)} %copy-done.31) | copy-start | bytes 393220
  270.0 9.1 %collective-permute-start.4 = (f32[512,128]{1,0:T(8,128)S(1)}, f32[512,128]{1,0:T(8,128)S(1)}, u32[]{:S(2)}, u32[]{:S(2)}) collective-permute-start(f32[512,128]{1,0:T(8,128)S(1)} %get-tuple-element.38), channel_id=1, source_target_pairs={{1,0},{2,1},{3,2},{4,3},{5,4},{6,5},{7,6},{8,7},{9,8},{10,9},{11,1... | collective-permute-start | bytes 786440 | tf_op jit(solution)/shard_map/ppermute | solution.py:497
  272.8 9.7 %collective-permute-start.5 = (f32[512,128]{1,0:T(8,128)S(1)}, f32[512,128]{1,0:T(8,128)S(1)}, u32[]{:S(2)}, u32[]{:S(2)}) collective-permute-start(f32[512,128]{1,0:T(8,128)S(1)} %get-tuple-element.38), channel_id=1, source_target_pairs={{0,1},{1,2},{2,3},{3,4},{4,5},{5,6},{6,7},{7,8},{8,9},{9,10},{10,1... | collective-permute-start | bytes 786440 | tf_op jit(solution)/shard_map/ppermute | solution.py:497
  283.9 31.6 %copy-start.10 = (f32[16,136,128]{2,1,0:T(8,128)S(1)}, f32[16,136,128]{2,1,0:T(8,128)}, u32[]{:S(2)}) copy-start(f32[16,136,128]{2,1,0:T(8,128)} %copy-done.8) | copy-start | bytes 3342340
  283.9 31.6 %copy-start.13 = (f32[2048,128]{1,0:T(8,128)S(1)}, f32[2048,128]{1,0:T(8,128)}, u32[]{:S(2)}) copy-start(f32[2048,128]{1,0:T(8,128)} %copy-done.11) | copy-start | bytes 3145732
  283.9 31.5 %copy-start.16 = (f32[2048,128]{1,0:T(8,128)S(1)}, f32[2048,128]{1,0:T(8,128)}, u32[]{:S(2)}) copy-start(f32[2048,128]{1,0:T(8,128)} %copy-done.14) | copy-start | bytes 3145732
  (15 other events, 12.9 us)

commit v2 on v1

v2 whole, which is shorter than its diff:
```python
import functools

import jax
import jax.numpy as jnp
from jax import lax
from jax.experimental import pallas as pl
from jax.experimental.pallas import tpu as pltpu
from jax.sharding import PartitionSpec as P

C = 32
HALF = 16
TILES = 64
NR = 16
CHIPS = NR // 2
CELLS = C * C
COARSE = HALF * HALF
LANES = 128
CG_ITERS = 4

cubic_weight = 8.0
radial_weight = 4.0
relax_factor = 0.8


def low(x):
    return lax.broadcasted_iota(jnp.int32, x.shape, x.ndim - 1) < TILES


def swap(x):
    return pltpu.roll(x, TILES, x.ndim - 1)


def pack(a, b):
    return jnp.where(low(a), a, b)


def first_twin(x):
    return jnp.where(low(x), x, swap(x))


def second_twin(x):
    return jnp.where(low(x), swap(x), x)


def glued(values, gluing):
    rows = values.shape[0]
    high = values.astype(jnp.bfloat16)
    rest = values - high.astype(jnp.float32)
    middle = rest.astype(jnp.bfloat16)
    lowest = (rest - middle.astype(jnp.float32)).astype(jnp.bfloat16)
    moved = jnp.dot(
        jnp.concatenate([high, middle, lowest], axis=0), gluing, preferred_element_type=jnp.float32
    )
    return moved[:rows] + (moved[rows : 2 * rows] + moved[2 * rows :])


def fine_ghosts(pad_ref, west_ref, east_ref, gluing, flips):
    north, south = pad_ref[C : 2 * C], pad_ref[CELLS : CELLS + C]
    west, east = pad_ref[pl.ds(C, C, stride=C)], pad_ref[pl.ds(2 * C - 1, C, stride=C)]
    moved = glued(jnp.concatenate([pack(north, south), pack(west, east)], axis=1), gluing)
    mirror = lax.broadcasted_iota(jnp.int32, (C, C), 0) + lax.broadcasted_iota(jnp.int32, (C, C), 1) == C - 1
    mirrored = jnp.dot(
        mirror.astype(jnp.float32), moved, precision=lax.Precision.HIGHEST, preferred_element_type=jnp.float32
    )
    pairs = []
    for pair in range(2):
        lanes = slice(pair * LANES, (pair + 1) * LANES)
        flip = pack(flips[2 * pair : 2 * pair + 1], flips[2 * pair + 1 : 2 * pair + 2])
        pairs.append(jnp.where(flip > 0, mirrored[:, lanes], moved[:, lanes]))
    pad_ref[0:C] = first_twin(pairs[0])
    pad_ref[CELLS + C : CELLS + 2 * C] = second_twin(pairs[0])
    west_ref[...] = first_twin(pairs[1])
    east_ref[...] = second_twin(pairs[1])


def row_of(i):
    return pl.ds(pl.multiple_of(i * C, C), C)


def lateral(pad_ref, west_ref, east_ref, i):
    own = pad_ref[row_of(i + 1)]
    column = lax.broadcasted_iota(jnp.int32, own.shape, 0)
    west = jnp.where(column == 0, west_ref[pl.ds(i, 1)], pltpu.roll(own, 1, 0))
    east = jnp.where(column == C - 1, east_ref[pl.ds(i, 1)], pltpu.roll(own, C - 1, 0))
    return own, (pad_ref[row_of(i)], pad_ref[row_of(i + 2)], west, east)


def coupled(conds, beside):
    total = conds[0] * beside[0]
    for cond, value in zip(conds[1:], beside[1:]):
        total = total + cond * value
    return total


def smooth_row(i, force, cond_total, own, image, residual_ref, smoothed_ref):
    cubic = cubic_weight * own * own
    residual = force - ((cond_total + cubic) * own - image)
    residual_ref[row_of(i)] = residual
    smoothed_ref[row_of(i)] = relax_factor * residual / (cond_total + 3.0 * cubic)


def pack_halves(smoothed_ref, packed_ref):
    packed_ref[...] = pack(smoothed_ref[: CELLS // 2], smoothed_ref[CELLS // 2 :])


def unpack_row(packed_ref, i, upper):
    block = packed_ref[row_of(i)]
    return second_twin(block) if upper else first_twin(block)


def unpack_halves(packed_ref, target_ref):
    target_ref[: CELLS // 2] = first_twin(packed_ref[...])
    target_ref[CELLS // 2 :] = second_twin(packed_ref[...])


def every(ref, start, count):
    return ref[pl.ds(start, count, stride=2)]


def rows_loop(count, step, body):
    @pl.loop(0, count, step=step)
    def _(first):
        for part in range(step):
            body(first + part)


def turned_layer(arrived_ref, first_field, second_field, group):
    parts = [arrived_ref[pl.ds(8 * field + group, TILES, stride=24)] for field in (first_field, second_field)]
    return jnp.concatenate(parts, axis=0).T


def spread_kernel(arrived_ref, pair_ref):
    for group in range(8):
        pair_ref[group * LANES : (group + 1) * LANES] = turned_layer(arrived_ref, 0, 1, group)


def lateral_kernel(
    arrived_ref, pair_ref, gluing_ref, flips_ref, viscous_ref, velocity_ref, force_ref, conds_ref, image_ref,
    total_ref, faces_ref, viscous_pad, viscous_west, viscous_east, pad, west, east,
):
    gluing, flips = gluing_ref[...], flips_ref[...]
    viscous_ref[...] = first_twin(pair_ref[...])
    velocity_ref[...] = second_twin(pair_ref[...])
    viscous_pad[C : C + CELLS] = viscous_ref[...]
    pad[C : C + CELLS] = velocity_ref[...]
    fine_ghosts(viscous_pad, viscous_west, viscous_east, gluing, flips)
    fine_ghosts(pad, west, east, gluing, flips)

    def body(i):
        own, beside = lateral(viscous_pad, viscous_west, viscous_east, i)
        conds = [0.5 * (own + other) for other in beside]
        for direction in range(4):
            conds_ref[direction, row_of(i)] = conds[direction]
        image_ref[row_of(i)] = coupled(conds, lateral(pad, west, east, i)[1])
        total_ref[row_of(i)] = conds[0] + conds[1] + conds[2] + conds[3]

    rows_loop(C, 4, body)
    sums, wests = [], []
    for big in range(HALF):
        upper, lower = big * 2 * C, big * 2 * C + C
        cells = slice(big * HALF, (big + 1) * HALF)

        def both(ref, start):
            return every(ref, start, HALF) + every(ref, start + 1, HALF)

        def column(direction, start):
            ref = conds_ref.at[direction]
            return every(ref, upper + start, HALF) + every(ref, lower + start, HALF)

        faces = pack(both(conds_ref.at[1], lower), column(3, 1))
        for copy in range(CHIPS):
            faces_ref[copy, cells] = faces
        if big == 0:
            north = both(conds_ref.at[0], upper)
        wests.append(column(2, 0)[0:1])
        sums.append(both(viscous_ref, upper) + both(viscous_ref, lower))
    start = COARSE + COARSE // 2
    edge = pack(north, jnp.concatenate(wests, axis=0))
    for copy in range(CHIPS):
        for big in range(HALF // 2):
            first = COARSE + big * HALF
            faces_ref[copy, first : first + HALF] = pack(sums[big], sums[big + HALF // 2])
        faces_ref[copy, start : start + HALF] = edge
    for group in range(8):
        force_ref[group * LANES : (group + 1) * LANES] = turned_layer(arrived_ref, 2, 2, group)


def first_kernel(
    force_ref, viscous_ref, velocity_ref, lateral_ref, lateral_total_ref, above_ref, below_ref,
    radials_ref, total_ref, residual_ref, smoothed_ref, packed_ref,
):
    def body(i):
        here = row_of(i)
        viscous, velocity = viscous_ref[here], velocity_ref[here]
        beside = above_ref[here], below_ref[here]
        conds = [radial_weight * 0.5 * (viscous + first_twin(pair)) for pair in beside]
        cond_total = lateral_total_ref[here] + conds[0] + conds[1]
        radials_ref[0, here] = conds[0]
        radials_ref[1, here] = conds[1]
        total_ref[here] = cond_total
        image = lateral_ref[here] + conds[0] * second_twin(beside[0]) + conds[1] * second_twin(beside[1])
        smooth_row(i, force_ref[here], cond_total, velocity, image, residual_ref, smoothed_ref)

    rows_loop(C, 4, body)
    pack_halves(smoothed_ref, packed_ref)


def remain_kernel(
    conds_ref, radials_ref, total_ref, velocity_ref, residual_ref, smoothed_ref, above_ref, below_ref,
    gluing_ref, flips_ref, coarse_ref, pad, west, east, remain, damping,
):
    pad[C : C + CELLS] = smoothed_ref[...]
    fine_ghosts(pad, west, east, gluing_ref[...], flips_ref[...])
    for upper in range(2):
        offset = upper * (C // 2)

        def body(source, upper=upper, offset=offset):
            i = source + offset
            here = row_of(i)
            velocity = velocity_ref[here]
            damp = 3.0 * (cubic_weight * velocity * velocity)
            own, beside = lateral(pad, west, east, i)
            beside = beside + (unpack_row(above_ref, source, upper), unpack_row(below_ref, source, upper))
            conds = [conds_ref[direction, here] for direction in range(4)]
            conds += [radials_ref[direction, here] for direction in range(2)]
            image = (total_ref[here] + damp) * own - coupled(conds, beside)
            remain[here] = residual_ref[here] - image
            damping[here] = damp

        rows_loop(C // 2, 4, body)

    for big in range(HALF):
        sums = []
        for ref in (remain, damping):
            start = big * 2 * C
            sums.append(
                every(ref, start, HALF)
                + every(ref, start + 1, HALF)
                + every(ref, start + C, HALF)
                + every(ref, start + C + 1, HALF)
            )
        cells = slice(big * HALF, (big + 1) * HALF)
        sums = pack(sums[0], sums[1])
        for copy in range(CHIPS):
            coarse_ref[copy, cells] = sums


def for_core(place_ref, own_ref, other_ref, body):
    @pl.when(place_ref[0] % 2 == 0)
    def _():
        body(own_ref, other_ref)

    @pl.when(place_ref[0] % 2 == 1)
    def _():
        body(other_ref, own_ref)


def radial_pair(values):
    swapped = swap(values)
    shaped = swapped.reshape(values.shape[0] // 8, 8, LANES)
    before = pltpu.roll(shaped, 1, 1).reshape(values.shape)
    after = pltpu.roll(shaped, 7, 1).reshape(values.shape)
    return pack(swapped, after), pack(before, swapped)


def faces_kernel(
    place_ref, own_ref, other_ref, rows_ref, columns_ref, up_ref, down_ref, face_total_ref, sums
):
    middle, last = COARSE, COARSE + COARSE // 2
    half = COARSE // 2

    def arrange(even_ref, odd_ref):
        for sub in range(8):
            a, b = even_ref[sub, :middle], odd_ref[sub, :middle]
            rows_ref[pl.ds(LANES + sub, COARSE, stride=8)] = pack(a, swap(b))
            east = pack(swap(a), b)
            for big in range(HALF):
                columns_ref[big, pl.ds(8 + sub, HALF, stride=8)] = east[big * HALF : (big + 1) * HALF]
            a, b = even_ref[sub, middle:last], odd_ref[sub, middle:last]
            sums[pl.ds(sub, half, stride=8)] = pack(a, swap(b))
            sums[pl.ds(8 * half + sub, half, stride=8)] = pack(swap(a), b)
            a, b = even_ref[sub, last : last + HALF], odd_ref[sub, last : last + HALF]
            rows_ref[pl.ds(sub, HALF, stride=8)] = pack(a, swap(b))
            west = pack(swap(a), b)
            for big in range(HALF):
                columns_ref[big, sub : sub + 1] = west[big : big + 1]

    for_core(place_ref, own_ref, other_ref, arrange)
    side = HALF * 8
    shape = (side, LANES)
    row = lax.broadcasted_iota(jnp.int32, shape, 0) % 8
    lane = lax.broadcasted_iota(jnp.int32, shape, 1)
    top = (row == 7) & (lane >= TILES)
    bottom = (row == 0) & (lane < TILES)

    @pl.loop(0, HALF)
    def _(big):
        here = pl.ds(pl.multiple_of(big * side, side), side)
        own = sums[here]
        above, below = radial_pair(own)
        up = radial_weight * 0.5 * (own + jnp.where(top, 0.0, above))
        down = radial_weight * 0.5 * (own + jnp.where(bottom, 0.0, below))
        up_ref[here] = jnp.where(top, 0.0, up)
        down_ref[here] = jnp.where(bottom, 0.0, down)
        face_total_ref[here] = (
            rows_ref[here]
            + rows_ref[pl.ds(pl.multiple_of((big + 1) * side, side), side)]
            + columns_ref[big, :side]
            + columns_ref[big, 8 : 8 + side]
            + up
            + down
        )


def coarse_ghosts(pad, gluing, flips):
    side = HALF * 8
    inner = slice(8, 8 + side)
    north, south = pad[1, inner], pad[HALF, inner]
    west = pad[1 : HALF + 1, 8:16].reshape(side, LANES)
    east = pad[1 : HALF + 1, side : side + 8].reshape(side, LANES)
    first = jnp.concatenate([pack(north, swap(south)), pack(west, swap(east))], axis=1)
    second = jnp.concatenate([pack(swap(north), south), pack(swap(west), east)], axis=1)
    moved = glued(jnp.concatenate([first, second], axis=0), gluing)
    ghosts = []
    for pair in range(2):
        lanes = slice(pair * LANES, (pair + 1) * LANES)
        a, b = moved[:side, lanes], moved[side:, lanes]
        ghosts += [pack(a, swap(b)), pack(swap(a), b)]
    for number, ghost in enumerate(ghosts):
        flip = jnp.broadcast_to(flips[number : number + 1], (8, LANES)) > 0
        for k in range(HALF):
            other = HALF - 1 - k
            value = jnp.where(flip, ghost[8 * other : 8 * other + 8], ghost[8 * k : 8 * k + 8])
            if number < 2:
                pad[0 if number == 0 else HALF + 1, 8 + 8 * k : 16 + 8 * k] = value
            else:
                column = 0 if number == 2 else 8 + side
                pad[1 + k, column : column + 8] = value


def total_of(x):
    return jnp.sum(jnp.sum(x, axis=0, keepdims=True), axis=1, keepdims=True)


def folded(x):
    return jnp.sum(x.reshape(x.shape[0] // 8, 8, LANES), axis=0)


def solve_coarse(
    place_ref, own_ref, other_ref, rows_ref, columns_ref, up_ref, down_ref, face_total_ref, gluing, flips,
    pad, diagonal, image, residual, solution,
):
    side = HALF * 8
    inner = slice(8, 8 + side)
    chunk = 64

    def arrange(even_ref, odd_ref):
        for sub in range(8):
            a, b = even_ref[sub], odd_ref[sub]
            residual[pl.ds(sub, COARSE, stride=8)] = pack(a, swap(b))
            diagonal[pl.ds(sub, COARSE, stride=8)] = pack(swap(a), b)

    for_core(place_ref, own_ref, other_ref, arrange)
    zero = jnp.zeros((8, LANES), jnp.float32)

    def here_of(big):
        return pl.ds(pl.multiple_of(big * side, side), side)

    def total_over(body):
        def several(first, total):
            for part in range(4):
                total = body(first * 4 + part, total)
            return total

        return total_of(lax.fori_loop(0, HALF // 4, several, zero))

    def start(big, total):
        here = here_of(big)
        values = residual[here]
        pad[big + 1, inner] = values
        diagonal[here] = diagonal[here] + face_total_ref[here]
        return total + folded(values * values)

    norm = total_over(start)

    def apply_row(big, total):
        for part in range(side // chunk):
            first = part * chunk
            here = pl.ds(pl.multiple_of(big * side + first, chunk), chunk)
            own = pad[big + 1, 8 + first : 8 + first + chunk]
            above, below = radial_pair(own)
            south = pl.ds(pl.multiple_of((big + 1) * side + first, chunk), chunk)
            value = (
                rows_ref[here] * pad[big, 8 + first : 8 + first + chunk]
                + rows_ref[south] * pad[big + 2, 8 + first : 8 + first + chunk]
                + columns_ref[big, first : first + chunk] * pad[big + 1, first : first + chunk]
                + columns_ref[big, 8 + first : 8 + first + chunk] * pad[big + 1, 16 + first : 16 + first + chunk]
                + up_ref[here] * above
                + down_ref[here] * below
            )
            value = diagonal[here] * own - value
            image[here] = value
            total = total + folded(own * value)
        return total

    for step in range(CG_ITERS):
        coarse_ghosts(pad, gluing, flips)
        length = norm / total_over(apply_row)

        def advance(big, total, length=length, step=step):
            here = here_of(big)
            moved = length * pad[big + 1, inner]
            solution[here] = moved if step == 0 else solution[here] + moved
            if step + 1 == CG_ITERS:
                return total
            values = residual[here] - length * image[here]
            residual[here] = values
            return total + folded(values * values)

        following = total_over(advance)
        if step + 1 < CG_ITERS:
            ratio = following / norm
            norm = following

            def turn(big, total, ratio=ratio):
                pad[big + 1, inner] = residual[here_of(big)] + ratio * pad[big + 1, inner]
                return total

            total_over(turn)


def prolong_layer(solution, layer, target):
    inside = (layer >= 0) & (layer < NR)
    place = jnp.clip(layer, 0, NR - 1)
    values = solution[pl.ds(place // 2, COARSE, stride=8)]
    values = jnp.where(place % 2 == 0, first_twin(values), second_twin(values))
    values = jnp.where(inside, values, 0.0)
    for big in range(HALF):
        row = values[big * HALF : (big + 1) * HALF]
        for start in (0, 1, C, C + 1):
            target[pl.ds(big * 2 * C + start, HALF, stride=2)] = row


COARSE_SCRATCH = [
    pltpu.VMEM((HALF + 2, (HALF + 2) * 8, LANES), jnp.float32),
    *[pltpu.VMEM((COARSE * 8, LANES), jnp.float32) for _ in range(4)],
]


def step_kernel(
    place_ref, own_ref, other_ref, rows_ref, columns_ref, up_ref, down_ref, face_total_ref, gluing_ref, flips_ref,
    velocity_ref, above_ref, below_ref, smoothed_ref, smoothed_above_ref, smoothed_below_ref, force_ref,
    conds_ref, radials_ref, total_ref, new_velocity_ref, new_residual_ref, new_smoothed_ref, packed_ref,
    pad, diagonal, image, residual, solution, velocity, west, east, above, below, spread,
):
    gluing, flips = gluing_ref[...], flips_ref[...]
    for pairs, smooth, target in ((above_ref, smoothed_above_ref, above), (below_ref, smoothed_below_ref, below)):
        unpack_halves(smooth, target)
        target[...] = target[...] + second_twin(pairs[...])
    solve_coarse(
        place_ref, own_ref, other_ref, rows_ref, columns_ref, up_ref, down_ref, face_total_ref, gluing, flips,
        pad, diagonal, image, residual, solution,
    )
    layer = place_ref[0]
    prolong_layer(solution, layer, spread)
    velocity[C : C + CELLS] = velocity_ref[...] + smoothed_ref[...] + spread[...]
    new_velocity_ref[...] = velocity[C : C + CELLS]
    fine_ghosts(velocity, west, east, gluing, flips)
    for shift, target in ((1, above), (-1, below)):
        prolong_layer(solution, layer + shift, spread)
        target[...] = target[...] + spread[...]

    def body(i):
        here = row_of(i)
        own, beside = lateral(velocity, west, east, i)
        beside = beside + (above[here], below[here])
        conds = [conds_ref[direction, here] for direction in range(4)]
        conds += [radials_ref[direction, here] for direction in range(2)]
        smooth_row(i, force_ref[here], total_ref[here], own, coupled(conds, beside), new_residual_ref, new_smoothed_ref)

    rows_loop(C, 4, body)
    pack_halves(new_smoothed_ref, packed_ref)


def last_kernel(
    place_ref, own_ref, other_ref, rows_ref, columns_ref, up_ref, down_ref, face_total_ref, gluing_ref, flips_ref,
    velocity_ref, smoothed_ref, out_ref, pad, diagonal, image, residual, solution, spread, turned,
):
    solve_coarse(
        place_ref, own_ref, other_ref, rows_ref, columns_ref, up_ref, down_ref, face_total_ref,
        gluing_ref[...], flips_ref[...], pad, diagonal, image, residual, solution,
    )
    prolong_layer(solution, place_ref[0], spread)
    for group in range(8):
        cells = slice(group * LANES, (group + 1) * LANES)
        turned[cells] = (velocity_ref[cells] + smoothed_ref[cells] + spread[cells]).T
    for group in range(8):
        out_ref[group : group + 1] = turned[pl.ds(group * LANES + place_ref[1], 1)]


def call(kernel, outs, scratch, args, scalars=0, mebibytes=4):
    vmem = pl.BlockSpec(memory_space=pltpu.VMEM)
    shapes = [jax.ShapeDtypeStruct(shape, jnp.float32) for shape in outs]
    return pl.pallas_call(
        kernel,
        out_shape=shapes,
        in_specs=[pl.BlockSpec(memory_space=pltpu.SMEM)] * scalars + [vmem] * (len(args) - scalars),
        out_specs=[vmem] * len(outs),
        scratch_shapes=[pltpu.VMEM(shape, jnp.float32) for shape in scratch],
        compiler_params=pltpu.CompilerParams(vmem_limit_bytes=VMEM_MIB << 20),
        cost_estimate=pl.CostEstimate(flops=mebibytes << 20, bytes_accessed=mebibytes << 20, transcendentals=0),
    )(*args)


VMEM_MIB = 20
PADDED = (CELLS + 2 * C, LANES)
FINE = (CELLS, LANES)
PACKED = (CELLS // 2, LANES)
EDGE = (C, LANES)
FACES = (CHIPS, COARSE + COARSE // 2 + HALF, LANES)
GRID = (COARSE * 8, LANES)
COARSE_SCRATCH = [(HALF + 2, (HALF + 2) * 8, LANES)] + [GRID] * 4


def spread_layer(arrived):
    return call(spread_kernel, [FINE], [], [arrived])[0]


def lateral_stage(*args):
    outs = [FINE, FINE, FINE, (4,) + FINE, FINE, FINE, FACES]
    return call(lateral_kernel, outs, [PADDED, EDGE, EDGE, PADDED, EDGE, EDGE], args, mebibytes=24)


def first_stage(*args):
    return call(first_kernel, [(2,) + FINE, FINE, FINE, FINE, PACKED], [], args)


def remain_stage(*args):
    return call(remain_kernel, [(CHIPS, COARSE, LANES)], [PADDED, EDGE, EDGE, FINE, FINE], args)[0]


def faces_stage(*args):
    outs = [((HALF + 1) * HALF * 8, LANES), (HALF, (HALF + 1) * 8, LANES)] + [GRID] * 3
    return call(faces_kernel, outs, [GRID], args, 1, 24)


def step_stage(*args):
    scratch = COARSE_SCRATCH + [PADDED, EDGE, EDGE, FINE, FINE, FINE]
    return call(step_kernel, [FINE, FINE, FINE, PACKED], scratch, args, 1)


def last_stage(*args):
    return call(last_kernel, [(8, LANES)], COARSE_SCRATCH + [FINE, FINE], args, 1)[0]


NEAR = 4
FAR = TILES // NEAR


def place_of(tile):
    return tile // 2 % NEAR * FAR + tile // (2 * NEAR) * 2 + tile % 2


def gluing_tables(glue_tile, glue_side, glue_flip):
    def lanes_of(table):
        return table.reshape(FAR // 2, NEAR, 2, 4).transpose(3, 1, 0, 2).reshape(4, TILES)

    source = (lanes_of(glue_side) * TILES + place_of(lanes_of(glue_tile))).reshape(1, 4 * TILES)
    gluing = (jnp.arange(4 * TILES)[:, None] == source).astype(jnp.bfloat16)
    flips = lanes_of(glue_flip).astype(jnp.float32)
    flips = jnp.concatenate([flips, flips], axis=1)
    return gluing, jnp.concatenate([flips, flips], axis=0)


def gather(values, axis, groups):
    sent = jnp.broadcast_to(values[None], (len(groups[0]),) + values.shape)
    arrived = lax.all_to_all(sent, axis, split_axis=0, concat_axis=0, axis_index_groups=groups, tiled=True)
    return arrived.reshape((-1,) + values.shape[1:])


def gather_lateral(values):
    tiles = sorted(range(TILES), key=place_of)
    far = [tiles[near * FAR : (near + 1) * FAR] for near in range(NEAR)]
    return gather(gather(values, "lat", far), "lat", [list(group) for group in zip(*far)])


def gather_radial(copies):
    groups = [list(range(core, NR, 2)) for core in range(2)]
    own = lax.all_to_all(copies, "rad", split_axis=0, concat_axis=0, axis_index_groups=groups, tiled=True)
    other = lax.ppermute(own, "rad", [(layer, layer ^ 1) for layer in range(NR)])
    return own, other


def radial(values):
    backward = [(layer + 1, layer) for layer in range(NR - 1)]
    forward = [(layer, layer + 1) for layer in range(NR - 1)]
    return lax.ppermute(values, "rad", backward), lax.ppermute(values, "rad", forward)


def on_device(rhs_force, viscosity, initial_guess, glue_tile, glue_side, glue_flip):
    tables = gluing_tables(glue_tile, glue_side, glue_flip)
    place = jnp.stack([lax.axis_index("rad"), place_of(lax.axis_index("lat"))]).astype(jnp.int32)
    own = jnp.concatenate([field.reshape(8, LANES) for field in (viscosity, initial_guess, rhs_force)], axis=0)
    arrived = gather_lateral(own)
    pair = spread_layer(arrived)
    pair_beside = radial(pair)
    viscous, velocity, force, conds, lateral_image, lateral_total, faces = lateral_stage(arrived, pair, *tables)
    faces, *pair_beside = lax.optimization_barrier((faces, *pair_beside))
    radials, total, residual, smoothed, packed = first_stage(
        force, viscous, velocity, lateral_image, lateral_total, *pair_beside
    )
    smoothed_beside = radial(packed)
    coefficients = faces_stage(place, *gather_radial(faces))
    coarse = remain_stage(conds, radials, total, velocity, residual, smoothed, *smoothed_beside, *tables)
    velocity, residual, smoothed, packed = step_stage(
        place, *gather_radial(coarse), *coefficients, *tables, velocity, *pair_beside, smoothed,
        *smoothed_beside, force, conds, radials, total,
    )
    smoothed_beside = radial(packed)
    coarse = remain_stage(conds, radials, total, velocity, residual, smoothed, *smoothed_beside, *tables)
    out = last_stage(place, *gather_radial(coarse), *coefficients, *tables, velocity, smoothed)
    return out.reshape(1, CELLS)


def solution(mesh):
    return jax.shard_map(
        on_device,
        mesh=mesh,
        in_specs=(P("rad", "lat"), P("rad", "lat"), P("rad", "lat"), P(), P(), P()),
        out_specs=P("rad", "lat"),
        check_vma=False,
    )
```

time: 331 us -> 230 us (0.69)
  waiting for transfers between devices: 139 us -> 49.7 us
  blocking collectives: 31.5 us -> 76.4 us
  Pallas kernels: 60.7 us -> 30.9 us
  starting transfers between devices: 70.7 us -> 49.8 us
  local copies, waits for them, and re-layouts: 26.5 us -> 20.7 us
    all_to_all x3, waiting for transfers between devices: 87.7 us -> 30.6 us  [the longest x1 18.2 us: gather(): lax.all_to_all(sent, axis, split_axis=0, concat_axis=0, axis_index_groups...]
    all_to_all x1 -> x2, blocking collectives: 31.5 us -> 76.4 us  [the longest x1 61.2 us: gather(): lax.all_to_all(sent, axis, split_axis=0, concat_axis=0, axis_index_groups...]
    ppermute x3, waiting for transfers between devices: 42.1 us -> 10.3 us  [radial(): lax.ppermute(values, 'rad', backward)]
    all_to_all x3, starting transfers between devices: 50.9 us -> 19.8 us  [the longest x1 9.99 us: gather(): lax.all_to_all(sent, axis, split_axis=0, concat_axis=0, axis_index_groups...]
    pallas_call x7 -> x8, Pallas kernels: 60.7 us -> 30.9 us  [call(): pl.pallas_call(kernel, out_shape=shapes, in_specs=[pl.BlockSpec(memory_sp...]
    ppermute x0 -> x3, starting transfers between devices: none -> 11.8 us  [gather_radial(): lax.ppermute(own, 'rad', [(layer, layer ^ 1) for layer in range(NR)])]
    broadcast_in_dim x4 -> x2, local copies, waits for them, and re-layouts: 5.61 us -> 0.97 us  [gather(): sent = jnp.broadcast_to(values[None], (len(groups[0]),) + values.shape)]
    unnamed x76 -> x59, local copies, waits for them, and re-layouts: 20.8 us -> 18.5 us
  transfers between devices with their start and end apart: 9 -> 12, of which waited for: 7 -> 8; matrix products, arithmetic and copies ran while one was open for 0% -> 1% of each run, Pallas kernels for 7% -> 4%
where the time goes in v2:
time: 230 us; the launch traced here: 229 us
  blocking collectives  76.4 us (33%)
  starting transfers between devices  49.8 us (22%)
  waiting for transfers between devices  49.7 us (22%)
  Pallas kernels  30.9 us (13%)
  local copies, waits for them, and re-layouts  20.7 us (9%)
    all_to_all x1, blocking collectives, gather(): lax.all_to_all(sent, axis, split_axis=0, concat_axis=0, axis_index_groups...  61.2 us
    pallas_call x8, Pallas kernels, call(): pl.pallas_call(kernel, out_shape=shapes, in_specs=[pl.BlockSpec(memory_sp...  30.9 us
    unnamed x59, local copies, waits for them, and re-layouts  18.5 us
    all_to_all x1, waiting for transfers between devices, gather(): lax.all_to_all(sent, axis, split_axis=0, concat_axis=0, axis_index_groups...  18.2 us
    all_to_all x1, blocking collectives, gather_radial(): lax.all_to_all(copies, 'rad', split_axis=0, concat_axis=0, axis_index_gro...  15.2 us
    all_to_all x2, waiting for transfers between devices, gather_radial(): lax.all_to_all(copies, 'rad', split_axis=0, concat_axis=0, axis_index_gro...  12.4 us
    ppermute x3, starting transfers between devices, gather_radial(): lax.ppermute(own, 'rad', [(layer, layer ^ 1) for layer in range(NR)])  11.8 us
    ppermute x3, waiting for transfers between devices, radial(): lax.ppermute(values, 'rad', backward)  10.3 us
  transfers between devices with their start and end apart: 12, of which 8 were waited for; matrix products, arithmetic and copies ran while one was open for 1% of the time, Pallas kernels for 4%

profile of v2, /device:TPU:1, one launch (start us, length us, event | category | flops | bytes accessed | tf_op | source)
XLA Modules:
  0.0 228.8 jit_solution(4629634844031176218)
XLA Ops:
  0.8 61.2 %all_to_all.25 = f32[16,24,128]{2,1,0:T(8,128)S(1)} all-to-all(f32[16,24,128]{2,1,0:T(8,128)S(1)} %broadcast_in_dim.6), channel_id=1, replica_groups={{0,16,128,144,256,272,384,400,512,528,640,656,768,784,896,912},{32,48,1..., dimensions={0} | all-to-all | bytes 393216 | tf_op jit(solution)/shard_map/all_to_all | solution.py:577
  62.9 10.0 %all-to-all-start.1 = ((f32[4,384,128]{2,1,0:T(8,128)}), f32[4,384,128]{2,1,0:T(8,128)S(1)}, u32[]{:S(2)}, u32[]{:S(2)}) async-start(f32[4,384,128]{2,1,0:T(8,128)} %broadcast_in_dim.16), calls=%async_computation.1 | async-start | bytes 1572864 | tf_op jit(solution)/shard_map/all_to_all | solution.py:577
  74.3 18.2 %all-to-all-done.1 = f32[4,384,128]{2,1,0:T(8,128)S(1)} async-done(((f32[4,384,128]{2,1,0:T(8,128)}), f32[4,384,128]{2,1,0:T(8,128)S(1)}, u32[]{:S(2)}, u32[]{:S(2)}) %all-to-all-start.1) | async-done | bytes 786464 | tf_op jit(solution)/shard_map/all_to_all | solution.py:577
  92.7 3.4 %collective-permute-start = (f32[1024,128]{1,0:T(8,128)S(1)}, f32[1024,128]{1,0:T(8,128)S(1)}, u32[]{:S(2)}, u32[]{:S(2)}) collective-permute-start(f32[1024,128]{1,0:T(8,128)S(1)} %shard_map.64.pair_ref), channel_id=1, source_target_pairs={{1,0},{2,1},{3,2},{4,3},{5,4},{6,5},{7,6},{8,7},{9,8},{10,9},{11,1... | collective-permute-start | bytes 1572872 | tf_op jit(solution)/shard_map/ppermute | solution.py:597
  96.1 2.2 collective-permute-start.1
  98.4 1.4 shard_map.65
  101.4 1.2 copy-done.17
  105.7 3.2 %collective-permute-done.1.below_ref = f32[1024,128]{1,0:T(8,128)S(1)} collective-permute-done((f32[1024,128]{1,0:T(8,128)S(1)}, f32[1024,128]{1,0:T(8,128)S(1)}, u32[]{:S(2)}, u32[]{:S(2)}) %collective-permute-start.1) | collective-permute-done | bytes 524320 | tf_op jit(solution)/shard_map/ppermute | solution.py:597
  109.7 4.7 %all-to-all-start.3 = ((f32[8,400,128]{2,1,0:T(8,128)}), f32[8,400,128]{2,1,0:T(8,128)}, u32[]{:S(2)}, u32[]{:S(2)}) async-start(f32[8,400,128]{2,1,0:T(8,128)} %copy-done.17), calls=%async_computation.3 | async-start | bytes 3276800 | tf_op jit(solution)/shard_map/all_to_all | solution.py:589
  116.5 1.0 copy-done.10
  117.5 1.0 copy-done.13
  118.6 1.0 copy-done.21
  121.7 1.0 shard_map.66
  122.8 3.5 %collective-permute-start.2 = (f32[512,128]{1,0:T(8,128)S(1)}, f32[512,128]{1,0:T(8,128)S(1)}, u32[]{:S(2)}, u32[]{:S(2)}) collective-permute-start(f32[512,128]{1,0:T(8,128)S(1)} %get-tuple-element.42), channel_id=1, source_target_pairs={{1,0},{2,1},{3,2},{4,3},{5,4},{6,5},{7,6},{8,7},{9,8},{10,9},{11,1... | collective-permute-start | bytes 786440 | tf_op jit(solution)/shard_map/ppermute | solution.py:597
  126.3 3.5 %collective-permute-start.3 = (f32[512,128]{1,0:T(8,128)S(1)}, f32[512,128]{1,0:T(8,128)S(1)}, u32[]{:S(2)}, u32[]{:S(2)}) collective-permute-start(f32[512,128]{1,0:T(8,128)S(1)} %get-tuple-element.42), channel_id=1, source_target_pairs={{0,1},{1,2},{2,3},{3,4},{4,5},{5,6},{6,7},{7,8},{8,9},{9,10},{10,1... | collective-permute-start | bytes 786440 | tf_op jit(solution)/shard_map/ppermute | solution.py:597
  129.8 8.2 %collective-permute-done.2.above_ref.smoothed_above_ref = f32[512,128]{1,0:T(8,128)S(1)} collective-permute-done((f32[512,128]{1,0:T(8,128)S(1)}, f32[512,128]{1,0:T(8,128)S(1)}, u32[]{:S(2)}, u32[]{:S(2)}) %collective-permute-start.2) | collective-permute-done | bytes 262176 | tf_op jit(solution)/shard_map/ppermute | solution.py:597
  139.1 1.4 shard_map.67
  143.8 5.1 %all-to-all-start.2 = ((f32[8,256,128]{2,1,0:T(8,128)}), f32[8,256,128]{2,1,0:T(8,128)}, u32[]{:S(2)}, u32[]{:S(2)}) async-start(f32[8,256,128]{2,1,0:T(8,128)} %copy-done.5), calls=%async_computation.2 | async-start | bytes 2097152 | tf_op jit(solution)/shard_map/all_to_all | solution.py:589
  148.9 2.9 %collective-permute-start.5 = (f32[8,400,128]{2,1,0:T(8,128)}, f32[8,400,128]{2,1,0:T(8,128)}, u32[]{:S(2)}, u32[]{:S(2)}) collective-permute-start(f32[8,400,128]{2,1,0:T(8,128)} %all-to-all-done.3.own_ref), channel_id=1, source_target_pairs={{0,1},{1,0},{2,3},{3,2},{4,5},{5,4},{6,7},{7,6},{8,9},{9,8},{10,11... | collective-permute-start | bytes 4915208 | tf_op jit(solution)/shard_map/ppermute | solution.py:590
  151.8 12.4 %all-to-all-done.2.own_ref = f32[8,256,128]{2,1,0:T(8,128)} async-done(((f32[8,256,128]{2,1,0:T(8,128)}), f32[8,256,128]{2,1,0:T(8,128)}, u32[]{:S(2)}, u32[]{:S(2)}) %all-to-all-start.2) | async-done | bytes 1048608 | tf_op jit(solution)/shard_map/all_to_all | solution.py:589
  164.2 3.5 %collective-permute-start.4 = (f32[8,256,128]{2,1,0:T(8,128)}, f32[8,256,128]{2,1,0:T(8,128)}, u32[]{:S(2)}, u32[]{:S(2)}) collective-permute-start(f32[8,256,128]{2,1,0:T(8,128)} %all-to-all-done.2.own_ref), channel_id=1, source_target_pairs={{0,1},{1,0},{2,3},{3,2},{4,5},{5,4},{6,7},{7,6},{8,9},{9,8},{10,11... | collective-permute-start | bytes 3145736 | tf_op jit(solution)/shard_map/ppermute | solution.py:590
  167.9 4.9 %shard_map.68 = (f32[2176,128]{1,0:T(8,128)S(1)}, f32[16,136,128]{2,1,0:T(8,128)S(1)}, f32[2048,128]{1,0:T(8,128)S(1)}, f32[2048,128]{1,0:T(8,128)S(1)}, f32[2048,128]{1,0:T(8,128)S(1)}) custom-call(s32[2]{0:T(128)S(1)} %pad_add_fusion.place_ref, f32[8,400,128]{2,1,0:T(8,128)} %all-to-all-done.3.own_ref, f32[8,400,128]{2,1,0:T(8,128)} %collective-permute-done.5.other_ref), custom_call_target="tpu_custom_call" | custom-call | flops 25165824 | bytes 25165824 | tf_op jit(solution)/shard_map/pallas_call | solution.py:504
  173.8 11.2 %shard_map.69 = (f32[1024,128]{1,0:T(8,128)S(1)}, f32[1024,128]{1,0:T(8,128)S(1)}, f32[1024,128]{1,0:T(8,128)S(1)}, f32[512,128]{1,0:T(8,128)S(1)}) custom-call(s32[2]{0:T(128)S(1)} %pad_add_fusion.place_ref, f32[8,256,128]{2,1,0:T(8,128)} %all-to-all-done.2.own_ref, f32[8,256,128]{2,1,0:T(8,128)} %collective-permute-done.4.other_ref, ...), custom_call_target="tpu_custom_call" | custom-call | flops 4194304 | bytes 4194304 | tf_op jit(solution)/shard_map/pallas_call | solution.py:504
  185.0 1.9 collective-permute-start.6
  187.0 3.6 %collective-permute-start.7 = (f32[512,128]{1,0:T(8,128)S(1)}, f32[512,128]{1,0:T(8,128)S(1)}, u32[]{:S(2)}, u32[]{:S(2)}) collective-permute-start(f32[512,128]{1,0:T(8,128)S(1)} %get-tuple-element.52), channel_id=1, source_target_pairs={{0,1},{1,2},{2,3},{3,4},{4,5},{5,6},{6,7},{7,8},{8,9},{9,10},{10,1... | collective-permute-start | bytes 786440 | tf_op jit(solution)/shard_map/ppermute | solution.py:597
  190.6 2.1 collective-permute-done.6.above_ref
  192.7 2.3 collective-permute-done.7.below_ref
  195.0 1.4 shard_map.70
  196.4 15.2 %all_to_all.26.own_ref = f32[8,256,128]{2,1,0:T(8,128)S(1)} all-to-all(f32[8,256,128]{2,1,0:T(8,128)S(1)} %shard_map.70), channel_id=1, replica_groups={{0,2,4,6,8,10,12,14},{1,3,5,7,9,11,13,15},{16,18,20,22,24,26,28,30},{17..., dimensions={0} | all-to-all | bytes 2097152 | tf_op jit(solution)/shard_map/all_to_all | solution.py:589
  211.6 5.4 %collective-permute-start.8 = (f32[8,256,128]{2,1,0:T(8,128)S(1)}, f32[8,256,128]{2,1,0:T(8,128)S(1)}, u32[]{:S(2)}, u32[]{:S(2)}) collective-permute-start(f32[8,256,128]{2,1,0:T(8,128)S(1)} %all_to_all.26.own_ref), channel_id=1, source_target_pairs={{0,1},{1,0},{2,3},{3,2},{4,5},{5,4},{6,7},{7,6},{8,9},{9,8},{10,11... | collective-permute-start | bytes 3145736 | tf_op jit(solution)/shard_map/ppermute | solution.py:590
  217.0 2.3 collective-permute-done.8.other_ref
  219.3 9.5 %shard_map.71 = f32[8,128]{1,0:T(8,128)} custom-call(s32[2]{0:T(128)S(1)} %pad_add_fusion.place_ref, f32[8,256,128]{2,1,0:T(8,128)S(1)} %all_to_all.26.own_ref, f32[8,256,128]{2,1,0:T(8,128)S(1)} %collective-permute-done.8.other_ref, f32[2176,128]{1,0:T(8,128)S(1)} %get-tuple-element.44.rows_ref, f32[16,136,128]{2,1,0:T(8,128)S(1)} %get-tuple-element.45.columns_ref, ...), custom_call_target="tpu_custom_call" | custom-call | flops 4194304 | bytes 4194304 | tf_op jit(solution)/shard_map/pallas_call | solution.py:504
  (78 shorter events, 18.5 us)
Async XLA Ops:
  0.0 72.9 %copy-start.27 = (s32[64,4]{0,1:T(4,128)S(1)}, s32[64,4]{0,1:T(4,128)}, u32[]{:S(2)}) copy-start(s32[64,4]{0,1:T(4,128)} %param.10) | copy-start | bytes 3076
  0.7 72.7 %copy-start.26 = (s32[64,4]{0,1:T(4,128)S(1)}, s32[64,4]{0,1:T(4,128)}, u32[]{:S(2)}) copy-start(s32[64,4]{0,1:T(4,128)} %param.9) | copy-start | bytes 3076
  0.8 73.3 %copy-start.28 = (s32[64,4]{0,1:T(4,128)S(1)}, s32[64,4]{0,1:T(4,128)}, u32[]{:S(2)}) copy-start(s32[64,4]{0,1:T(4,128)} %param.11) | copy-start | bytes 3076
  62.9 29.6 %all-to-all-start.1 = ((f32[4,384,128]{2,1,0:T(8,128)}), f32[4,384,128]{2,1,0:T(8,128)S(1)}, u32[]{:S(2)}, u32[]{:S(2)}) async-start(f32[4,384,128]{2,1,0:T(8,128)} %broadcast_in_dim.16), calls=%async_computation.1 | async-start | bytes 1572864 | tf_op jit(solution)/shard_map/all_to_all | solution.py:577
  92.7 12.3 %collective-permute-start = (f32[1024,128]{1,0:T(8,128)S(1)}, f32[1024,128]{1,0:T(8,128)S(1)}, u32[]{:S(2)}, u32[]{:S(2)}) collective-permute-start(f32[1024,128]{1,0:T(8,128)S(1)} %shard_map.64.pair_ref), channel_id=1, source_target_pairs={{1,0},{2,1},{3,2},{4,3},{5,4},{6,5},{7,6},{8,7},{9,8},{10,9},{11,1... | collective-permute-start | bytes 1572872 | tf_op jit(solution)/shard_map/ppermute | solution.py:597
  96.1 12.8 %collective-permute-start.1 = (f32[1024,128]{1,0:T(8,128)S(1)}, f32[1024,128]{1,0:T(8,128)S(1)}, u32[]{:S(2)}, u32[]{:S(2)}) collective-permute-start(f32[1024,128]{1,0:T(8,128)S(1)} %shard_map.64.pair_ref), channel_id=1, source_target_pairs={{0,1},{1,2},{2,3},{3,4},{4,5},{5,6},{6,7},{7,8},{8,9},{9,10},{10,1... | collective-permute-start | bytes 1572872 | tf_op jit(solution)/shard_map/ppermute | solution.py:597
  101.4 1.2 copy-start.17
  109.7 34.1 %all-to-all-start.3 = ((f32[8,400,128]{2,1,0:T(8,128)}), f32[8,400,128]{2,1,0:T(8,128)}, u32[]{:S(2)}, u32[]{:S(2)}) async-start(f32[8,400,128]{2,1,0:T(8,128)} %copy-done.17), calls=%async_computation.3 | async-start | bytes 3276800 | tf_op jit(solution)/shard_map/all_to_all | solution.py:589
  114.4 1.0 copy-start.3
  115.5 1.0 copy-start.7
  116.5 1.0 copy-start.10
  117.5 1.0 copy-start.13
  118.6 1.0 copy-start.21
  119.6 1.0 copy-start.23
  120.7 1.0 copy-start.25
  122.8 15.3 %collective-permute-start.2 = (f32[512,128]{1,0:T(8,128)S(1)}, f32[512,128]{1,0:T(8,128)S(1)}, u32[]{:S(2)}, u32[]{:S(2)}) collective-permute-start(f32[512,128]{1,0:T(8,128)S(1)} %get-tuple-element.42), channel_id=1, source_target_pairs={{1,0},{2,1},{3,2},{4,3},{5,4},{6,5},{7,6},{8,7},{9,8},{10,9},{11,1... | collective-permute-start | bytes 786440 | tf_op jit(solution)/shard_map/ppermute | solution.py:597
  126.3 12.8 %collective-permute-start.3 = (f32[512,128]{1,0:T(8,128)S(1)}, f32[512,128]{1,0:T(8,128)S(1)}, u32[]{:S(2)}, u32[]{:S(2)}) collective-permute-start(f32[512,128]{1,0:T(8,128)S(1)} %get-tuple-element.42), channel_id=1, source_target_pairs={{0,1},{1,2},{2,3},{3,4},{4,5},{5,6},{6,7},{7,8},{8,9},{9,10},{10,1... | collective-permute-start | bytes 786440 | tf_op jit(solution)/shard_map/ppermute | solution.py:597
  140.4 0.9 copy-start
  141.3 1.0 copy-start.5
  143.8 20.4 %all-to-all-start.2 = ((f32[8,256,128]{2,1,0:T(8,128)}), f32[8,256,128]{2,1,0:T(8,128)}, u32[]{:S(2)}, u32[]{:S(2)}) async-start(f32[8,256,128]{2,1,0:T(8,128)} %copy-done.5), calls=%async_computation.2 | async-start | bytes 2097152 | tf_op jit(solution)/shard_map/all_to_all | solution.py:589
  148.9 19.0 %collective-permute-start.5 = (f32[8,400,128]{2,1,0:T(8,128)}, f32[8,400,128]{2,1,0:T(8,128)}, u32[]{:S(2)}, u32[]{:S(2)}) collective-permute-start(f32[8,400,128]{2,1,0:T(8,128)} %all-to-all-done.3.own_ref), channel_id=1, source_target_pairs={{0,1},{1,0},{2,3},{3,2},{4,5},{5,4},{6,7},{7,6},{8,9},{9,8},{10,11... | collective-permute-start | bytes 4915208 | tf_op jit(solution)/shard_map/ppermute | solution.py:590
  164.2 8.6 %collective-permute-start.4 = (f32[8,256,128]{2,1,0:T(8,128)}, f32[8,256,128]{2,1,0:T(8,128)}, u32[]{:S(2)}, u32[]{:S(2)}) collective-permute-start(f32[8,256,128]{2,1,0:T(8,128)} %all-to-all-done.2.own_ref), channel_id=1, source_target_pairs={{0,1},{1,0},{2,3},{3,2},{4,5},{5,4},{6,7},{7,6},{8,9},{9,8},{10,11... | collective-permute-start | bytes 3145736 | tf_op jit(solution)/shard_map/ppermute | solution.py:590
  167.9 5.0 %copy-start.1 = (f32[1024,128]{1,0:T(8,128)S(1)}, f32[1024,128]{1,0:T(8,128)}, u32[]{:S(2)}) copy-start(f32[1024,128]{1,0:T(8,128)} %copy-done) | copy-start | bytes 1572868
  167.9 5.0 %copy-start.4 = (f32[1024,128]{1,0:T(8,128)S(1)}, f32[1024,128]{1,0:T(8,128)}, u32[]{:S(2)}) copy-start(f32[1024,128]{1,0:T(8,128)} %copy-done.2) | copy-start | bytes 1572868
  167.9 5.0 %copy-start.8 = (f32[1024,128]{1,0:T(8,128)S(1)}, f32[1024,128]{1,0:T(8,128)}, u32[]{:S(2)}) copy-start(f32[1024,128]{1,0:T(8,128)} %copy-done.6) | copy-start | bytes 1572868
  167.9 5.0 %copy-start.11 = (f32[1024,128]{1,0:T(8,128)S(1)}, f32[1024,128]{1,0:T(8,128)}, u32[]{:S(2)}) copy-start(f32[1024,128]{1,0:T(8,128)} %copy-done.9) | copy-start | bytes 1572868
  167.9 5.0 %copy-start.14 = (f32[1024,128]{1,0:T(8,128)S(1)}, f32[1024,128]{1,0:T(8,128)}, u32[]{:S(2)}) copy-start(f32[1024,128]{1,0:T(8,128)} %copy-done.12) | copy-start | bytes 1572868
  167.9 5.0 %copy-start.16 = (f32[1024,128]{1,0:T(8,128)S(1)}, f32[1024,128]{1,0:T(8,128)}, u32[]{:S(2)}) copy-start(f32[1024,128]{1,0:T(8,128)} %copy-done.15) | copy-start | bytes 1572868
  172.9 1.0 copy-start.19
  185.0 7.7 %collective-permute-start.6 = (f32[512,128]{1,0:T(8,128)S(1)}, f32[512,128]{1,0:T(8,128)S(1)}, u32[]{:S(2)}, u32[]{:S(2)}) collective-permute-start(f32[512,128]{1,0:T(8,128)S(1)} %get-tuple-element.52), channel_id=1, source_target_pairs={{1,0},{2,1},{3,2},{4,3},{5,4},{6,5},{7,6},{8,7},{9,8},{10,9},{11,1... | collective-permute-start | bytes 786440 | tf_op jit(solution)/shard_map/ppermute | solution.py:597
  187.0 8.0 %collective-permute-start.7 = (f32[512,128]{1,0:T(8,128)S(1)}, f32[512,128]{1,0:T(8,128)S(1)}, u32[]{:S(2)}, u32[]{:S(2)}) collective-permute-start(f32[512,128]{1,0:T(8,128)S(1)} %get-tuple-element.52), channel_id=1, source_target_pairs={{0,1},{1,2},{2,3},{3,4},{4,5},{5,6},{6,7},{7,8},{8,9},{9,10},{10,1... | collective-permute-start | bytes 786440 | tf_op jit(solution)/shard_map/ppermute | solution.py:597
  211.6 7.7 %collective-permute-start.8 = (f32[8,256,128]{2,1,0:T(8,128)S(1)}, f32[8,256,128]{2,1,0:T(8,128)S(1)}, u32[]{:S(2)}, u32[]{:S(2)}) collective-permute-start(f32[8,256,128]{2,1,0:T(8,128)S(1)} %all_to_all.26.own_ref), channel_id=1, source_target_pairs={{0,1},{1,0},{2,3},{3,2},{4,5},{5,4},{6,7},{7,6},{8,9},{9,8},{10,11... | collective-permute-start | bytes 3145736 | tf_op jit(solution)/shard_map/ppermute | solution.py:590
  (9 other events, 7.1 us)

commit v3 on v2

--- a/solution.py
+++ b/solution.py
@@ -1,4 +1,4 @@
-import functools
+import math
 
 import jax
 import jax.numpy as jnp
@@ -40,6 +40,11 @@
 
 def second_twin(x):
     return jnp.where(low(x), swap(x), x)
+
+
+def twins(x):
+    swapped = swap(x)
+    return jnp.where(low(x), x, swapped), jnp.where(low(x), swapped, x)
 
 
 def glued(values, gluing):
@@ -129,30 +134,33 @@
     return jnp.concatenate(parts, axis=0).T
 
 
-def spread_kernel(arrived_ref, pair_ref):
+def spread_kernel(ready, arrived_ref, pair_ref):
     for group in range(8):
         pair_ref[group * LANES : (group + 1) * LANES] = turned_layer(arrived_ref, 0, 1, group)
 
 
 def lateral_kernel(
-    arrived_ref, pair_ref, gluing_ref, flips_ref, viscous_ref, velocity_ref, force_ref, conds_ref, image_ref,
-    total_ref, faces_ref, viscous_pad, viscous_west, viscous_east, pad, west, east,
+    ready, arrived_ref, pair_ref, gluing_ref, flips_ref, faces_ref, both_ref, rows_ref, columns_ref, lateral_ref,
+    force_ref, viscous, conds, viscous_pad, viscous_west, viscous_east, pad, west, east,
 ):
     gluing, flips = gluing_ref[...], flips_ref[...]
-    viscous_ref[...] = first_twin(pair_ref[...])
-    velocity_ref[...] = second_twin(pair_ref[...])
-    viscous_pad[C : C + CELLS] = viscous_ref[...]
-    pad[C : C + CELLS] = velocity_ref[...]
+    both_ref[...] = pair_ref[...]
+    viscous[...] = first_twin(pair_ref[...])
+    viscous_pad[C : C + CELLS] = viscous[...]
+    pad[C : C + CELLS] = second_twin(pair_ref[...])
     fine_ghosts(viscous_pad, viscous_west, viscous_east, gluing, flips)
     fine_ghosts(pad, west, east, gluing, flips)
 
     def body(i):
+        here = row_of(i)
         own, beside = lateral(viscous_pad, viscous_west, viscous_east, i)
-        conds = [0.5 * (own + other) for other in beside]
+        weights = [0.5 * (own + other) for other in beside]
         for direction in range(4):
-            conds_ref[direction, row_of(i)] = conds[direction]
-        image_ref[row_of(i)] = coupled(conds, lateral(pad, west, east, i)[1])
-        total_ref[row_of(i)] = conds[0] + conds[1] + conds[2] + conds[3]
+            conds[direction, here] = weights[direction]
+        rows_ref[here] = pack(weights[0], weights[1])
+        columns_ref[here] = pack(weights[2], weights[3])
+        image = coupled(weights, lateral(pad, west, east, i)[1])
+        lateral_ref[here] = pack(image, weights[0] + weights[1] + weights[2] + weights[3])
 
     rows_loop(C, 4, body)
     sums, wests = [], []
@@ -164,16 +172,16 @@
             return every(ref, start, HALF) + every(ref, start + 1, HALF)
 
         def column(direction, start):
-            ref = conds_ref.at[direction]
+            ref = conds.at[direction]
             return every(ref, upper + start, HALF) + every(ref, lower + start, HALF)
 
-        faces = pack(both(conds_ref.at[1], lower), column(3, 1))
+        faces = pack(both(conds.at[1], lower), column(3, 1))
         for copy in range(CHIPS):
             faces_ref[copy, cells] = faces
         if big == 0:
-            north = both(conds_ref.at[0], upper)
+            north = both(conds.at[0], upper)
         wests.append(column(2, 0)[0:1])
-        sums.append(both(viscous_ref, upper) + both(viscous_ref, lower))
+        sums.append(both(viscous, upper) + both(viscous, lower))
     start = COARSE + COARSE // 2
     edge = pack(north, jnp.concatenate(wests, axis=0))
     for copy in range(CHIPS):
@@ -186,45 +194,48 @@
 
 
 def first_kernel(
-    force_ref, viscous_ref, velocity_ref, lateral_ref, lateral_total_ref, above_ref, below_ref,
-    radials_ref, total_ref, residual_ref, smoothed_ref, packed_ref,
+    ready, above_ref, below_ref, pair_ref, lateral_ref, force_ref, packed_ref, radials_ref, total_ref, state_ref,
+    residual, smoothed,
 ):
+    ready()
+
     def body(i):
         here = row_of(i)
-        viscous, velocity = viscous_ref[here], velocity_ref[here]
-        beside = above_ref[here], below_ref[here]
-        conds = [radial_weight * 0.5 * (viscous + first_twin(pair)) for pair in beside]
-        cond_total = lateral_total_ref[here] + conds[0] + conds[1]
-        radials_ref[0, here] = conds[0]
-        radials_ref[1, here] = conds[1]
-        total_ref[here] = cond_total
-        image = lateral_ref[here] + conds[0] * second_twin(beside[0]) + conds[1] * second_twin(beside[1])
-        smooth_row(i, force_ref[here], cond_total, velocity, image, residual_ref, smoothed_ref)
+        own, lateral_sums = twins(pair_ref[here]), twins(lateral_ref[here])
+        beside = twins(above_ref[here]), twins(below_ref[here])
+        conds = [radial_weight * 0.5 * (own[0] + other[0]) for other in beside]
+        cond_total = lateral_sums[1] + conds[0] + conds[1]
+        radials_ref[here] = pack(conds[0], conds[1])
+        total_ref[here] = pack(cond_total, force_ref[here])
+        image = lateral_sums[0] + conds[0] * beside[0][1] + conds[1] * beside[1][1]
+        smooth_row(i, force_ref[here], cond_total, own[1], image, residual, smoothed)
+        state_ref[here] = pack(residual[here], smoothed[here])
 
     rows_loop(C, 4, body)
-    pack_halves(smoothed_ref, packed_ref)
+    pack_halves(smoothed, packed_ref)
 
 
 def remain_kernel(
-    conds_ref, radials_ref, total_ref, velocity_ref, residual_ref, smoothed_ref, above_ref, below_ref,
-    gluing_ref, flips_ref, coarse_ref, pad, west, east, remain, damping,
+    ready, gluing_ref, flips_ref, above_ref, below_ref, state_ref, rows_ref, columns_ref, radials_ref, total_ref,
+    velocity_ref, coarse_ref, pad, west, east, remain, damping,
 ):
-    pad[C : C + CELLS] = smoothed_ref[...]
+    ready(0)
+    pad[C : C + CELLS] = second_twin(state_ref[...])
     fine_ghosts(pad, west, east, gluing_ref[...], flips_ref[...])
+    ready(*range(1, 6))
     for upper in range(2):
         offset = upper * (C // 2)
 
         def body(source, upper=upper, offset=offset):
             i = source + offset
             here = row_of(i)
-            velocity = velocity_ref[here]
+            velocity = second_twin(velocity_ref[here])
             damp = 3.0 * (cubic_weight * velocity * velocity)
             own, beside = lateral(pad, west, east, i)
             beside = beside + (unpack_row(above_ref, source, upper), unpack_row(below_ref, source, upper))
-            conds = [conds_ref[direction, here] for direction in range(4)]
-            conds += [radials_ref[direction, here] for direction in range(2)]
-            image = (total_ref[here] + damp) * own - coupled(conds, beside)
-            remain[here] = residual_ref[here] - image
+            conds = twins(rows_ref[here]) + twins(columns_ref[here]) + twins(radials_ref[here])
+            image = (first_twin(total_ref[here]) + damp) * own - coupled(conds, beside)
+            remain[here] = first_twin(state_ref[here]) - image
             damping[here] = damp
 
         rows_loop(C // 2, 4, body)
@@ -264,7 +275,7 @@
 
 
 def faces_kernel(
-    place_ref, own_ref, other_ref, rows_ref, columns_ref, up_ref, down_ref, face_total_ref, sums
+    ready, place_ref, own_ref, other_ref, rows_ref, columns_ref, up_ref, down_ref, face_total_ref, sums
 ):
     middle, last = COARSE, COARSE + COARSE // 2
     half = COARSE // 2
@@ -352,7 +363,6 @@
 ):
     side = HALF * 8
     inner = slice(8, 8 + side)
-    chunk = 64
 
     def arrange(even_ref, odd_ref):
         for sub in range(8):
@@ -384,24 +394,21 @@
     norm = total_over(start)
 
     def apply_row(big, total):
-        for part in range(side // chunk):
-            first = part * chunk
-            here = pl.ds(pl.multiple_of(big * side + first, chunk), chunk)
-            own = pad[big + 1, 8 + first : 8 + first + chunk]
-            above, below = radial_pair(own)
-            south = pl.ds(pl.multiple_of((big + 1) * side + first, chunk), chunk)
-            value = (
-                rows_ref[here] * pad[big, 8 + first : 8 + first + chunk]
-                + rows_ref[south] * pad[big + 2, 8 + first : 8 + first + chunk]
-                + columns_ref[big, first : first + chunk] * pad[big + 1, first : first + chunk]
-                + columns_ref[big, 8 + first : 8 + first + chunk] * pad[big + 1, 16 + first : 16 + first + chunk]
-                + up_ref[here] * above
-                + down_ref[here] * below
-            )
-            value = diagonal[here] * own - value
-            image[here] = value
-            total = total + folded(own * value)
-        return total
+        here, south = here_of(big), here_of(big + 1)
+        row, columns = pad[big + 1], columns_ref[big]
+        own = row[inner]
+        above, below = radial_pair(own)
+        value = (
+            rows_ref[here] * pad[big, inner]
+            + rows_ref[south] * pad[big + 2, inner]
+            + columns[:side] * row[:side]
+            + columns[inner] * row[16 : 16 + side]
+            + up_ref[here] * above
+            + down_ref[here] * below
+        )
+        value = diagonal[here] * own - value
+        image[here] = value
+        return total + folded(own * value)
 
     for step in range(CG_ITERS):
         coarse_ghosts(pad, gluing, flips)
@@ -448,71 +455,111 @@
 
 
 def step_kernel(
-    place_ref, own_ref, other_ref, rows_ref, columns_ref, up_ref, down_ref, face_total_ref, gluing_ref, flips_ref,
-    velocity_ref, above_ref, below_ref, smoothed_ref, smoothed_above_ref, smoothed_below_ref, force_ref,
-    conds_ref, radials_ref, total_ref, new_velocity_ref, new_residual_ref, new_smoothed_ref, packed_ref,
-    pad, diagonal, image, residual, solution, velocity, west, east, above, below, spread,
+    ready, place_ref, own_ref, other_ref, rows_ref, columns_ref, up_ref, down_ref, face_total_ref, gluing_ref,
+    flips_ref, state_ref, smoothed_above_ref, smoothed_below_ref, fine_rows_ref, fine_columns_ref, radials_ref,
+    total_ref, pair_ref, above_ref, below_ref, packed_ref, new_state_ref, new_velocity_ref,
+    pad, diagonal, image, residual, solution, velocity, west, east, above, below, spread, fine_residual, smoothed,
 ):
     gluing, flips = gluing_ref[...], flips_ref[...]
-    for pairs, smooth, target in ((above_ref, smoothed_above_ref, above), (below_ref, smoothed_below_ref, below)):
-        unpack_halves(smooth, target)
-        target[...] = target[...] + second_twin(pairs[...])
     solve_coarse(
         place_ref, own_ref, other_ref, rows_ref, columns_ref, up_ref, down_ref, face_total_ref, gluing, flips,
         pad, diagonal, image, residual, solution,
     )
+    ready()
     layer = place_ref[0]
     prolong_layer(solution, layer, spread)
-    velocity[C : C + CELLS] = velocity_ref[...] + smoothed_ref[...] + spread[...]
+    velocity[C : C + CELLS] = second_twin(pair_ref[...]) + second_twin(state_ref[...]) + spread[...]
     new_velocity_ref[...] = velocity[C : C + CELLS]
     fine_ghosts(velocity, west, east, gluing, flips)
-    for shift, target in ((1, above), (-1, below)):
+    for shift, pairs, smooth, target in (
+        (1, above_ref, smoothed_above_ref, above),
+        (-1, below_ref, smoothed_below_ref, below),
+    ):
         prolong_layer(solution, layer + shift, spread)
-        target[...] = target[...] + spread[...]
+        unpack_halves(smooth, target)
+        target[...] = second_twin(pairs[...]) + target[...] + spread[...]
 
     def body(i):
         here = row_of(i)
         own, beside = lateral(velocity, west, east, i)
         beside = beside + (above[here], below[here])
-        conds = [conds_ref[direction, here] for direction in range(4)]
-        conds += [radials_ref[direction, here] for direction in range(2)]
-        smooth_row(i, force_ref[here], total_ref[here], own, coupled(conds, beside), new_residual_ref, new_smoothed_ref)
+        conds = twins(fine_rows_ref[here]) + twins(fine_columns_ref[here]) + twins(radials_ref[here])
+        cond_total, force = twins(total_ref[here])
+        smooth_row(i, force, cond_total, own, coupled(conds, beside), fine_residual, smoothed)
+        new_state_ref[here] = pack(fine_residual[here], smoothed[here])
 
     rows_loop(C, 4, body)
-    pack_halves(new_smoothed_ref, packed_ref)
+    pack_halves(smoothed, packed_ref)
 
 
 def last_kernel(
-    place_ref, own_ref, other_ref, rows_ref, columns_ref, up_ref, down_ref, face_total_ref, gluing_ref, flips_ref,
-    velocity_ref, smoothed_ref, out_ref, pad, diagonal, image, residual, solution, spread, turned,
+    ready, place_ref, own_ref, other_ref, rows_ref, columns_ref, up_ref, down_ref, face_total_ref, gluing_ref,
+    flips_ref, state_ref, velocity_ref, out_ref, pad, diagonal, image, residual, solution, spread, turned,
 ):
     solve_coarse(
         place_ref, own_ref, other_ref, rows_ref, columns_ref, up_ref, down_ref, face_total_ref,
         gluing_ref[...], flips_ref[...], pad, diagonal, image, residual, solution,
     )
+    ready()
     prolong_layer(solution, place_ref[0], spread)
     for group in range(8):
         cells = slice(group * LANES, (group + 1) * LANES)
-        turned[cells] = (velocity_ref[cells] + smoothed_ref[cells] + spread[cells]).T
+        turned[cells] = (velocity_ref[cells] + second_twin(state_ref[cells]) + spread[cells]).T
     for group in range(8):
         out_ref[group : group + 1] = turned[pl.ds(group * LANES + place_ref[1], 1)]
 
 
-def call(kernel, outs, scratch, args, scalars=0, mebibytes=4):
-    vmem = pl.BlockSpec(memory_space=pltpu.VMEM)
-    shapes = [jax.ShapeDtypeStruct(shape, jnp.float32) for shape in outs]
+VMEM_BYTES = 24 << 20
+CROWDED_BYTES = 125 << 19
+
+
+def call(kernel, outs, scratch, args, scalars=0, fetched=0, stored=0, mebibytes=4, crowded=False):
+    near_args, near_outs = len(args) - fetched, len(outs) - stored
+    room = VMEM_BYTES
+    if crowded:
+        near_shapes = [arg.shape for arg in args[scalars:near_args]] + list(outs[:near_outs])
+        room = CROWDED_BYTES - 4 * sum(math.prod(shape) for shape in near_shapes)
+    far_shapes = [arg.shape for arg in args[near_args:]] + list(outs[near_outs:])
+
+    def body(*refs):
+        ins, results, rest = refs[: len(args)], refs[len(args) : len(args) + len(outs)], refs[len(args) + len(outs) :]
+        semaphores, slots, rest = rest[0], rest[1 : 1 + len(far_shapes)], rest[1 + len(far_shapes) :]
+        incoming = [
+            pltpu.make_async_copy(ins[near_args + k], slots[k], semaphores.at[k]) for k in range(fetched)
+        ]
+        for copy in incoming:
+            copy.start()
+
+        def ready(*numbers):
+            for number in numbers or range(fetched):
+                incoming[number].wait()
+
+        kernel(ready, *ins[:near_args], *slots[:fetched], *results[:near_outs], *slots[fetched:], *rest)
+        outgoing = [
+            pltpu.make_async_copy(slots[fetched + k], results[near_outs + k], semaphores.at[fetched + k])
+            for k in range(stored)
+        ]
+        for copy in outgoing:
+            copy.start()
+        for copy in outgoing:
+            copy.wait()
+
+    def specs(near, far):
+        return [pl.BlockSpec(memory_space=pltpu.VMEM)] * near + [pl.BlockSpec(memory_space=pltpu.HBM)] * far
+
     return pl.pallas_call(
-        kernel,
-        out_shape=shapes,
-        in_specs=[pl.BlockSpec(memory_space=pltpu.SMEM)] * scalars + [vmem] * (len(args) - scalars),
-        out_specs=[vmem] * len(outs),
-        scratch_shapes=[pltpu.VMEM(shape, jnp.float32) for shape in scratch],
-        compiler_params=pltpu.CompilerParams(vmem_limit_bytes=VMEM_MIB << 20),
+        body,
+        out_shape=[jax.ShapeDtypeStruct(shape, jnp.float32) for shape in outs],
+        in_specs=[pl.BlockSpec(memory_space=pltpu.SMEM)] * scalars + specs(near_args - scalars, fetched),
+        out_specs=specs(near_outs, stored),
+        scratch_shapes=[pltpu.SemaphoreType.DMA((max(len(far_shapes), 1),))]
+        + [pltpu.VMEM(shape, jnp.float32) for shape in far_shapes + scratch],
+        compiler_params=pltpu.CompilerParams(vmem_limit_bytes=room),
         cost_estimate=pl.CostEstimate(flops=mebibytes << 20, bytes_accessed=mebibytes << 20, transcendentals=0),
+        name=kernel.__name__,
     )(*args)
 
 
-VMEM_MIB = 20
 PADDED = (CELLS + 2 * C, LANES)
 FINE = (CELLS, LANES)
 PACKED = (CELLS // 2, LANES)
@@ -527,30 +574,31 @@
 
 
 def lateral_stage(*args):
-    outs = [FINE, FINE, FINE, (4,) + FINE, FINE, FINE, FACES]
-    return call(lateral_kernel, outs, [PADDED, EDGE, EDGE, PADDED, EDGE, EDGE], args, mebibytes=24)
+    scratch = [FINE, (4,) + FINE, PADDED, EDGE, EDGE, PADDED, EDGE, EDGE]
+    return call(lateral_kernel, [FACES] + [FINE] * 5, scratch, args, stored=5, mebibytes=24, crowded=True)
 
 
 def first_stage(*args):
-    return call(first_kernel, [(2,) + FINE, FINE, FINE, FINE, PACKED], [], args)
-
-
-def remain_stage(*args):
-    return call(remain_kernel, [(CHIPS, COARSE, LANES)], [PADDED, EDGE, EDGE, FINE, FINE], args)[0]
+    return call(first_kernel, [PACKED] + [FINE] * 3, [FINE, FINE], args, fetched=3, stored=3, crowded=True)
+
+
+def remain_stage(*args, crowded):
+    scratch = [PADDED, EDGE, EDGE, FINE, FINE]
+    return call(remain_kernel, [(CHIPS, COARSE, LANES)], scratch, args, fetched=6, crowded=crowded)[0]
 
 
 def faces_stage(*args):
     outs = [((HALF + 1) * HALF * 8, LANES), (HALF, (HALF + 1) * 8, LANES)] + [GRID] * 3
-    return call(faces_kernel, outs, [GRID], args, 1, 24)
+    return call(faces_kernel, outs, [GRID], args, 1, mebibytes=24)
 
 
 def step_stage(*args):
-    scratch = COARSE_SCRATCH + [PADDED, EDGE, EDGE, FINE, FINE, FINE]
-    return call(step_kernel, [FINE, FINE, FINE, PACKED], scratch, args, 1)
+    scratch = COARSE_SCRATCH + [PADDED, EDGE, EDGE] + [FINE] * 5
+    return call(step_kernel, [PACKED, FINE, FINE], scratch, args, 1, fetched=10, stored=2)
 
 
 def last_stage(*args):
-    return call(last_kernel, [(8, LANES)], COARSE_SCRATCH + [FINE, FINE], args, 1)[0]
+    return call(last_kernel, [(8, LANES)], COARSE_SCRATCH + [FINE, FINE], args, 1, fetched=2)[0]
 
 
 NEAR = 4
@@ -603,22 +651,19 @@
     own = jnp.concatenate([field.reshape(8, LANES) for field in (viscosity, initial_guess, rhs_force)], axis=0)
     arrived = gather_lateral(own)
     pair = spread_layer(arrived)
-    pair_beside = radial(pair)
-    viscous, velocity, force, conds, lateral_image, lateral_total, faces = lateral_stage(arrived, pair, *tables)
-    faces, *pair_beside = lax.optimization_barrier((faces, *pair_beside))
-    radials, total, residual, smoothed, packed = first_stage(
-        force, viscous, velocity, lateral_image, lateral_total, *pair_beside
-    )
+    beside = radial(pair)
+    faces, pair, rows, columns, lateral_sums, force = lateral_stage(arrived, pair, *tables)
+    faces, *beside = lax.optimization_barrier((faces, *beside))
+    packed, radials, total, state = first_stage(*beside, pair, lateral_sums, force)
     smoothed_beside = radial(packed)
     coefficients = faces_stage(place, *gather_radial(faces))
-    coarse = remain_stage(conds, radials, total, velocity, residual, smoothed, *smoothed_beside, *tables)
-    velocity, residual, smoothed, packed = step_stage(
-        place, *gather_radial(coarse), *coefficients, *tables, velocity, *pair_beside, smoothed,
-        *smoothed_beside, force, conds, radials, total,
+    fine = rows, columns, radials, total
+    coarse = remain_stage(*tables, *smoothed_beside, state, *fine, pair, crowded=True)
+    packed, state, velocity = step_stage(
+        place, *gather_radial(coarse), *coefficients, *tables, state, *smoothed_beside, *fine, pair, *beside
     )
-    smoothed_beside = radial(packed)
-    coarse = remain_stage(conds, radials, total, velocity, residual, smoothed, *smoothed_beside, *tables)
-    out = last_stage(place, *gather_radial(coarse), *coefficients, *tables, velocity, smoothed)
+    coarse = remain_stage(*tables, *radial(packed), state, *fine, velocity, crowded=False)
+    out = last_stage(place, *gather_radial(coarse), *coefficients, *tables, state, velocity)
     return out.reshape(1, CELLS)
 
 

time: 230 us -> 236 us (1.026)
  Pallas kernels: 30.9 us -> 46.7 us
  local copies, waits for them, and re-layouts: 20.7 us -> 6.77 us
    pallas_call x8, Pallas kernels: 30.9 us -> 46.7 us  [call(): pl.pallas_call(body, out_shape=[jax.ShapeDtypeStruct(shape, jnp.float32)...]
    unnamed x59 -> x43, local copies, waits for them, and re-layouts: 18.5 us -> 4.59 us
  transfers between devices with their start and end apart: 12 -> 12, of which waited for: 8 -> 8; matrix products, arithmetic and copies ran while one was open for 1% -> 1% of each run, Pallas kernels for 4% -> 9%
where the time goes in v3:
time: 236 us; the launch traced here: 235 us
  blocking collectives  76.4 us (32%)
  waiting for transfers between devices  51.7 us (22%)
  starting transfers between devices  50.7 us (21%)
  Pallas kernels  46.7 us (20%)
  local copies, waits for them, and re-layouts  6.77 us (3%)
    all_to_all x1, blocking collectives, gather(): lax.all_to_all(sent, axis, split_axis=0, concat_axis=0, axis_index_groups...  61.2 us
    pallas_call x8, Pallas kernels, call(): pl.pallas_call(body, out_shape=[jax.ShapeDtypeStruct(shape, jnp.float32)...  46.7 us
    all_to_all x1, waiting for transfers between devices, gather(): lax.all_to_all(sent, axis, split_axis=0, concat_axis=0, axis_index_groups...  18.2 us
    all_to_all x1, blocking collectives, gather_radial(): lax.all_to_all(copies, 'rad', split_axis=0, concat_axis=0, axis_index_gro...  15.2 us
    all_to_all x2, waiting for transfers between devices, gather_radial(): lax.all_to_all(copies, 'rad', split_axis=0, concat_axis=0, axis_index_gro...  12.5 us
    ppermute x3, waiting for transfers between devices, radial(): lax.ppermute(values, 'rad', backward)  12.1 us
    ppermute x3, starting transfers between devices, gather_radial(): lax.ppermute(own, 'rad', [(layer, layer ^ 1) for layer in range(NR)])  11.7 us
    all_to_all x2, starting transfers between devices, gather_radial(): lax.all_to_all(copies, 'rad', split_axis=0, concat_axis=0, axis_index_gro...  10.1 us
  transfers between devices with their start and end apart: 12, of which 8 were waited for; matrix products, arithmetic and copies ran while one was open for 1% of the time, Pallas kernels for 9%

profile of v3, /device:TPU:1, one launch (start us, length us, event | category | flops | bytes accessed | tf_op | source)
XLA Modules:
  0.0 235.1 jit_solution(11428690202617967219)
XLA Ops:
  0.8 61.2 %all_to_all.25 = f32[16,24,128]{2,1,0:T(8,128)S(1)} all-to-all(f32[16,24,128]{2,1,0:T(8,128)S(1)} %broadcast_in_dim.6), channel_id=1, replica_groups={{0,16,128,144,256,272,384,400,512,528,640,656,768,784,896,912},{32,48,1..., dimensions={0} | all-to-all | bytes 393216 | tf_op jit(solution)/shard_map/all_to_all | solution.py:625
  61.9 0.9 broadcast_in_dim.16
  62.9 10.0 %all-to-all-start.1 = ((f32[4,384,128]{2,1,0:T(8,128)}), f32[4,384,128]{2,1,0:T(8,128)S(1)}, u32[]{:S(2)}, u32[]{:S(2)}) async-start(f32[4,384,128]{2,1,0:T(8,128)} %broadcast_in_dim.16), calls=%async_computation.1 | async-start | bytes 1572864 | tf_op jit(solution)/shard_map/all_to_all | solution.py:625
  74.2 18.2 %all-to-all-done.1 = f32[4,384,128]{2,1,0:T(8,128)S(1)} async-done(((f32[4,384,128]{2,1,0:T(8,128)}), f32[4,384,128]{2,1,0:T(8,128)S(1)}, u32[]{:S(2)}, u32[]{:S(2)}) %all-to-all-start.1) | async-done | bytes 786464 | tf_op jit(solution)/shard_map/all_to_all | solution.py:625
  92.7 3.4 %collective-permute-start = (f32[1024,128]{1,0:T(8,128)S(1)}, f32[1024,128]{1,0:T(8,128)S(1)}, u32[]{:S(2)}, u32[]{:S(2)}) collective-permute-start(f32[1024,128]{1,0:T(8,128)S(1)} %spread_kernel.1.refs_1_), channel_id=1, source_target_pairs={{1,0},{2,1},{3,2},{4,3},{5,4},{6,5},{7,6},{8,7},{9,8},{10,9},{11,1... | collective-permute-start | bytes 1572872 | tf_op jit(solution)/shard_map/ppermute | solution.py:645
  96.1 2.2 collective-permute-start.1
  99.7 5.1 %lateral_kernel.1 = (f32[8,400,128]{2,1,0:T(8,128)}, f32[1024,128]{1,0:T(8,128)}, f32[1024,128]{1,0:T(8,128)}, f32[1024,128]{1,0:T(8,128)}, f32[1024,128]{1,0:T(8,128)}, /*index=5*/f32[1024,128]{1,0:T(8,128)}) custom-call(f32[1536,128]{1,0:T(8,128)} %bitcast.23, f32[1024,128]{1,0:T(8,128)} %copy-done.11, bf16[256,256]{1,0:T(8,128)(2,1)} %fusion.refs_2_.refs_0_.refs_8_, ...), custom_call_target="tpu_custom_call" | custom-call | flops 25165824 | bytes 25165824 | tf_op jit(solution)/shard_map/lateral_kernel/pallas_call | solution.py:550
  104.8 4.1 %collective-permute-done.1.refs_1_.refs_19_ = f32[1024,128]{1,0:T(8,128)S(1)} collective-permute-done((f32[1024,128]{1,0:T(8,128)S(1)}, f32[1024,128]{1,0:T(8,128)S(1)}, u32[]{:S(2)}, u32[]{:S(2)}) %collective-permute-start.1) | collective-permute-done | bytes 524320 | tf_op jit(solution)/shard_map/ppermute | solution.py:645
  109.7 4.1 %all-to-all-start.3 = ((f32[8,400,128]{2,1,0:T(8,128)}), f32[8,400,128]{2,1,0:T(8,128)S(1)}, u32[]{:S(2)}, u32[]{:S(2)}) async-start(f32[8,400,128]{2,1,0:T(8,128)} %get-tuple-element.38), calls=%async_computation.3 | async-start | bytes 3276800 | tf_op jit(solution)/shard_map/all_to_all | solution.py:637
  113.8 5.8 %first_kernel.1 = (f32[512,128]{1,0:T(8,128)}, f32[1024,128]{1,0:T(8,128)}, f32[1024,128]{1,0:T(8,128)}, f32[1024,128]{1,0:T(8,128)}) custom-call(f32[1024,128]{1,0:T(8,128)} %copy-done.7, f32[1024,128]{1,0:T(8,128)} %copy-done.9, f32[1024,128]{1,0:T(8,128)} %get-tuple-element.29.refs_2_.refs_9_.refs_17_, f32[1024,128]{1,0:T(8,128)} %get-tuple-element.30.refs_3_, ...), custom_call_target="tpu_custom_call" | custom-call | flops 4194304 | bytes 4194304 | tf_op jit(solution)/shard_map/first_kernel/pallas_call | solution.py:550
  119.6 4.1 %collective-permute-start.2 = (f32[512,128]{1,0:T(8,128)}, f32[512,128]{1,0:T(8,128)S(1)}, u32[]{:S(2)}, u32[]{:S(2)}) collective-permute-start(f32[512,128]{1,0:T(8,128)} %get-tuple-element.32), channel_id=1, source_target_pairs={{1,0},{2,1},{3,2},{4,3},{5,4},{6,5},{7,6},{8,7},{9,8},{10,9},{11,1... | collective-permute-start | bytes 786440 | tf_op jit(solution)/shard_map/ppermute | solution.py:645
  123.7 3.5 %collective-permute-start.3 = (f32[512,128]{1,0:T(8,128)}, f32[512,128]{1,0:T(8,128)S(1)}, u32[]{:S(2)}, u32[]{:S(2)}) collective-permute-start(f32[512,128]{1,0:T(8,128)} %get-tuple-element.32), channel_id=1, source_target_pairs={{0,1},{1,2},{2,3},{3,4},{4,5},{5,6},{6,7},{7,8},{8,9},{9,10},{10,1... | collective-permute-start | bytes 786440 | tf_op jit(solution)/shard_map/ppermute | solution.py:645
  127.3 10.1 %collective-permute-done.2.refs_2_.refs_11_ = f32[512,128]{1,0:T(8,128)S(1)} collective-permute-done((f32[512,128]{1,0:T(8,128)}, f32[512,128]{1,0:T(8,128)S(1)}, u32[]{:S(2)}, u32[]{:S(2)}) %collective-permute-start.2) | collective-permute-done | bytes 262176 | tf_op jit(solution)/shard_map/ppermute | solution.py:645
  138.5 5.7 %remain_kernel.2 = f32[8,256,128]{2,1,0:T(8,128)} custom-call(bf16[256,256]{1,0:T(8,128)(2,1)} %fusion.refs_2_.refs_0_.refs_8_, f32[8,128]{1,0:T(8,128)} %maximum_maximum_fusion.refs_3_.refs_1_.refs_9_, f32[512,128]{1,0:T(8,128)} %copy-done.13, f32[512,128]{1,0:T(8,128)} %copy-done.15, f32[1024,128]{1,0:T(8,128)} %get-tuple-element.33.refs_4_.refs_10_, ...), custom_call_target="tpu_custom_call" | custom-call | flops 4194304 | bytes 4194304 | tf_op jit(solution)/shard_map/remain_kernel/pallas_call | solution.py:550
  144.2 6.0 %all-to-all-start.2 = ((f32[8,256,128]{2,1,0:T(8,128)}), f32[8,256,128]{2,1,0:T(8,128)S(1)}, u32[]{:S(2)}, u32[]{:S(2)}) async-start(f32[8,256,128]{2,1,0:T(8,128)} %remain_kernel.2), calls=%async_computation.2 | async-start | bytes 2097152 | tf_op jit(solution)/shard_map/all_to_all | solution.py:637
  150.2 2.8 %collective-permute-start.5 = (f32[8,400,128]{2,1,0:T(8,128)S(1)}, f32[8,400,128]{2,1,0:T(8,128)}, u32[]{:S(2)}, u32[]{:S(2)}) collective-permute-start(f32[8,400,128]{2,1,0:T(8,128)S(1)} %all-to-all-done.3.refs_1_), channel_id=1, source_target_pairs={{0,1},{1,0},{2,3},{3,2},{4,5},{5,4},{6,7},{7,6},{8,9},{9,8},{10,11... | collective-permute-start | bytes 4915208 | tf_op jit(solution)/shard_map/ppermute | solution.py:638
  153.0 12.5 %all-to-all-done.2.refs_1_ = f32[8,256,128]{2,1,0:T(8,128)S(1)} async-done(((f32[8,256,128]{2,1,0:T(8,128)}), f32[8,256,128]{2,1,0:T(8,128)S(1)}, u32[]{:S(2)}, u32[]{:S(2)}) %all-to-all-start.2) | async-done | bytes 1048608 | tf_op jit(solution)/shard_map/all_to_all | solution.py:637
  165.5 3.5 %collective-permute-start.4 = (f32[8,256,128]{2,1,0:T(8,128)S(1)}, f32[8,256,128]{2,1,0:T(8,128)}, u32[]{:S(2)}, u32[]{:S(2)}) collective-permute-start(f32[8,256,128]{2,1,0:T(8,128)S(1)} %all-to-all-done.2.refs_1_), channel_id=1, source_target_pairs={{0,1},{1,0},{2,3},{3,2},{4,5},{5,4},{6,7},{7,6},{8,9},{9,8},{10,11... | collective-permute-start | bytes 3145736 | tf_op jit(solution)/shard_map/ppermute | solution.py:638
  169.2 4.4 %faces_kernel.1 = (f32[2176,128]{1,0:T(8,128)S(1)}, f32[16,136,128]{2,1,0:T(8,128)S(1)}, f32[2048,128]{1,0:T(8,128)S(1)}, f32[2048,128]{1,0:T(8,128)S(1)}, f32[2048,128]{1,0:T(8,128)S(1)}) custom-call(s32[2]{0:T(128)S(1)} %pad_add_fusion.refs_0_, f32[8,400,128]{2,1,0:T(8,128)S(1)} %all-to-all-done.3.refs_1_, f32[8,400,128]{2,1,0:T(8,128)} %collective-permute-done.5.refs_2_), custom_call_target="tpu_custom_call" | custom-call | flops 25165824 | bytes 25165824 | tf_op jit(solution)/shard_map/faces_kernel/pallas_call | solution.py:550
  173.8 1.0 copy-done.12
  174.8 0.9 copy-done.14
  175.8 0.9 copy-done.16
  176.7 12.8 %step_kernel.1 = (f32[512,128]{1,0:T(8,128)S(1)}, f32[1024,128]{1,0:T(8,128)S(1)}, f32[1024,128]{1,0:T(8,128)S(1)}) custom-call(s32[2]{0:T(128)S(1)} %pad_add_fusion.refs_0_, f32[8,256,128]{2,1,0:T(8,128)S(1)} %all-to-all-done.2.refs_1_, f32[8,256,128]{2,1,0:T(8,128)} %collective-permute-done.4.refs_2_, f32[2176,128]{1,0:T(8,128)S(1)} %get-tuple-element.39.refs_3_, ...), custom_call_target="tpu_custom_call" | custom-call | flops 4194304 | bytes 4194304 | tf_op jit(solution)/shard_map/step_kernel/pallas_call | solution.py:550
  189.5 1.9 collective-permute-start.6
  191.4 3.8 %collective-permute-start.7 = (f32[512,128]{1,0:T(8,128)S(1)}, f32[512,128]{1,0:T(8,128)S(1)}, u32[]{:S(2)}, u32[]{:S(2)}) collective-permute-start(f32[512,128]{1,0:T(8,128)S(1)} %get-tuple-element.44), channel_id=1, source_target_pairs={{0,1},{1,2},{2,3},{3,4},{4,5},{5,6},{6,7},{7,8},{8,9},{9,10},{10,1... | collective-permute-start | bytes 786440 | tf_op jit(solution)/shard_map/ppermute | solution.py:645
  195.3 1.9 collective-permute-done.6.refs_2_
  197.2 2.2 collective-permute-done.7.refs_3_
  199.4 2.5 %remain_kernel.3 = f32[8,256,128]{2,1,0:T(8,128)S(1)} custom-call(bf16[256,256]{1,0:T(8,128)(2,1)S(1)} %copy-done.1, f32[8,128]{1,0:T(8,128)S(1)} %copy-done.17, f32[512,128]{1,0:T(8,128)S(1)} %collective-permute-done.6.refs_2_, f32[512,128]{1,0:T(8,128)S(1)} %collective-permute-done.7.refs_3_, f32[1024,128]{1,0:T(8,128)S(1)} %get-tuple-element.45.refs_4_.refs_10_, ...), custom_call_target="tpu_custom_call" | custom-call | flops 4194304 | bytes 4194304 | tf_op jit(solution)/shard_map/remain_kernel/pallas_call | solution.py:550
  201.9 15.2 %all_to_all.26.refs_1_ = f32[8,256,128]{2,1,0:T(8,128)S(1)} all-to-all(f32[8,256,128]{2,1,0:T(8,128)S(1)} %remain_kernel.3), channel_id=1, replica_groups={{0,2,4,6,8,10,12,14},{1,3,5,7,9,11,13,15},{16,18,20,22,24,26,28,30},{17..., dimensions={0} | all-to-all | bytes 2097152 | tf_op jit(solution)/shard_map/all_to_all | solution.py:637
  217.1 5.4 %collective-permute-start.8 = (f32[8,256,128]{2,1,0:T(8,128)S(1)}, f32[8,256,128]{2,1,0:T(8,128)S(1)}, u32[]{:S(2)}, u32[]{:S(2)}) collective-permute-start(f32[8,256,128]{2,1,0:T(8,128)S(1)} %all_to_all.26.refs_1_), channel_id=1, source_target_pairs={{0,1},{1,0},{2,3},{3,2},{4,5},{5,4},{6,7},{7,6},{8,9},{9,8},{10,11... | collective-permute-start | bytes 3145736 | tf_op jit(solution)/shard_map/ppermute | solution.py:638
  222.5 2.3 collective-permute-done.8.refs_2_
  224.8 10.1 %last_kernel.1 = f32[8,128]{1,0:T(8,128)} custom-call(s32[2]{0:T(128)S(1)} %pad_add_fusion.refs_0_, f32[8,256,128]{2,1,0:T(8,128)S(1)} %all_to_all.26.refs_1_, f32[8,256,128]{2,1,0:T(8,128)S(1)} %collective-permute-done.8.refs_2_, f32[2176,128]{1,0:T(8,128)S(1)} %get-tuple-element.39.refs_3_, f32[16,136,128]{2,1,0:T(8,128)S(1)} %get-tuple-element.40.refs_4_, ...), custom_call_target="tpu_custom_call" | custom-call | flops 4194304 | bytes 4194304 | tf_op jit(solution)/shard_map/last_kernel/pallas_call | solution.py:550
  (62 shorter events, 5.7 us)
Async XLA Ops:
  0.0 72.9 %copy-start.19 = (s32[64,4]{0,1:T(4,128)S(1)}, s32[64,4]{0,1:T(4,128)}, u32[]{:S(2)}) copy-start(s32[64,4]{0,1:T(4,128)} %param.10) | copy-start | bytes 3076
  0.7 72.7 %copy-start.18 = (s32[64,4]{0,1:T(4,128)S(1)}, s32[64,4]{0,1:T(4,128)}, u32[]{:S(2)}) copy-start(s32[64,4]{0,1:T(4,128)} %param.9) | copy-start | bytes 3076
  0.8 73.3 %copy-start.20 = (s32[64,4]{0,1:T(4,128)S(1)}, s32[64,4]{0,1:T(4,128)}, u32[]{:S(2)}) copy-start(s32[64,4]{0,1:T(4,128)} %param.11) | copy-start | bytes 3076
  62.9 29.6 %all-to-all-start.1 = ((f32[4,384,128]{2,1,0:T(8,128)}), f32[4,384,128]{2,1,0:T(8,128)S(1)}, u32[]{:S(2)}, u32[]{:S(2)}) async-start(f32[4,384,128]{2,1,0:T(8,128)} %broadcast_in_dim.16), calls=%async_computation.1 | async-start | bytes 1572864 | tf_op jit(solution)/shard_map/all_to_all | solution.py:625
  92.5 7.2 %copy-start = (f32[4,384,128]{2,1,0:T(8,128)}, f32[4,384,128]{2,1,0:T(8,128)S(1)}, u32[]{:S(2)}) copy-start(f32[4,384,128]{2,1,0:T(8,128)S(1)} %all-to-all-done.1) | copy-start | bytes 2359300
  92.7 7.0 %copy-start.11 = (f32[1024,128]{1,0:T(8,128)}, f32[1024,128]{1,0:T(8,128)S(1)}, u32[]{:S(2)}) copy-start(f32[1024,128]{1,0:T(8,128)S(1)} %spread_kernel.1.refs_1_) | copy-start | bytes 1572868
  92.7 12.1 %collective-permute-start = (f32[1024,128]{1,0:T(8,128)S(1)}, f32[1024,128]{1,0:T(8,128)S(1)}, u32[]{:S(2)}, u32[]{:S(2)}) collective-permute-start(f32[1024,128]{1,0:T(8,128)S(1)} %spread_kernel.1.refs_1_), channel_id=1, source_target_pairs={{1,0},{2,1},{3,2},{4,3},{5,4},{6,5},{7,6},{8,7},{9,8},{10,9},{11,1... | collective-permute-start | bytes 1572872 | tf_op jit(solution)/shard_map/ppermute | solution.py:645
  96.1 12.8 %collective-permute-start.1 = (f32[1024,128]{1,0:T(8,128)S(1)}, f32[1024,128]{1,0:T(8,128)S(1)}, u32[]{:S(2)}, u32[]{:S(2)}) collective-permute-start(f32[1024,128]{1,0:T(8,128)S(1)} %spread_kernel.1.refs_1_), channel_id=1, source_target_pairs={{0,1},{1,2},{2,3},{3,4},{4,5},{5,6},{6,7},{7,8},{8,9},{9,10},{10,1... | collective-permute-start | bytes 1572872 | tf_op jit(solution)/shard_map/ppermute | solution.py:645
  104.8 4.1 %copy-start.7 = (f32[1024,128]{1,0:T(8,128)}, f32[1024,128]{1,0:T(8,128)S(1)}, u32[]{:S(2)}) copy-start(f32[1024,128]{1,0:T(8,128)S(1)} %collective-permute-done.refs_0_.refs_18_) | copy-start | bytes 1572868
  108.9 0.8 copy-start.9
  109.7 34.5 %all-to-all-start.3 = ((f32[8,400,128]{2,1,0:T(8,128)}), f32[8,400,128]{2,1,0:T(8,128)S(1)}, u32[]{:S(2)}, u32[]{:S(2)}) async-start(f32[8,400,128]{2,1,0:T(8,128)} %get-tuple-element.38), calls=%async_computation.3 | async-start | bytes 3276800 | tf_op jit(solution)/shard_map/all_to_all | solution.py:637
  119.6 17.8 %collective-permute-start.2 = (f32[512,128]{1,0:T(8,128)}, f32[512,128]{1,0:T(8,128)S(1)}, u32[]{:S(2)}, u32[]{:S(2)}) collective-permute-start(f32[512,128]{1,0:T(8,128)} %get-tuple-element.32), channel_id=1, source_target_pairs={{1,0},{2,1},{3,2},{4,3},{5,4},{6,5},{7,6},{8,7},{9,8},{10,9},{11,1... | collective-permute-start | bytes 786440 | tf_op jit(solution)/shard_map/ppermute | solution.py:645
  123.7 14.1 %collective-permute-start.3 = (f32[512,128]{1,0:T(8,128)}, f32[512,128]{1,0:T(8,128)S(1)}, u32[]{:S(2)}, u32[]{:S(2)}) collective-permute-start(f32[512,128]{1,0:T(8,128)} %get-tuple-element.32), channel_id=1, source_target_pairs={{0,1},{1,2},{2,3},{3,4},{4,5},{5,6},{6,7},{7,8},{8,9},{9,10},{10,1... | collective-permute-start | bytes 786440 | tf_op jit(solution)/shard_map/ppermute | solution.py:645
  137.8 0.7 copy-start.15
  144.2 29.4 %copy-start.10 = (f32[1024,128]{1,0:T(8,128)S(1)}, f32[1024,128]{1,0:T(8,128)}, u32[]{:S(2)}) copy-start(f32[1024,128]{1,0:T(8,128)} %copy-done.9) | copy-start | bytes 1572868
  144.2 21.3 %all-to-all-start.2 = ((f32[8,256,128]{2,1,0:T(8,128)}), f32[8,256,128]{2,1,0:T(8,128)S(1)}, u32[]{:S(2)}, u32[]{:S(2)}) async-start(f32[8,256,128]{2,1,0:T(8,128)} %remain_kernel.2), calls=%async_computation.2 | async-start | bytes 2097152 | tf_op jit(solution)/shard_map/all_to_all | solution.py:637
  150.2 19.0 %collective-permute-start.5 = (f32[8,400,128]{2,1,0:T(8,128)S(1)}, f32[8,400,128]{2,1,0:T(8,128)}, u32[]{:S(2)}, u32[]{:S(2)}) collective-permute-start(f32[8,400,128]{2,1,0:T(8,128)S(1)} %all-to-all-done.3.refs_1_), channel_id=1, source_target_pairs={{0,1},{1,0},{2,3},{3,2},{4,5},{5,4},{6,7},{7,6},{8,9},{9,8},{10,11... | collective-permute-start | bytes 4915208 | tf_op jit(solution)/shard_map/ppermute | solution.py:638
  165.5 8.1 %collective-permute-start.4 = (f32[8,256,128]{2,1,0:T(8,128)S(1)}, f32[8,256,128]{2,1,0:T(8,128)}, u32[]{:S(2)}, u32[]{:S(2)}) collective-permute-start(f32[8,256,128]{2,1,0:T(8,128)S(1)} %all-to-all-done.2.refs_1_), channel_id=1, source_target_pairs={{0,1},{1,0},{2,3},{3,2},{4,5},{5,4},{6,7},{7,6},{8,9},{9,8},{10,11... | collective-permute-start | bytes 3145736 | tf_op jit(solution)/shard_map/ppermute | solution.py:638
  169.2 4.5 %copy-start.1 = (bf16[256,256]{1,0:T(8,128)(2,1)S(1)}, bf16[256,256]{1,0:T(8,128)(2,1)}, u32[]{:S(2)}) copy-start(bf16[256,256]{1,0:T(8,128)(2,1)} %fusion.refs_2_.refs_0_.refs_8_) | copy-start | bytes 393220
  169.2 4.5 %copy-start.2 = (f32[1024,128]{1,0:T(8,128)S(1)}, f32[1024,128]{1,0:T(8,128)}, u32[]{:S(2)}) copy-start(f32[1024,128]{1,0:T(8,128)} %get-tuple-element.29.refs_2_.refs_9_.refs_17_) | copy-start | bytes 1572868
  169.2 4.5 %copy-start.3 = (f32[1024,128]{1,0:T(8,128)S(1)}, f32[1024,128]{1,0:T(8,128)}, u32[]{:S(2)}) copy-start(f32[1024,128]{1,0:T(8,128)} %get-tuple-element.34.refs_5_.refs_13_) | copy-start | bytes 1572868
  169.2 4.5 %copy-start.4 = (f32[1024,128]{1,0:T(8,128)S(1)}, f32[1024,128]{1,0:T(8,128)}, u32[]{:S(2)}) copy-start(f32[1024,128]{1,0:T(8,128)} %get-tuple-element.35.refs_6_.refs_14_) | copy-start | bytes 1572868
  169.2 4.6 %copy-start.5 = (f32[1024,128]{1,0:T(8,128)S(1)}, f32[1024,128]{1,0:T(8,128)}, u32[]{:S(2)}) copy-start(f32[1024,128]{1,0:T(8,128)} %get-tuple-element.36.refs_7_.refs_15_) | copy-start | bytes 1572868
  169.2 4.6 %copy-start.6 = (f32[1024,128]{1,0:T(8,128)S(1)}, f32[1024,128]{1,0:T(8,128)}, u32[]{:S(2)}) copy-start(f32[1024,128]{1,0:T(8,128)} %get-tuple-element.37.refs_8_.refs_16_) | copy-start | bytes 1572868
  169.2 4.6 %copy-start.8 = (f32[1024,128]{1,0:T(8,128)S(1)}, f32[1024,128]{1,0:T(8,128)}, u32[]{:S(2)}) copy-start(f32[1024,128]{1,0:T(8,128)} %copy-done.7) | copy-start | bytes 1572868
  169.2 4.6 %copy-start.17 = (f32[8,128]{1,0:T(8,128)S(1)}, f32[8,128]{1,0:T(8,128)}, u32[]{:S(2)}) copy-start(f32[8,128]{1,0:T(8,128)} %maximum_maximum_fusion.refs_3_.refs_1_.refs_9_) | copy-start | bytes 12292
  173.8 1.0 copy-start.12
  174.8 0.9 copy-start.14
  175.7 0.9 copy-start.16
  189.5 7.7 %collective-permute-start.6 = (f32[512,128]{1,0:T(8,128)S(1)}, f32[512,128]{1,0:T(8,128)S(1)}, u32[]{:S(2)}, u32[]{:S(2)}) collective-permute-start(f32[512,128]{1,0:T(8,128)S(1)} %get-tuple-element.44), channel_id=1, source_target_pairs={{1,0},{2,1},{3,2},{4,3},{5,4},{6,5},{7,6},{8,7},{9,8},{10,9},{11,1... | collective-permute-start | bytes 786440 | tf_op jit(solution)/shard_map/ppermute | solution.py:645
  191.4 8.0 %collective-permute-start.7 = (f32[512,128]{1,0:T(8,128)S(1)}, f32[512,128]{1,0:T(8,128)S(1)}, u32[]{:S(2)}, u32[]{:S(2)}) collective-permute-start(f32[512,128]{1,0:T(8,128)S(1)} %get-tuple-element.44), channel_id=1, source_target_pairs={{0,1},{1,2},{2,3},{3,4},{4,5},{5,6},{6,7},{7,8},{8,9},{9,10},{10,1... | collective-permute-start | bytes 786440 | tf_op jit(solution)/shard_map/ppermute | solution.py:645
  217.1 7.7 %collective-permute-start.8 = (f32[8,256,128]{2,1,0:T(8,128)S(1)}, f32[8,256,128]{2,1,0:T(8,128)S(1)}, u32[]{:S(2)}, u32[]{:S(2)}) collective-permute-start(f32[8,256,128]{2,1,0:T(8,128)S(1)} %all_to_all.26.refs_1_), channel_id=1, source_target_pairs={{0,1},{1,0},{2,3},{3,2},{4,5},{5,4},{6,7},{7,6},{8,9},{9,8},{10,11... | collective-permute-start | bytes 3145736 | tf_op jit(solution)/shard_map/ppermute | solution.py:638
  (1 other events, 0.7 us)

commit v4 on v2

--- a/solution.py
+++ b/solution.py
@@ -584,11 +584,18 @@
     return gather(gather(values, "lat", far), "lat", [list(group) for group in zip(*far)])
 
 
+def gather_cores(copies):
+    groups = [list(range(core, NR, 2)) for core in range(2)]
+    return lax.all_to_all(copies, "rad", split_axis=0, concat_axis=0, axis_index_groups=groups, tiled=True)
+
+
+def swap_cores(own):
+    return lax.ppermute(own, "rad", [(layer, layer ^ 1) for layer in range(NR)])
+
+
 def gather_radial(copies):
-    groups = [list(range(core, NR, 2)) for core in range(2)]
-    own = lax.all_to_all(copies, "rad", split_axis=0, concat_axis=0, axis_index_groups=groups, tiled=True)
-    other = lax.ppermute(own, "rad", [(layer, layer ^ 1) for layer in range(NR)])
-    return own, other
+    own = gather_cores(copies)
+    return own, swap_cores(own)
 
 
 def radial(values):
@@ -601,16 +608,19 @@
     tables = gluing_tables(glue_tile, glue_side, glue_flip)
     place = jnp.stack([lax.axis_index("rad"), place_of(lax.axis_index("lat"))]).astype(jnp.int32)
     own = jnp.concatenate([field.reshape(8, LANES) for field in (viscosity, initial_guess, rhs_force)], axis=0)
+    own, place = lax.optimization_barrier((own, place))
     arrived = gather_lateral(own)
     pair = spread_layer(arrived)
     pair_beside = radial(pair)
     viscous, velocity, force, conds, lateral_image, lateral_total, faces = lateral_stage(arrived, pair, *tables)
     faces, *pair_beside = lax.optimization_barrier((faces, *pair_beside))
+    faces_gathered, *pair_beside = lax.optimization_barrier((gather_cores(faces), *pair_beside))
+    faces_swapped = swap_cores(faces_gathered)
     radials, total, residual, smoothed, packed = first_stage(
         force, viscous, velocity, lateral_image, lateral_total, *pair_beside
     )
-    smoothed_beside = radial(packed)
-    coefficients = faces_stage(place, *gather_radial(faces))
+    coefficients = faces_stage(place, faces_gathered, faces_swapped)
+    *smoothed_beside, coefficients = lax.optimization_barrier((*radial(packed), coefficients))
     coarse = remain_stage(conds, radials, total, velocity, residual, smoothed, *smoothed_beside, *tables)
     velocity, residual, smoothed, packed = step_stage(
         place, *gather_radial(coarse), *coefficients, *tables, velocity, *pair_beside, smoothed,

time: 230 us -> 232 us (level)
  blocking collectives: 76.4 us -> 128 us
  local copies, waits for them, and re-layouts: 20.7 us -> 2.32 us
  starting transfers between devices: 49.8 us -> 31.9 us
  waiting for transfers between devices: 49.7 us -> 38.6 us
    all_to_all x1 -> x3, blocking collectives: 15.2 us -> 66.4 us  [gather_cores(): lax.all_to_all(copies, 'rad', split_axis=0, concat_axis=0, axis_index_gro...]
    unnamed x59 -> x7, local copies, waits for them, and re-layouts: 18.5 us -> 0.11 us
    all_to_all x2 -> x0, waiting for transfers between devices: 12.4 us -> none  [gather_radial(): lax.all_to_all(copies, 'rad', split_axis=0, concat_axis=0, axis_index_gro...]
    all_to_all x2 -> x0, starting transfers between devices: 9.84 us -> none  [gather_radial(): lax.all_to_all(copies, 'rad', split_axis=0, concat_axis=0, axis_index_gro...]
    ppermute x3, starting transfers between devices: 11.8 us -> 7.23 us  [swap_cores(): return lax.ppermute(own, 'rad', [(layer, layer ^ 1) for layer in range(NR)])]
    ppermute x3, waiting for transfers between devices: 2.27 us -> 5.25 us  [swap_cores(): return lax.ppermute(own, 'rad', [(layer, layer ^ 1) for layer in range(NR)])]
    ppermute x3, starting transfers between devices: 8.79 us -> 5.83 us  [radial(): lax.ppermute(values, 'rad', backward)]
    ppermute x3, waiting for transfers between devices: 6.46 us -> 4.05 us  [radial(): lax.ppermute(values, 'rad', forward)]
  transfers between devices with their start and end apart: 12 -> 10, of which waited for: 8 -> 8; matrix products, arithmetic and copies ran while one was open for 1% -> 1% of each run, Pallas kernels for 4% -> 2%
where the time goes in v4:
time: 232 us
  blocking collectives  128 us (55%)
  waiting for transfers between devices  38.6 us (17%)
  starting transfers between devices  31.9 us (14%)
  Pallas kernels  30.3 us (13%)
  local copies, waits for them, and re-layouts  2.32 us (1%)
    all_to_all x3, blocking collectives, gather_cores(): lax.all_to_all(copies, 'rad', split_axis=0, concat_axis=0, axis_index_gro...  66.4 us
    all_to_all x1, blocking collectives, gather(): lax.all_to_all(sent, axis, split_axis=0, concat_axis=0, axis_index_groups...  61.2 us
    pallas_call x8, Pallas kernels, call(): pl.pallas_call(kernel, out_shape=shapes, in_specs=[pl.BlockSpec(memory_sp...  30.3 us
    all_to_all x1, waiting for transfers between devices, gather(): lax.all_to_all(sent, axis, split_axis=0, concat_axis=0, axis_index_groups...  18.2 us
    ppermute x3, waiting for transfers between devices, radial(): lax.ppermute(values, 'rad', backward)  11.1 us
    all_to_all x1, starting transfers between devices, gather(): lax.all_to_all(sent, axis, split_axis=0, concat_axis=0, axis_index_groups...  9.99 us
    ppermute x3, starting transfers between devices, radial(): lax.ppermute(values, 'rad', forward)  8.86 us
    ppermute x3, starting transfers between devices, swap_cores(): return lax.ppermute(own, 'rad', [(layer, layer ^ 1) for layer in range(NR)])  7.23 us
  transfers between devices with their start and end apart: 10, of which 8 were waited for; matrix products, arithmetic and copies ran while one was open for 1% of the time, Pallas kernels for 2%

profile of v4, /device:TPU:1, one launch (start us, length us, event | category | flops | bytes accessed | tf_op | source)
XLA Modules:
  0.0 231.8 jit_solution(16618709737495605276)
XLA Ops:
  0.1 0.7 pad_maximum_fusion
  0.8 61.2 %all_to_all.25 = f32[16,24,128]{2,1,0:T(8,128)S(1)} all-to-all(f32[16,24,128]{2,1,0:T(8,128)S(1)} %broadcast_in_dim.6), channel_id=1, replica_groups={{0,16,128,144,256,272,384,400,512,528,640,656,768,784,896,912},{32,48,1..., dimensions={0} | all-to-all | bytes 393216 | tf_op jit(solution)/shard_map/all_to_all | solution.py:577
  62.0 0.9 broadcast_in_dim.16
  62.9 10.0 %all-to-all-start.1 = ((f32[4,384,128]{2,1,0:T(8,128)}), f32[4,384,128]{2,1,0:T(8,128)S(1)}, u32[]{:S(2)}, u32[]{:S(2)}) async-start(f32[4,384,128]{2,1,0:T(8,128)} %broadcast_in_dim.16), calls=%async_computation.1 | async-start | bytes 1572864 | tf_op jit(solution)/shard_map/all_to_all | solution.py:577
  73.2 0.3 copy.9
  74.3 18.2 %all-to-all-done.1 = f32[4,384,128]{2,1,0:T(8,128)S(1)} async-done(((f32[4,384,128]{2,1,0:T(8,128)}), f32[4,384,128]{2,1,0:T(8,128)S(1)}, u32[]{:S(2)}, u32[]{:S(2)}) %all-to-all-start.1) | async-done | bytes 786464 | tf_op jit(solution)/shard_map/all_to_all | solution.py:577
  92.7 3.6 %collective-permute-start.1 = (f32[1024,128]{1,0:T(8,128)S(1)}, f32[1024,128]{1,0:T(8,128)S(1)}, u32[]{:S(2)}, u32[]{:S(2)}) collective-permute-start(f32[1024,128]{1,0:T(8,128)S(1)} %shard_map.64.pair_ref), channel_id=1, source_target_pairs={{0,1},{1,2},{2,3},{3,4},{4,5},{5,6},{6,7},{7,8},{8,9},{9,10},{10,1... | collective-permute-start | bytes 1572872 | tf_op jit(solution)/shard_map/ppermute | solution.py:604
  96.4 1.9 collective-permute-start
  98.5 1.4 shard_map.65
  99.8 2.7 %collective-permute-done.1.below_ref = f32[1024,128]{1,0:T(8,128)S(1)} collective-permute-done((f32[1024,128]{1,0:T(8,128)S(1)}, f32[1024,128]{1,0:T(8,128)S(1)}, u32[]{:S(2)}, u32[]{:S(2)}) %collective-permute-start.1) | collective-permute-done | bytes 524320 | tf_op jit(solution)/shard_map/ppermute | solution.py:604
  102.5 4.4 %collective-permute-done.above_ref = f32[1024,128]{1,0:T(8,128)S(1)} collective-permute-done((f32[1024,128]{1,0:T(8,128)S(1)}, f32[1024,128]{1,0:T(8,128)S(1)}, u32[]{:S(2)}, u32[]{:S(2)}) %collective-permute-start) | collective-permute-done | bytes 524320 | tf_op jit(solution)/shard_map/ppermute | solution.py:604
  106.9 28.9 %all_to_all.26.own_ref = f32[8,400,128]{2,1,0:T(8,128)S(1)} all-to-all(f32[8,400,128]{2,1,0:T(8,128)S(1)} %get-tuple-element.50), channel_id=1, replica_groups={{0,2,4,6,8,10,12,14},{1,3,5,7,9,11,13,15},{16,18,20,22,24,26,28,30},{17..., dimensions={0} | all-to-all | bytes 3276800 | tf_op jit(solution)/shard_map/all_to_all | solution.py:589
  135.8 3.4 %collective-permute-start.4 = (f32[8,400,128]{2,1,0:T(8,128)S(1)}, f32[8,400,128]{2,1,0:T(8,128)S(1)}, u32[]{:S(2)}, u32[]{:S(2)}) collective-permute-start(f32[8,400,128]{2,1,0:T(8,128)S(1)} %all_to_all.26.own_ref), channel_id=1, source_target_pairs={{0,1},{1,0},{2,3},{3,2},{4,5},{5,4},{6,7},{7,6},{8,9},{9,8},{10,11... | collective-permute-start | bytes 4915208 | tf_op jit(solution)/shard_map/ppermute | solution.py:593
  139.2 1.1 shard_map.66
  140.3 2.4 %collective-permute-start.3 = (f32[512,128]{1,0:T(8,128)S(1)}, f32[512,128]{1,0:T(8,128)S(1)}, u32[]{:S(2)}, u32[]{:S(2)}) collective-permute-start(f32[512,128]{1,0:T(8,128)S(1)} %get-tuple-element.59), channel_id=1, source_target_pairs={{0,1},{1,2},{2,3},{3,4},{4,5},{5,6},{6,7},{7,8},{8,9},{9,10},{10,1... | collective-permute-start | bytes 786440 | tf_op jit(solution)/shard_map/ppermute | solution.py:604
  142.7 2.0 collective-permute-start.2
  144.7 3.4 %shard_map.67 = (f32[2176,128]{1,0:T(8,128)S(1)}, f32[16,136,128]{2,1,0:T(8,128)S(1)}, f32[2048,128]{1,0:T(8,128)S(1)}, f32[2048,128]{1,0:T(8,128)S(1)}, f32[2048,128]{1,0:T(8,128)S(1)}) custom-call(s32[2]{0:T(128)S(1)} %pad_add_fusion.place_ref, f32[8,400,128]{2,1,0:T(8,128)S(1)} %all_to_all.26.own_ref, f32[8,400,128]{2,1,0:T(8,128)S(1)} %collective-permute-done.4.other_ref), custom_call_target="tpu_custom_call" | custom-call | flops 25165824 | bytes 25165824 | tf_op jit(solution)/shard_map/pallas_call | solution.py:504
  148.1 2.3 collective-permute-done.2.above_ref.smoothed_above_ref
  150.4 1.4 shard_map.68
  151.8 18.8 %all_to_all.27.own_ref = f32[8,256,128]{2,1,0:T(8,128)S(1)} all-to-all(f32[8,256,128]{2,1,0:T(8,128)S(1)} %shard_map.68), channel_id=1, replica_groups={{0,2,4,6,8,10,12,14},{1,3,5,7,9,11,13,15},{16,18,20,22,24,26,28,30},{17..., dimensions={0} | all-to-all | bytes 2097152 | tf_op jit(solution)/shard_map/all_to_all | solution.py:589
  170.6 1.9 collective-permute-start.5
  172.6 2.6 %collective-permute-done.5.other_ref = f32[8,256,128]{2,1,0:T(8,128)S(1)} collective-permute-done((f32[8,256,128]{2,1,0:T(8,128)S(1)}, f32[8,256,128]{2,1,0:T(8,128)S(1)}, u32[]{:S(2)}, u32[]{:S(2)}) %collective-permute-start.5) | collective-permute-done | bytes 1048608 | tf_op jit(solution)/shard_map/ppermute | solution.py:593
  175.2 11.1 %shard_map.69 = (f32[1024,128]{1,0:T(8,128)S(1)}, f32[1024,128]{1,0:T(8,128)S(1)}, f32[1024,128]{1,0:T(8,128)S(1)}, f32[512,128]{1,0:T(8,128)S(1)}) custom-call(s32[2]{0:T(128)S(1)} %pad_add_fusion.place_ref, f32[8,256,128]{2,1,0:T(8,128)S(1)} %all_to_all.27.own_ref, f32[8,256,128]{2,1,0:T(8,128)S(1)} %collective-permute-done.5.other_ref, ...), custom_call_target="tpu_custom_call" | custom-call | flops 4194304 | bytes 4194304 | tf_op jit(solution)/shard_map/pallas_call | solution.py:504
  186.3 2.9 %collective-permute-start.7 = (f32[512,128]{1,0:T(8,128)S(1)}, f32[512,128]{1,0:T(8,128)S(1)}, u32[]{:S(2)}, u32[]{:S(2)}) collective-permute-start(f32[512,128]{1,0:T(8,128)S(1)} %get-tuple-element.76), channel_id=1, source_target_pairs={{0,1},{1,2},{2,3},{3,4},{4,5},{5,6},{6,7},{7,8},{8,9},{9,10},{10,1... | collective-permute-start | bytes 786440 | tf_op jit(solution)/shard_map/ppermute | solution.py:604
  189.2 1.9 collective-permute-start.6
  191.1 1.4 collective-permute-done.7.below_ref
  192.5 4.4 %collective-permute-done.6.above_ref = f32[512,128]{1,0:T(8,128)S(1)} collective-permute-done((f32[512,128]{1,0:T(8,128)S(1)}, f32[512,128]{1,0:T(8,128)S(1)}, u32[]{:S(2)}, u32[]{:S(2)}) %collective-permute-start.6) | collective-permute-done | bytes 262176 | tf_op jit(solution)/shard_map/ppermute | solution.py:604
  196.9 1.4 shard_map.70
  198.3 18.7 %all_to_all.28.own_ref = f32[8,256,128]{2,1,0:T(8,128)S(1)} all-to-all(f32[8,256,128]{2,1,0:T(8,128)S(1)} %shard_map.70), channel_id=1, replica_groups={{0,2,4,6,8,10,12,14},{1,3,5,7,9,11,13,15},{16,18,20,22,24,26,28,30},{17..., dimensions={0} | all-to-all | bytes 2097152 | tf_op jit(solution)/shard_map/all_to_all | solution.py:589
  217.0 1.9 collective-permute-start.8
  218.9 2.6 %collective-permute-done.8.other_ref = f32[8,256,128]{2,1,0:T(8,128)S(1)} collective-permute-done((f32[8,256,128]{2,1,0:T(8,128)S(1)}, f32[8,256,128]{2,1,0:T(8,128)S(1)}, u32[]{:S(2)}, u32[]{:S(2)}) %collective-permute-start.8) | collective-permute-done | bytes 1048608 | tf_op jit(solution)/shard_map/ppermute | solution.py:593
  221.5 10.3 %shard_map.71 = f32[8,128]{1,0:T(8,128)} custom-call(s32[2]{0:T(128)S(1)} %pad_add_fusion.place_ref, f32[8,256,128]{2,1,0:T(8,128)S(1)} %all_to_all.28.own_ref, f32[8,256,128]{2,1,0:T(8,128)S(1)} %collective-permute-done.8.other_ref, f32[2176,128]{1,0:T(8,128)S(1)} %get-tuple-element.68.rows_ref, f32[16,136,128]{2,1,0:T(8,128)S(1)} %get-tuple-element.69.columns_ref, ...), custom_call_target="tpu_custom_call" | custom-call | flops 4194304 | bytes 4194304 | tf_op jit(solution)/shard_map/pallas_call | solution.py:504
  (24 shorter events, 1.4 us)
Async XLA Ops:
  0.0 72.9 %copy-start.1 = (s32[64,4]{0,1:T(4,128)S(1)}, s32[64,4]{0,1:T(4,128)}, u32[]{:S(2)}) copy-start(s32[64,4]{0,1:T(4,128)} %param.11) | copy-start | bytes 3076
  0.8 72.3 %copy-start.2 = (s32[64,4]{0,1:T(4,128)S(1)}, s32[64,4]{0,1:T(4,128)}, u32[]{:S(2)}) copy-start(s32[64,4]{0,1:T(4,128)} %param.10) | copy-start | bytes 3076
  0.8 72.9 %copy-start = (s32[64,4]{0,1:T(4,128)S(1)}, s32[64,4]{0,1:T(4,128)}, u32[]{:S(2)}) copy-start(s32[64,4]{0,1:T(4,128)} %param.9) | copy-start | bytes 3076
  62.9 29.6 %all-to-all-start.1 = ((f32[4,384,128]{2,1,0:T(8,128)}), f32[4,384,128]{2,1,0:T(8,128)S(1)}, u32[]{:S(2)}, u32[]{:S(2)}) async-start(f32[4,384,128]{2,1,0:T(8,128)} %broadcast_in_dim.16), calls=%async_computation.1 | async-start | bytes 1572864 | tf_op jit(solution)/shard_map/all_to_all | solution.py:577
  92.7 9.8 %collective-permute-start.1 = (f32[1024,128]{1,0:T(8,128)S(1)}, f32[1024,128]{1,0:T(8,128)S(1)}, u32[]{:S(2)}, u32[]{:S(2)}) collective-permute-start(f32[1024,128]{1,0:T(8,128)S(1)} %shard_map.64.pair_ref), channel_id=1, source_target_pairs={{0,1},{1,2},{2,3},{3,4},{4,5},{5,6},{6,7},{7,8},{8,9},{9,10},{10,1... | collective-permute-start | bytes 1572872 | tf_op jit(solution)/shard_map/ppermute | solution.py:604
  96.4 10.5 %collective-permute-start = (f32[1024,128]{1,0:T(8,128)S(1)}, f32[1024,128]{1,0:T(8,128)S(1)}, u32[]{:S(2)}, u32[]{:S(2)}) collective-permute-start(f32[1024,128]{1,0:T(8,128)S(1)} %shard_map.64.pair_ref), channel_id=1, source_target_pairs={{1,0},{2,1},{3,2},{4,3},{5,4},{6,5},{7,6},{8,7},{9,8},{10,9},{11,1... | collective-permute-start | bytes 1572872 | tf_op jit(solution)/shard_map/ppermute | solution.py:604
  135.8 8.8 %collective-permute-start.4 = (f32[8,400,128]{2,1,0:T(8,128)S(1)}, f32[8,400,128]{2,1,0:T(8,128)S(1)}, u32[]{:S(2)}, u32[]{:S(2)}) collective-permute-start(f32[8,400,128]{2,1,0:T(8,128)S(1)} %all_to_all.26.own_ref), channel_id=1, source_target_pairs={{0,1},{1,0},{2,3},{3,2},{4,5},{5,4},{6,7},{7,6},{8,9},{9,8},{10,11... | collective-permute-start | bytes 4915208 | tf_op jit(solution)/shard_map/ppermute | solution.py:593
  140.3 7.7 %collective-permute-start.3 = (f32[512,128]{1,0:T(8,128)S(1)}, f32[512,128]{1,0:T(8,128)S(1)}, u32[]{:S(2)}, u32[]{:S(2)}) collective-permute-start(f32[512,128]{1,0:T(8,128)S(1)} %get-tuple-element.59), channel_id=1, source_target_pairs={{0,1},{1,2},{2,3},{3,4},{4,5},{5,6},{6,7},{7,8},{8,9},{9,10},{10,1... | collective-permute-start | bytes 786440 | tf_op jit(solution)/shard_map/ppermute | solution.py:604
  142.7 7.7 %collective-permute-start.2 = (f32[512,128]{1,0:T(8,128)S(1)}, f32[512,128]{1,0:T(8,128)S(1)}, u32[]{:S(2)}, u32[]{:S(2)}) collective-permute-start(f32[512,128]{1,0:T(8,128)S(1)} %get-tuple-element.59), channel_id=1, source_target_pairs={{1,0},{2,1},{3,2},{4,3},{5,4},{6,5},{7,6},{8,7},{9,8},{10,9},{11,1... | collective-permute-start | bytes 786440 | tf_op jit(solution)/shard_map/ppermute | solution.py:604
  170.6 4.5 %collective-permute-start.5 = (f32[8,256,128]{2,1,0:T(8,128)S(1)}, f32[8,256,128]{2,1,0:T(8,128)S(1)}, u32[]{:S(2)}, u32[]{:S(2)}) collective-permute-start(f32[8,256,128]{2,1,0:T(8,128)S(1)} %all_to_all.27.own_ref), channel_id=1, source_target_pairs={{0,1},{1,0},{2,3},{3,2},{4,5},{5,4},{6,7},{7,6},{8,9},{9,8},{10,11... | collective-permute-start | bytes 3145736 | tf_op jit(solution)/shard_map/ppermute | solution.py:593
  186.3 6.2 %collective-permute-start.7 = (f32[512,128]{1,0:T(8,128)S(1)}, f32[512,128]{1,0:T(8,128)S(1)}, u32[]{:S(2)}, u32[]{:S(2)}) collective-permute-start(f32[512,128]{1,0:T(8,128)S(1)} %get-tuple-element.76), channel_id=1, source_target_pairs={{0,1},{1,2},{2,3},{3,4},{4,5},{5,6},{6,7},{7,8},{8,9},{9,10},{10,1... | collective-permute-start | bytes 786440 | tf_op jit(solution)/shard_map/ppermute | solution.py:604
  189.2 7.7 %collective-permute-start.6 = (f32[512,128]{1,0:T(8,128)S(1)}, f32[512,128]{1,0:T(8,128)S(1)}, u32[]{:S(2)}, u32[]{:S(2)}) collective-permute-start(f32[512,128]{1,0:T(8,128)S(1)} %get-tuple-element.76), channel_id=1, source_target_pairs={{1,0},{2,1},{3,2},{4,3},{5,4},{6,5},{7,6},{8,7},{9,8},{10,9},{11,1... | collective-permute-start | bytes 786440 | tf_op jit(solution)/shard_map/ppermute | solution.py:604
  217.0 4.5 %collective-permute-start.8 = (f32[8,256,128]{2,1,0:T(8,128)S(1)}, f32[8,256,128]{2,1,0:T(8,128)S(1)}, u32[]{:S(2)}, u32[]{:S(2)}) collective-permute-start(f32[8,256,128]{2,1,0:T(8,128)S(1)} %all_to_all.28.own_ref), channel_id=1, source_target_pairs={{0,1},{1,0},{2,3},{3,2},{4,5},{5,4},{6,7},{7,6},{8,9},{9,8},{10,11... | collective-permute-start | bytes 3145736 | tf_op jit(solution)/shard_map/ppermute | solution.py:593

commit v5 on v4

--- a/solution.py
+++ b/solution.py
@@ -168,19 +168,17 @@
             return every(ref, upper + start, HALF) + every(ref, lower + start, HALF)
 
         faces = pack(both(conds_ref.at[1], lower), column(3, 1))
-        for copy in range(CHIPS):
-            faces_ref[copy, cells] = faces
+        faces_ref[cells] = faces
         if big == 0:
             north = both(conds_ref.at[0], upper)
         wests.append(column(2, 0)[0:1])
         sums.append(both(viscous_ref, upper) + both(viscous_ref, lower))
     start = COARSE + COARSE // 2
     edge = pack(north, jnp.concatenate(wests, axis=0))
-    for copy in range(CHIPS):
-        for big in range(HALF // 2):
-            first = COARSE + big * HALF
-            faces_ref[copy, first : first + HALF] = pack(sums[big], sums[big + HALF // 2])
-        faces_ref[copy, start : start + HALF] = edge
+    for big in range(HALF // 2):
+        first = COARSE + big * HALF
+        faces_ref[first : first + HALF] = pack(sums[big], sums[big + HALF // 2])
+    faces_ref[start : start + HALF] = edge
     for group in range(8):
         force_ref[group * LANES : (group + 1) * LANES] = turned_layer(arrived_ref, 2, 2, group)
 
@@ -207,8 +205,12 @@
 
 def remain_kernel(
     conds_ref, radials_ref, total_ref, velocity_ref, residual_ref, smoothed_ref, above_ref, below_ref,
-    gluing_ref, flips_ref, coarse_ref, pad, west, east, remain, damping,
+    gluing_ref, flips_ref, *rest,
 ):
+    *faces, coarse_ref, pad, west, east, remain, damping = rest
+    for faces_ref in faces:
+        for copy in range(CHIPS):
+            coarse_ref[copy, COARSE:] = faces_ref[...]
     pad[C : C + CELLS] = smoothed_ref[...]
     fine_ghosts(pad, west, east, gluing_ref[...], flips_ref[...])
     for upper in range(2):
@@ -266,12 +268,12 @@
 def faces_kernel(
     place_ref, own_ref, other_ref, rows_ref, columns_ref, up_ref, down_ref, face_total_ref, sums
 ):
-    middle, last = COARSE, COARSE + COARSE // 2
+    first, middle, last = COARSE, 2 * COARSE, 2 * COARSE + COARSE // 2
     half = COARSE // 2
 
     def arrange(even_ref, odd_ref):
         for sub in range(8):
-            a, b = even_ref[sub, :middle], odd_ref[sub, :middle]
+            a, b = even_ref[sub, first:middle], odd_ref[sub, first:middle]
             rows_ref[pl.ds(LANES + sub, COARSE, stride=8)] = pack(a, swap(b))
             east = pack(swap(a), b)
             for big in range(HALF):
@@ -356,7 +358,7 @@
 
     def arrange(even_ref, odd_ref):
         for sub in range(8):
-            a, b = even_ref[sub], odd_ref[sub]
+            a, b = even_ref[sub, :COARSE], odd_ref[sub, :COARSE]
             residual[pl.ds(sub, COARSE, stride=8)] = pack(a, swap(b))
             diagonal[pl.ds(sub, COARSE, stride=8)] = pack(swap(a), b)
 
@@ -517,7 +519,7 @@
 FINE = (CELLS, LANES)
 PACKED = (CELLS // 2, LANES)
 EDGE = (C, LANES)
-FACES = (CHIPS, COARSE + COARSE // 2 + HALF, LANES)
+FACES = (COARSE + COARSE // 2 + HALF, LANES)
 GRID = (COARSE * 8, LANES)
 COARSE_SCRATCH = [(HALF + 2, (HALF + 2) * 8, LANES)] + [GRID] * 4
 
@@ -535,8 +537,11 @@
     return call(first_kernel, [(2,) + FINE, FINE, FINE, FINE, PACKED], [], args)
 
 
-def remain_stage(*args):
-    return call(remain_kernel, [(CHIPS, COARSE, LANES)], [PADDED, EDGE, EDGE, FINE, FINE], args)[0]
+def remain_stage(*args, faces=None):
+    rows = COARSE
+    if faces is not None:
+        args, rows = args + (faces,), COARSE + FACES[0]
+    return call(remain_kernel, [(CHIPS, rows, LANES)], [PADDED, EDGE, EDGE, FINE, FINE], args)[0]
 
 
 def faces_stage(*args):
@@ -599,9 +604,14 @@
 
 
 def radial(values):
-    backward = [(layer + 1, layer) for layer in range(NR - 1)]
-    forward = [(layer, layer + 1) for layer in range(NR - 1)]
-    return lax.ppermute(values, "rad", backward), lax.ppermute(values, "rad", forward)
+    lat = lax.axis_size("lat")
+    above, below = [], []
+    for tile in range(lat):
+        for layer in range(NR - 1):
+            other = tile ^ 1 if layer % 4 == 3 else tile
+            above.append((other * NR + layer + 1, tile * NR + layer))
+            below.append((tile * NR + layer, other * NR + layer + 1))
+    return lax.ppermute(values, ("lat", "rad"), above), lax.ppermute(values, ("lat", "rad"), below)
 
 
 def on_device(rhs_force, viscosity, initial_guess, glue_tile, glue_side, glue_flip):
@@ -613,17 +623,17 @@
     pair = spread_layer(arrived)
     pair_beside = radial(pair)
     viscous, velocity, force, conds, lateral_image, lateral_total, faces = lateral_stage(arrived, pair, *tables)
-    faces, *pair_beside = lax.optimization_barrier((faces, *pair_beside))
-    faces_gathered, *pair_beside = lax.optimization_barrier((gather_cores(faces), *pair_beside))
-    faces_swapped = swap_cores(faces_gathered)
     radials, total, residual, smoothed, packed = first_stage(
         force, viscous, velocity, lateral_image, lateral_total, *pair_beside
     )
-    coefficients = faces_stage(place, faces_gathered, faces_swapped)
-    *smoothed_beside, coefficients = lax.optimization_barrier((*radial(packed), coefficients))
-    coarse = remain_stage(conds, radials, total, velocity, residual, smoothed, *smoothed_beside, *tables)
+    smoothed_beside = radial(packed)
+    coarse = remain_stage(
+        conds, radials, total, velocity, residual, smoothed, *smoothed_beside, *tables, faces=faces
+    )
+    coarse = gather_radial(coarse)
+    coefficients = faces_stage(place, *coarse)
     velocity, residual, smoothed, packed = step_stage(
-        place, *gather_radial(coarse), *coefficients, *tables, velocity, *pair_beside, smoothed,
+        place, *coarse, *coefficients, *tables, velocity, *pair_beside, smoothed,
         *smoothed_beside, force, conds, radials, total,
     )
     smoothed_beside = radial(packed)

time: 232 us -> 227 us (0.978)
  blocking collectives: 128 us -> 117 us
  waiting for transfers between devices: 38.6 us -> 43.6 us
    all_to_all x3 -> x2, blocking collectives: 66.4 us -> 55.7 us  [gather_cores(): lax.all_to_all(copies, 'rad', split_axis=0, concat_axis=0, axis_index_gro...]
    ppermute x6, waiting for transfers between devices: 15.1 us -> 18.1 us  [the longest x3 13.2 us: radial(): lax.ppermute(values, ('lat', 'rad'), above)]
    ppermute x3 -> x2, waiting for transfers between devices: 5.25 us -> 7.23 us  [swap_cores(): return lax.ppermute(own, 'rad', [(layer, layer ^ 1) for layer in range(NR)])]
    ppermute x3 -> x2, starting transfers between devices: 7.23 us -> 7.76 us  [swap_cores(): return lax.ppermute(own, 'rad', [(layer, layer ^ 1) for layer in range(NR)])]
  transfers between devices with their start and end apart: 10 -> 9, of which waited for: 8 -> 9; matrix products, arithmetic and copies ran while one was open for 1% -> 1% of each run, Pallas kernels for 2% -> 1%
where the time goes in v5:
time: 227 us; the launch traced here: 226 us
  blocking collectives  117 us (52%)
  waiting for transfers between devices  43.6 us (19%)
  starting transfers between devices  32.3 us (14%)
  Pallas kernels  30.1 us (13%)
  local copies, waits for them, and re-layouts  2.32 us (1%)
    all_to_all x1, blocking collectives, gather(): lax.all_to_all(sent, axis, split_axis=0, concat_axis=0, axis_index_groups...  61.2 us
    all_to_all x2, blocking collectives, gather_cores(): lax.all_to_all(copies, 'rad', split_axis=0, concat_axis=0, axis_index_gro...  55.7 us
    pallas_call x8, Pallas kernels, call(): pl.pallas_call(kernel, out_shape=shapes, in_specs=[pl.BlockSpec(memory_sp...  30.1 us
    all_to_all x1, waiting for transfers between devices, gather(): lax.all_to_all(sent, axis, split_axis=0, concat_axis=0, axis_index_groups...  18.2 us
    ppermute x3, waiting for transfers between devices, radial(): lax.ppermute(values, ('lat', 'rad'), above)  13.2 us
    all_to_all x1, starting transfers between devices, gather(): lax.all_to_all(sent, axis, split_axis=0, concat_axis=0, axis_index_groups...  9.99 us
    ppermute x3, starting transfers between devices, radial(): lax.ppermute(values, ('lat', 'rad'), below)  8.28 us
    ppermute x2, starting transfers between devices, swap_cores(): return lax.ppermute(own, 'rad', [(layer, layer ^ 1) for layer in range(NR)])  7.76 us
  transfers between devices with their start and end apart: 9, of which 9 were waited for; matrix products, arithmetic and copies ran while one was open for 1% of the time, Pallas kernels for 1%

profile of v5, /device:TPU:1, one launch (start us, length us, event | category | flops | bytes accessed | tf_op | source)
XLA Modules:
  0.0 226.3 jit_solution(12084948214809922614)
XLA Ops:
  0.1 0.7 pad_maximum_fusion
  0.9 61.2 %all_to_all.20 = f32[16,24,128]{2,1,0:T(8,128)S(1)} all-to-all(f32[16,24,128]{2,1,0:T(8,128)S(1)} %broadcast_in_dim.6), channel_id=1, replica_groups={{0,16,128,144,256,272,384,400,512,528,640,656,768,784,896,912},{32,48,1..., dimensions={0} | all-to-all | bytes 393216 | tf_op jit(solution)/shard_map/all_to_all | solution.py:582
  62.0 1.0 broadcast_in_dim.16
  63.0 10.0 %all-to-all-start.1 = ((f32[4,384,128]{2,1,0:T(8,128)}), f32[4,384,128]{2,1,0:T(8,128)S(1)}, u32[]{:S(2)}, u32[]{:S(2)}) async-start(f32[4,384,128]{2,1,0:T(8,128)} %broadcast_in_dim.16), calls=%async_computation.1 | async-start | bytes 1572864 | tf_op jit(solution)/shard_map/all_to_all | solution.py:582
  73.3 0.3 copy.9
  73.9 0.3 copy.11
  74.4 18.2 %all-to-all-done.1 = f32[4,384,128]{2,1,0:T(8,128)S(1)} async-done(((f32[4,384,128]{2,1,0:T(8,128)}), f32[4,384,128]{2,1,0:T(8,128)S(1)}, u32[]{:S(2)}, u32[]{:S(2)}) %all-to-all-start.1) | async-done | bytes 786464 | tf_op jit(solution)/shard_map/all_to_all | solution.py:582
  92.8 3.6 %collective-permute-start.1 = (f32[1024,128]{1,0:T(8,128)S(1)}, f32[1024,128]{1,0:T(8,128)S(1)}, u32[]{:S(2)}, u32[]{:S(2)}) collective-permute-start(f32[1024,128]{1,0:T(8,128)S(1)} %shard_map.64.pair_ref), channel_id=1, source_target_pairs={{0,1},{1,2},{2,3},{3,20},{4,5},{5,6},{6,7},{7,24},{8,9},{9,10},{10... | collective-permute-start | bytes 1572872 | tf_op jit(solution)/shard_map/ppermute | solution.py:614
  96.4 1.9 collective-permute-start
  98.5 1.3 shard_map.65
  99.8 2.7 %collective-permute-done.1.below_ref = f32[1024,128]{1,0:T(8,128)S(1)} collective-permute-done((f32[1024,128]{1,0:T(8,128)S(1)}, f32[1024,128]{1,0:T(8,128)S(1)}, u32[]{:S(2)}, u32[]{:S(2)}) %collective-permute-start.1) | collective-permute-done | bytes 524320 | tf_op jit(solution)/shard_map/ppermute | solution.py:614
  102.5 4.4 %collective-permute-done.above_ref = f32[1024,128]{1,0:T(8,128)S(1)} collective-permute-done((f32[1024,128]{1,0:T(8,128)S(1)}, f32[1024,128]{1,0:T(8,128)S(1)}, u32[]{:S(2)}, u32[]{:S(2)}) %collective-permute-start) | collective-permute-done | bytes 524320 | tf_op jit(solution)/shard_map/ppermute | solution.py:614
  106.9 1.1 shard_map.66
  108.0 1.9 collective-permute-start.3
  109.9 2.4 %collective-permute-start.2 = (f32[512,128]{1,0:T(8,128)S(1)}, f32[512,128]{1,0:T(8,128)S(1)}, u32[]{:S(2)}, u32[]{:S(2)}) collective-permute-start(f32[512,128]{1,0:T(8,128)S(1)} %get-tuple-element.40), channel_id=1, source_target_pairs={{1,0},{2,1},{3,2},{20,3},{5,4},{6,5},{7,6},{24,7},{9,8},{10,9},{11... | collective-permute-start | bytes 786440 | tf_op jit(solution)/shard_map/ppermute | solution.py:614
  112.4 0.9 collective-permute-done.3.below_ref.smoothed_below_ref
  113.2 4.4 %collective-permute-done.2.above_ref.smoothed_above_ref = f32[512,128]{1,0:T(8,128)S(1)} collective-permute-done((f32[512,128]{1,0:T(8,128)S(1)}, f32[512,128]{1,0:T(8,128)S(1)}, u32[]{:S(2)}, u32[]{:S(2)}) %collective-permute-start.2) | collective-permute-done | bytes 262176 | tf_op jit(solution)/shard_map/ppermute | solution.py:614
  117.6 1.6 shard_map.67
  119.2 35.6 %all_to_all.21.own_ref = f32[8,656,128]{2,1,0:T(8,128)S(1)} all-to-all(f32[8,656,128]{2,1,0:T(8,128)S(1)} %shard_map.67), channel_id=1, replica_groups={{0,2,4,6,8,10,12,14},{1,3,5,7,9,11,13,15},{16,18,20,22,24,26,28,30},{17..., dimensions={0} | all-to-all | bytes 5373952 | tf_op jit(solution)/shard_map/all_to_all | solution.py:594
  154.8 5.8 %collective-permute-start.4 = (f32[8,656,128]{2,1,0:T(8,128)S(1)}, f32[8,656,128]{2,1,0:T(8,128)S(1)}, u32[]{:S(2)}, u32[]{:S(2)}) collective-permute-start(f32[8,656,128]{2,1,0:T(8,128)S(1)} %all_to_all.21.own_ref), channel_id=1, source_target_pairs={{0,1},{1,0},{2,3},{3,2},{4,5},{5,4},{6,7},{7,6},{8,9},{9,8},{10,11... | collective-permute-start | bytes 8060936 | tf_op jit(solution)/shard_map/ppermute | solution.py:598
  160.7 4.6 %collective-permute-done.4.other_ref = f32[8,656,128]{2,1,0:T(8,128)S(1)} collective-permute-done((f32[8,656,128]{2,1,0:T(8,128)S(1)}, f32[8,656,128]{2,1,0:T(8,128)S(1)}, u32[]{:S(2)}, u32[]{:S(2)}) %collective-permute-start.4) | collective-permute-done | bytes 2687008 | tf_op jit(solution)/shard_map/ppermute | solution.py:598
  165.3 3.4 %shard_map.68 = (f32[2176,128]{1,0:T(8,128)S(1)}, f32[16,136,128]{2,1,0:T(8,128)S(1)}, f32[2048,128]{1,0:T(8,128)S(1)}, f32[2048,128]{1,0:T(8,128)S(1)}, f32[2048,128]{1,0:T(8,128)S(1)}) custom-call(s32[2]{0:T(128)S(1)} %pad_add_fusion.place_ref, f32[8,656,128]{2,1,0:T(8,128)S(1)} %all_to_all.21.own_ref, f32[8,656,128]{2,1,0:T(8,128)S(1)} %collective-permute-done.4.other_ref), custom_call_target="tpu_custom_call" | custom-call | flops 25165824 | bytes 25165824 | tf_op jit(solution)/shard_map/pallas_call | solution.py:506
  168.7 10.9 %shard_map.69 = (f32[1024,128]{1,0:T(8,128)S(1)}, f32[1024,128]{1,0:T(8,128)S(1)}, f32[1024,128]{1,0:T(8,128)S(1)}, f32[512,128]{1,0:T(8,128)S(1)}) custom-call(s32[2]{0:T(128)S(1)} %pad_add_fusion.place_ref, f32[8,656,128]{2,1,0:T(8,128)S(1)} %all_to_all.21.own_ref, f32[8,656,128]{2,1,0:T(8,128)S(1)} %collective-permute-done.4.other_ref, ...), custom_call_target="tpu_custom_call" | custom-call | flops 4194304 | bytes 4194304 | tf_op jit(solution)/shard_map/pallas_call | solution.py:506
  179.6 2.7 %collective-permute-start.6 = (f32[512,128]{1,0:T(8,128)S(1)}, f32[512,128]{1,0:T(8,128)S(1)}, u32[]{:S(2)}, u32[]{:S(2)}) collective-permute-start(f32[512,128]{1,0:T(8,128)S(1)} %get-tuple-element.50), channel_id=1, source_target_pairs={{0,1},{1,2},{2,3},{3,20},{4,5},{5,6},{6,7},{7,24},{8,9},{9,10},{10... | collective-permute-start | bytes 786440 | tf_op jit(solution)/shard_map/ppermute | solution.py:614
  182.3 1.9 collective-permute-start.5
  184.3 1.4 collective-permute-done.6.below_ref
  185.6 4.4 %collective-permute-done.5.above_ref = f32[512,128]{1,0:T(8,128)S(1)} collective-permute-done((f32[512,128]{1,0:T(8,128)S(1)}, f32[512,128]{1,0:T(8,128)S(1)}, u32[]{:S(2)}, u32[]{:S(2)}) %collective-permute-start.5) | collective-permute-done | bytes 262176 | tf_op jit(solution)/shard_map/ppermute | solution.py:614
  190.0 1.5 shard_map.70
  191.5 20.1 %all_to_all.22.own_ref = f32[8,256,128]{2,1,0:T(8,128)S(1)} all-to-all(f32[8,256,128]{2,1,0:T(8,128)S(1)} %shard_map.70), channel_id=1, replica_groups={{0,2,4,6,8,10,12,14},{1,3,5,7,9,11,13,15},{16,18,20,22,24,26,28,30},{17..., dimensions={0} | all-to-all | bytes 2097152 | tf_op jit(solution)/shard_map/all_to_all | solution.py:594
  211.6 1.9 collective-permute-start.7
  213.5 2.6 %collective-permute-done.7.other_ref = f32[8,256,128]{2,1,0:T(8,128)S(1)} collective-permute-done((f32[8,256,128]{2,1,0:T(8,128)S(1)}, f32[8,256,128]{2,1,0:T(8,128)S(1)}, u32[]{:S(2)}, u32[]{:S(2)}) %collective-permute-start.7) | collective-permute-done | bytes 1048608 | tf_op jit(solution)/shard_map/ppermute | solution.py:598
  216.1 10.2 %shard_map.71 = f32[8,128]{1,0:T(8,128)} custom-call(s32[2]{0:T(128)S(1)} %pad_add_fusion.place_ref, f32[8,256,128]{2,1,0:T(8,128)S(1)} %all_to_all.22.own_ref, f32[8,256,128]{2,1,0:T(8,128)S(1)} %collective-permute-done.7.other_ref, f32[2176,128]{1,0:T(8,128)S(1)} %get-tuple-element.42.rows_ref, f32[16,136,128]{2,1,0:T(8,128)S(1)} %get-tuple-element.43.columns_ref, ...), custom_call_target="tpu_custom_call" | custom-call | flops 4194304 | bytes 4194304 | tf_op jit(solution)/shard_map/pallas_call | solution.py:506
  (21 shorter events, 1.1 us)
Async XLA Ops:
  0.0 73.0 %copy-start.1 = (s32[64,4]{0,1:T(4,128)S(1)}, s32[64,4]{0,1:T(4,128)}, u32[]{:S(2)}) copy-start(s32[64,4]{0,1:T(4,128)} %param.11) | copy-start | bytes 3076
  0.0 73.2 %copy-start.2 = (s32[64,4]{0,1:T(4,128)S(1)}, s32[64,4]{0,1:T(4,128)}, u32[]{:S(2)}) copy-start(s32[64,4]{0,1:T(4,128)} %param.10) | copy-start | bytes 3076
  0.0 73.8 %copy-start = (s32[64,4]{0,1:T(4,128)S(1)}, s32[64,4]{0,1:T(4,128)}, u32[]{:S(2)}) copy-start(s32[64,4]{0,1:T(4,128)} %param.9) | copy-start | bytes 3076
  63.0 29.6 %all-to-all-start.1 = ((f32[4,384,128]{2,1,0:T(8,128)}), f32[4,384,128]{2,1,0:T(8,128)S(1)}, u32[]{:S(2)}, u32[]{:S(2)}) async-start(f32[4,384,128]{2,1,0:T(8,128)} %broadcast_in_dim.16), calls=%async_computation.1 | async-start | bytes 1572864 | tf_op jit(solution)/shard_map/all_to_all | solution.py:582
  92.8 9.8 %collective-permute-start.1 = (f32[1024,128]{1,0:T(8,128)S(1)}, f32[1024,128]{1,0:T(8,128)S(1)}, u32[]{:S(2)}, u32[]{:S(2)}) collective-permute-start(f32[1024,128]{1,0:T(8,128)S(1)} %shard_map.64.pair_ref), channel_id=1, source_target_pairs={{0,1},{1,2},{2,3},{3,20},{4,5},{5,6},{6,7},{7,24},{8,9},{9,10},{10... | collective-permute-start | bytes 1572872 | tf_op jit(solution)/shard_map/ppermute | solution.py:614
  96.4 10.5 %collective-permute-start = (f32[1024,128]{1,0:T(8,128)S(1)}, f32[1024,128]{1,0:T(8,128)S(1)}, u32[]{:S(2)}, u32[]{:S(2)}) collective-permute-start(f32[1024,128]{1,0:T(8,128)S(1)} %shard_map.64.pair_ref), channel_id=1, source_target_pairs={{1,0},{2,1},{3,2},{20,3},{5,4},{6,5},{7,6},{24,7},{9,8},{10,9},{11... | collective-permute-start | bytes 1572872 | tf_op jit(solution)/shard_map/ppermute | solution.py:614
  108.0 5.2 %collective-permute-start.3 = (f32[512,128]{1,0:T(8,128)S(1)}, f32[512,128]{1,0:T(8,128)S(1)}, u32[]{:S(2)}, u32[]{:S(2)}) collective-permute-start(f32[512,128]{1,0:T(8,128)S(1)} %get-tuple-element.40), channel_id=1, source_target_pairs={{0,1},{1,2},{2,3},{3,20},{4,5},{5,6},{6,7},{7,24},{8,9},{9,10},{10... | collective-permute-start | bytes 786440 | tf_op jit(solution)/shard_map/ppermute | solution.py:614
  109.9 7.7 %collective-permute-start.2 = (f32[512,128]{1,0:T(8,128)S(1)}, f32[512,128]{1,0:T(8,128)S(1)}, u32[]{:S(2)}, u32[]{:S(2)}) collective-permute-start(f32[512,128]{1,0:T(8,128)S(1)} %get-tuple-element.40), channel_id=1, source_target_pairs={{1,0},{2,1},{3,2},{20,3},{5,4},{6,5},{7,6},{24,7},{9,8},{10,9},{11... | collective-permute-start | bytes 786440 | tf_op jit(solution)/shard_map/ppermute | solution.py:614
  154.8 10.5 %collective-permute-start.4 = (f32[8,656,128]{2,1,0:T(8,128)S(1)}, f32[8,656,128]{2,1,0:T(8,128)S(1)}, u32[]{:S(2)}, u32[]{:S(2)}) collective-permute-start(f32[8,656,128]{2,1,0:T(8,128)S(1)} %all_to_all.21.own_ref), channel_id=1, source_target_pairs={{0,1},{1,0},{2,3},{3,2},{4,5},{5,4},{6,7},{7,6},{8,9},{9,8},{10,11... | collective-permute-start | bytes 8060936 | tf_op jit(solution)/shard_map/ppermute | solution.py:598
  179.6 6.0 %collective-permute-start.6 = (f32[512,128]{1,0:T(8,128)S(1)}, f32[512,128]{1,0:T(8,128)S(1)}, u32[]{:S(2)}, u32[]{:S(2)}) collective-permute-start(f32[512,128]{1,0:T(8,128)S(1)} %get-tuple-element.50), channel_id=1, source_target_pairs={{0,1},{1,2},{2,3},{3,20},{4,5},{5,6},{6,7},{7,24},{8,9},{9,10},{10... | collective-permute-start | bytes 786440 | tf_op jit(solution)/shard_map/ppermute | solution.py:614
  182.3 7.7 %collective-permute-start.5 = (f32[512,128]{1,0:T(8,128)S(1)}, f32[512,128]{1,0:T(8,128)S(1)}, u32[]{:S(2)}, u32[]{:S(2)}) collective-permute-start(f32[512,128]{1,0:T(8,128)S(1)} %get-tuple-element.50), channel_id=1, source_target_pairs={{1,0},{2,1},{3,2},{20,3},{5,4},{6,5},{7,6},{24,7},{9,8},{10,9},{11... | collective-permute-start | bytes 786440 | tf_op jit(solution)/shard_map/ppermute | solution.py:614
  211.6 4.5 %collective-permute-start.7 = (f32[8,256,128]{2,1,0:T(8,128)S(1)}, f32[8,256,128]{2,1,0:T(8,128)S(1)}, u32[]{:S(2)}, u32[]{:S(2)}) collective-permute-start(f32[8,256,128]{2,1,0:T(8,128)S(1)} %all_to_all.22.own_ref), channel_id=1, source_target_pairs={{0,1},{1,0},{2,3},{3,2},{4,5},{5,4},{6,7},{7,6},{8,9},{9,8},{10,11... | collective-permute-start | bytes 3145736 | tf_op jit(solution)/shard_map/ppermute | solution.py:598

commit v6 on v5

--- a/solution.py
+++ b/solution.py
@@ -255,6 +255,10 @@
     @pl.when(place_ref[0] % 2 == 1)
     def _():
         body(other_ref, own_ref)
+
+
+def aligned(start, count):
+    return pl.ds(pl.multiple_of(start, count), count)
 
 
 def radial_pair(values):
@@ -385,50 +389,61 @@
 
     norm = total_over(start)
 
-    def apply_row(big, total):
+    def apply_rows(block, total):
+        first = block * 4
         for part in range(side // chunk):
-            first = part * chunk
-            here = pl.ds(pl.multiple_of(big * side + first, chunk), chunk)
-            own = pad[big + 1, 8 + first : 8 + first + chunk]
-            above, below = radial_pair(own)
-            south = pl.ds(pl.multiple_of((big + 1) * side + first, chunk), chunk)
-            value = (
-                rows_ref[here] * pad[big, 8 + first : 8 + first + chunk]
-                + rows_ref[south] * pad[big + 2, 8 + first : 8 + first + chunk]
-                + columns_ref[big, first : first + chunk] * pad[big + 1, first : first + chunk]
-                + columns_ref[big, 8 + first : 8 + first + chunk] * pad[big + 1, 16 + first : 16 + first + chunk]
-                + up_ref[here] * above
-                + down_ref[here] * below
-            )
-            value = diagonal[here] * own - value
-            image[here] = value
-            total = total + folded(own * value)
+            start = part * chunk
+            inside = slice(8 + start, 8 + start + chunk)
+            before, own = pad[first, inside], pad[first + 1, inside]
+            north = rows_ref[aligned(first * side + start, chunk)]
+            for big in range(4):
+                here = aligned((first + big) * side + start, chunk)
+                after = pad[first + big + 2, inside]
+                south = rows_ref[aligned((first + big + 1) * side + start, chunk)]
+                columns = columns_ref[first + big, start : start + chunk + 8]
+                west_end = pad[first + big + 1, start : start + 8]
+                east_end = pad[first + big + 1, start + chunk + 8 : start + chunk + 16]
+                row = jnp.concatenate([west_end, own, east_end], axis=0)
+                above, below = radial_pair(own)
+                value = (
+                    north * before
+                    + south * after
+                    + columns[:chunk] * row[:chunk]
+                    + columns[8:] * row[16:]
+                    + up_ref[here] * above
+                    + down_ref[here] * below
+                )
+                value = diagonal[here] * own - value
+                image[here] = value
+                total = total + folded(own * value)
+                before, own, north = own, after, south
         return total
 
     for step in range(CG_ITERS):
         coarse_ghosts(pad, gluing, flips)
-        length = norm / total_over(apply_row)
-
-        def advance(big, total, length=length, step=step):
+        length = norm / total_of(lax.fori_loop(0, HALF // 4, apply_rows, zero))
+
+        def advance(big, total, length=length):
             here = here_of(big)
-            moved = length * pad[big + 1, inner]
-            solution[here] = moved if step == 0 else solution[here] + moved
-            if step + 1 == CG_ITERS:
-                return total
             values = residual[here] - length * image[here]
             residual[here] = values
             return total + folded(values * values)
 
-        following = total_over(advance)
+        ratio = 0.0
         if step + 1 < CG_ITERS:
+            following = total_over(advance)
             ratio = following / norm
             norm = following
 
-            def turn(big, total, ratio=ratio):
-                pad[big + 1, inner] = residual[here_of(big)] + ratio * pad[big + 1, inner]
-                return total
-
-            total_over(turn)
+        def turn(big, total, length=length, ratio=ratio, step=step):
+            here = here_of(big)
+            old = pad[big + 1, inner]
+            solution[here] = length * old if step == 0 else solution[here] + length * old
+            if step + 1 < CG_ITERS:
+                pad[big + 1, inner] = residual[here] + ratio * old
+            return total
+
+        total_over(turn)
 
 
 def prolong_layer(solution, layer, target):
@@ -558,17 +573,17 @@
     return call(last_kernel, [(8, LANES)], COARSE_SCRATCH + [FINE, FINE], args, 1)[0]
 
 
-NEAR = 4
+NEAR = 8
 FAR = TILES // NEAR
 
 
 def place_of(tile):
-    return tile // 2 % NEAR * FAR + tile // (2 * NEAR) * 2 + tile % 2
+    return tile % NEAR * FAR + tile // NEAR
 
 
 def gluing_tables(glue_tile, glue_side, glue_flip):
     def lanes_of(table):
-        return table.reshape(FAR // 2, NEAR, 2, 4).transpose(3, 1, 0, 2).reshape(4, TILES)
+        return table.reshape(FAR, NEAR, 4).transpose(2, 1, 0).reshape(4, TILES)
 
     source = (lanes_of(glue_side) * TILES + place_of(lanes_of(glue_tile))).reshape(1, 4 * TILES)
     gluing = (jnp.arange(4 * TILES)[:, None] == source).astype(jnp.bfloat16)

time: 227 us -> 217 us (0.956)
  blocking collectives: 117 us -> 108 us
    all_to_all x1, blocking collectives: 61.2 us -> 51.3 us  [gather(): lax.all_to_all(sent, axis, split_axis=0, concat_axis=0, axis_index_groups...]
    ppermute x3, waiting for transfers between devices: 13.2 us -> 15.5 us  [radial(): lax.ppermute(values, ('lat', 'rad'), above)]
  transfers between devices with their start and end apart: 9 -> 9, of which waited for: 9 -> 9; matrix products, arithmetic and copies ran while one was open for 1% -> 0% of each run, Pallas kernels for 1% -> 1%
where the time goes in v6:
time: 217 us; the launch traced here: 216 us
  blocking collectives  108 us (50%)
  waiting for transfers between devices  44.5 us (21%)
  starting transfers between devices  31.4 us (14%)
  Pallas kernels  29.3 us (14%)
    all_to_all x2, blocking collectives, gather_cores(): lax.all_to_all(copies, 'rad', split_axis=0, concat_axis=0, axis_index_gro...  57.1 us
    all_to_all x1, blocking collectives, gather(): lax.all_to_all(sent, axis, split_axis=0, concat_axis=0, axis_index_groups...  51.3 us
    pallas_call x8, Pallas kernels, call(): pl.pallas_call(kernel, out_shape=shapes, in_specs=[pl.BlockSpec(memory_sp...  29.3 us
    all_to_all x1, waiting for transfers between devices, gather(): lax.all_to_all(sent, axis, split_axis=0, concat_axis=0, axis_index_groups...  17.2 us
    ppermute x3, waiting for transfers between devices, radial(): lax.ppermute(values, ('lat', 'rad'), above)  15.5 us
    ppermute x3, starting transfers between devices, radial(): lax.ppermute(values, ('lat', 'rad'), below)  10 us
    all_to_all x1, starting transfers between devices, gather(): lax.all_to_all(sent, axis, split_axis=0, concat_axis=0, axis_index_groups...  8.72 us
    ppermute x2, waiting for transfers between devices, swap_cores(): return lax.ppermute(own, 'rad', [(layer, layer ^ 1) for layer in range(NR)])  6.87 us
  transfers between devices with their start and end apart: 9, of which 9 were waited for; matrix products, arithmetic and copies ran while one was open for 0% of the time, Pallas kernels for 1%

profile of v6, /device:TPU:1, one launch (start us, length us, event | category | flops | bytes accessed | tf_op | source)
XLA Modules:
  0.0 216.4 jit_solution(15253990296149142770)
XLA Ops:
  0.1 0.7 pad_maximum_fusion
  0.8 51.3 %all_to_all.20 = f32[8,24,128]{2,1,0:T(8,128)S(1)} all-to-all(f32[8,24,128]{2,1,0:T(8,128)S(1)} %broadcast_in_dim.6), channel_id=1, replica_groups={{0,128,256,384,512,640,768,896},{16,144,272,400,528,656,784,912},{32,16..., dimensions={0} | all-to-all | bytes 196608 | tf_op jit(solution)/shard_map/all_to_all | solution.py:597
  52.1 1.0 broadcast_in_dim.16
  53.1 8.7 %all-to-all-start.1 = ((f32[8,192,128]{2,1,0:T(8,128)}), f32[8,192,128]{2,1,0:T(8,128)S(1)}, u32[]{:S(2)}, u32[]{:S(2)}) async-start(f32[8,192,128]{2,1,0:T(8,128)} %broadcast_in_dim.16), calls=%async_computation.1 | async-start | bytes 1572864 | tf_op jit(solution)/shard_map/all_to_all | solution.py:597
  62.2 0.1 mul.35
  62.6 17.2 %all-to-all-done.1 = f32[8,192,128]{2,1,0:T(8,128)S(1)} async-done(((f32[8,192,128]{2,1,0:T(8,128)}), f32[8,192,128]{2,1,0:T(8,128)S(1)}, u32[]{:S(2)}, u32[]{:S(2)}) %all-to-all-start.1) | async-done | bytes 786464 | tf_op jit(solution)/shard_map/all_to_all | solution.py:597
  79.8 0.2 shard_map.64.pair_ref
  79.9 5.4 %collective-permute-start.1 = (f32[1024,128]{1,0:T(8,128)S(1)}, f32[1024,128]{1,0:T(8,128)S(1)}, u32[]{:S(2)}, u32[]{:S(2)}) collective-permute-start(f32[1024,128]{1,0:T(8,128)S(1)} %shard_map.64.pair_ref), channel_id=1, source_target_pairs={{0,1},{1,2},{2,3},{3,20},{4,5},{5,6},{6,7},{7,24},{8,9},{9,10},{10... | collective-permute-start | bytes 1572872 | tf_op jit(solution)/shard_map/ppermute | solution.py:629
  85.4 1.9 collective-permute-start
  87.4 1.3 shard_map.65
  88.8 2.7 %collective-permute-done.1.below_ref = f32[1024,128]{1,0:T(8,128)S(1)} collective-permute-done((f32[1024,128]{1,0:T(8,128)S(1)}, f32[1024,128]{1,0:T(8,128)S(1)}, u32[]{:S(2)}, u32[]{:S(2)}) %collective-permute-start.1) | collective-permute-done | bytes 524320 | tf_op jit(solution)/shard_map/ppermute | solution.py:629
  91.5 4.4 %collective-permute-done.above_ref = f32[1024,128]{1,0:T(8,128)S(1)} collective-permute-done((f32[1024,128]{1,0:T(8,128)S(1)}, f32[1024,128]{1,0:T(8,128)S(1)}, u32[]{:S(2)}, u32[]{:S(2)}) %collective-permute-start) | collective-permute-done | bytes 524320 | tf_op jit(solution)/shard_map/ppermute | solution.py:629
  95.9 1.1 shard_map.66
  96.9 1.9 collective-permute-start.3
  98.9 2.4 %collective-permute-start.2 = (f32[512,128]{1,0:T(8,128)S(1)}, f32[512,128]{1,0:T(8,128)S(1)}, u32[]{:S(2)}, u32[]{:S(2)}) collective-permute-start(f32[512,128]{1,0:T(8,128)S(1)} %get-tuple-element.40), channel_id=1, source_target_pairs={{1,0},{2,1},{3,2},{20,3},{5,4},{6,5},{7,6},{24,7},{9,8},{10,9},{11... | collective-permute-start | bytes 786440 | tf_op jit(solution)/shard_map/ppermute | solution.py:629
  101.3 0.9 collective-permute-done.3.below_ref.smoothed_below_ref
  102.2 6.7 %collective-permute-done.2.above_ref.smoothed_above_ref = f32[512,128]{1,0:T(8,128)S(1)} collective-permute-done((f32[512,128]{1,0:T(8,128)S(1)}, f32[512,128]{1,0:T(8,128)S(1)}, u32[]{:S(2)}, u32[]{:S(2)}) %collective-permute-start.2) | collective-permute-done | bytes 262176 | tf_op jit(solution)/shard_map/ppermute | solution.py:629
  108.9 1.6 shard_map.67
  110.4 38.3 %all_to_all.21.own_ref = f32[8,656,128]{2,1,0:T(8,128)S(1)} all-to-all(f32[8,656,128]{2,1,0:T(8,128)S(1)} %shard_map.67), channel_id=1, replica_groups={{0,2,4,6,8,10,12,14},{1,3,5,7,9,11,13,15},{16,18,20,22,24,26,28,30},{17..., dimensions={0} | all-to-all | bytes 5373952 | tf_op jit(solution)/shard_map/all_to_all | solution.py:609
  148.8 3.3 %collective-permute-start.4 = (f32[8,656,128]{2,1,0:T(8,128)S(1)}, f32[8,656,128]{2,1,0:T(8,128)S(1)}, u32[]{:S(2)}, u32[]{:S(2)}) collective-permute-start(f32[8,656,128]{2,1,0:T(8,128)S(1)} %all_to_all.21.own_ref), channel_id=1, source_target_pairs={{0,1},{1,0},{2,3},{3,2},{4,5},{5,4},{6,7},{7,6},{8,9},{9,8},{10,11... | collective-permute-start | bytes 8060936 | tf_op jit(solution)/shard_map/ppermute | solution.py:613
  152.1 4.6 %collective-permute-done.4.other_ref = f32[8,656,128]{2,1,0:T(8,128)S(1)} collective-permute-done((f32[8,656,128]{2,1,0:T(8,128)S(1)}, f32[8,656,128]{2,1,0:T(8,128)S(1)}, u32[]{:S(2)}, u32[]{:S(2)}) %collective-permute-start.4) | collective-permute-done | bytes 2687008 | tf_op jit(solution)/shard_map/ppermute | solution.py:613
  156.7 3.4 %shard_map.68 = (f32[2176,128]{1,0:T(8,128)S(1)}, f32[16,136,128]{2,1,0:T(8,128)S(1)}, f32[2048,128]{1,0:T(8,128)S(1)}, f32[2048,128]{1,0:T(8,128)S(1)}, f32[2048,128]{1,0:T(8,128)S(1)}) custom-call(s32[2]{0:T(128)S(1)} %pad_add_fusion.place_ref, f32[8,656,128]{2,1,0:T(8,128)S(1)} %all_to_all.21.own_ref, f32[8,656,128]{2,1,0:T(8,128)S(1)} %collective-permute-done.4.other_ref), custom_call_target="tpu_custom_call" | custom-call | flops 25165824 | bytes 25165824 | tf_op jit(solution)/shard_map/pallas_call | solution.py:521
  160.1 10.6 %shard_map.69 = (f32[1024,128]{1,0:T(8,128)S(1)}, f32[1024,128]{1,0:T(8,128)S(1)}, f32[1024,128]{1,0:T(8,128)S(1)}, f32[512,128]{1,0:T(8,128)S(1)}) custom-call(s32[2]{0:T(128)S(1)} %pad_add_fusion.place_ref, f32[8,656,128]{2,1,0:T(8,128)S(1)} %all_to_all.21.own_ref, f32[8,656,128]{2,1,0:T(8,128)S(1)} %collective-permute-done.4.other_ref, ...), custom_call_target="tpu_custom_call" | custom-call | flops 4194304 | bytes 4194304 | tf_op jit(solution)/shard_map/pallas_call | solution.py:521
  170.7 2.7 %collective-permute-start.6 = (f32[512,128]{1,0:T(8,128)S(1)}, f32[512,128]{1,0:T(8,128)S(1)}, u32[]{:S(2)}, u32[]{:S(2)}) collective-permute-start(f32[512,128]{1,0:T(8,128)S(1)} %get-tuple-element.50), channel_id=1, source_target_pairs={{0,1},{1,2},{2,3},{3,20},{4,5},{5,6},{6,7},{7,24},{8,9},{9,10},{10... | collective-permute-start | bytes 786440 | tf_op jit(solution)/shard_map/ppermute | solution.py:629
  173.4 1.9 collective-permute-start.5
  175.3 1.4 collective-permute-done.6.below_ref
  176.7 4.4 %collective-permute-done.5.above_ref = f32[512,128]{1,0:T(8,128)S(1)} collective-permute-done((f32[512,128]{1,0:T(8,128)S(1)}, f32[512,128]{1,0:T(8,128)S(1)}, u32[]{:S(2)}, u32[]{:S(2)}) %collective-permute-start.5) | collective-permute-done | bytes 262176 | tf_op jit(solution)/shard_map/ppermute | solution.py:629
  181.1 1.5 shard_map.70
  182.6 18.8 %all_to_all.22.own_ref = f32[8,256,128]{2,1,0:T(8,128)S(1)} all-to-all(f32[8,256,128]{2,1,0:T(8,128)S(1)} %shard_map.70), channel_id=1, replica_groups={{0,2,4,6,8,10,12,14},{1,3,5,7,9,11,13,15},{16,18,20,22,24,26,28,30},{17..., dimensions={0} | all-to-all | bytes 2097152 | tf_op jit(solution)/shard_map/all_to_all | solution.py:609
  201.4 3.0 %collective-permute-start.7 = (f32[8,256,128]{2,1,0:T(8,128)S(1)}, f32[8,256,128]{2,1,0:T(8,128)S(1)}, u32[]{:S(2)}, u32[]{:S(2)}) collective-permute-start(f32[8,256,128]{2,1,0:T(8,128)S(1)} %all_to_all.22.own_ref), channel_id=1, source_target_pairs={{0,1},{1,0},{2,3},{3,2},{4,5},{5,4},{6,7},{7,6},{8,9},{9,8},{10,11... | collective-permute-start | bytes 3145736 | tf_op jit(solution)/shard_map/ppermute | solution.py:613
  204.4 2.3 %collective-permute-done.7.other_ref = f32[8,256,128]{2,1,0:T(8,128)S(1)} collective-permute-done((f32[8,256,128]{2,1,0:T(8,128)S(1)}, f32[8,256,128]{2,1,0:T(8,128)S(1)}, u32[]{:S(2)}, u32[]{:S(2)}) %collective-permute-start.7) | collective-permute-done | bytes 1048608 | tf_op jit(solution)/shard_map/ppermute | solution.py:613
  206.7 9.8 %shard_map.71 = f32[8,128]{1,0:T(8,128)} custom-call(s32[2]{0:T(128)S(1)} %pad_add_fusion.place_ref, f32[8,256,128]{2,1,0:T(8,128)S(1)} %all_to_all.22.own_ref, f32[8,256,128]{2,1,0:T(8,128)S(1)} %collective-permute-done.7.other_ref, f32[2176,128]{1,0:T(8,128)S(1)} %get-tuple-element.42.rows_ref, f32[16,136,128]{2,1,0:T(8,128)S(1)} %get-tuple-element.43.columns_ref, ...), custom_call_target="tpu_custom_call" | custom-call | flops 4194304 | bytes 4194304 | tf_op jit(solution)/shard_map/pallas_call | solution.py:521
  (21 shorter events, 0.9 us)
Async XLA Ops:
  0.0 61.8 %copy-start.1 = (s32[64,4]{0,1:T(4,128)S(1)}, s32[64,4]{0,1:T(4,128)}, u32[]{:S(2)}) copy-start(s32[64,4]{0,1:T(4,128)} %param.11) | copy-start | bytes 3076
  0.0 62.0 %copy-start.2 = (s32[64,4]{0,1:T(4,128)S(1)}, s32[64,4]{0,1:T(4,128)}, u32[]{:S(2)}) copy-start(s32[64,4]{0,1:T(4,128)} %param.10) | copy-start | bytes 3076
  0.0 62.3 %copy-start = (s32[64,4]{0,1:T(4,128)S(1)}, s32[64,4]{0,1:T(4,128)}, u32[]{:S(2)}) copy-start(s32[64,4]{0,1:T(4,128)} %param.9) | copy-start | bytes 3076
  53.1 26.7 %all-to-all-start.1 = ((f32[8,192,128]{2,1,0:T(8,128)}), f32[8,192,128]{2,1,0:T(8,128)S(1)}, u32[]{:S(2)}, u32[]{:S(2)}) async-start(f32[8,192,128]{2,1,0:T(8,128)} %broadcast_in_dim.16), calls=%async_computation.1 | async-start | bytes 1572864 | tf_op jit(solution)/shard_map/all_to_all | solution.py:597
  79.9 11.5 %collective-permute-start.1 = (f32[1024,128]{1,0:T(8,128)S(1)}, f32[1024,128]{1,0:T(8,128)S(1)}, u32[]{:S(2)}, u32[]{:S(2)}) collective-permute-start(f32[1024,128]{1,0:T(8,128)S(1)} %shard_map.64.pair_ref), channel_id=1, source_target_pairs={{0,1},{1,2},{2,3},{3,20},{4,5},{5,6},{6,7},{7,24},{8,9},{9,10},{10... | collective-permute-start | bytes 1572872 | tf_op jit(solution)/shard_map/ppermute | solution.py:629
  85.4 10.5 %collective-permute-start = (f32[1024,128]{1,0:T(8,128)S(1)}, f32[1024,128]{1,0:T(8,128)S(1)}, u32[]{:S(2)}, u32[]{:S(2)}) collective-permute-start(f32[1024,128]{1,0:T(8,128)S(1)} %shard_map.64.pair_ref), channel_id=1, source_target_pairs={{1,0},{2,1},{3,2},{20,3},{5,4},{6,5},{7,6},{24,7},{9,8},{10,9},{11... | collective-permute-start | bytes 1572872 | tf_op jit(solution)/shard_map/ppermute | solution.py:629
  96.9 5.2 %collective-permute-start.3 = (f32[512,128]{1,0:T(8,128)S(1)}, f32[512,128]{1,0:T(8,128)S(1)}, u32[]{:S(2)}, u32[]{:S(2)}) collective-permute-start(f32[512,128]{1,0:T(8,128)S(1)} %get-tuple-element.40), channel_id=1, source_target_pairs={{0,1},{1,2},{2,3},{3,20},{4,5},{5,6},{6,7},{7,24},{8,9},{9,10},{10... | collective-permute-start | bytes 786440 | tf_op jit(solution)/shard_map/ppermute | solution.py:629
  98.9 10.0 %collective-permute-start.2 = (f32[512,128]{1,0:T(8,128)S(1)}, f32[512,128]{1,0:T(8,128)S(1)}, u32[]{:S(2)}, u32[]{:S(2)}) collective-permute-start(f32[512,128]{1,0:T(8,128)S(1)} %get-tuple-element.40), channel_id=1, source_target_pairs={{1,0},{2,1},{3,2},{20,3},{5,4},{6,5},{7,6},{24,7},{9,8},{10,9},{11... | collective-permute-start | bytes 786440 | tf_op jit(solution)/shard_map/ppermute | solution.py:629
  148.8 7.9 %collective-permute-start.4 = (f32[8,656,128]{2,1,0:T(8,128)S(1)}, f32[8,656,128]{2,1,0:T(8,128)S(1)}, u32[]{:S(2)}, u32[]{:S(2)}) collective-permute-start(f32[8,656,128]{2,1,0:T(8,128)S(1)} %all_to_all.21.own_ref), channel_id=1, source_target_pairs={{0,1},{1,0},{2,3},{3,2},{4,5},{5,4},{6,7},{7,6},{8,9},{9,8},{10,11... | collective-permute-start | bytes 8060936 | tf_op jit(solution)/shard_map/ppermute | solution.py:613
  170.7 6.0 %collective-permute-start.6 = (f32[512,128]{1,0:T(8,128)S(1)}, f32[512,128]{1,0:T(8,128)S(1)}, u32[]{:S(2)}, u32[]{:S(2)}) collective-permute-start(f32[512,128]{1,0:T(8,128)S(1)} %get-tuple-element.50), channel_id=1, source_target_pairs={{0,1},{1,2},{2,3},{3,20},{4,5},{5,6},{6,7},{7,24},{8,9},{9,10},{10... | collective-permute-start | bytes 786440 | tf_op jit(solution)/shard_map/ppermute | solution.py:629
  173.4 7.7 %collective-permute-start.5 = (f32[512,128]{1,0:T(8,128)S(1)}, f32[512,128]{1,0:T(8,128)S(1)}, u32[]{:S(2)}, u32[]{:S(2)}) collective-permute-start(f32[512,128]{1,0:T(8,128)S(1)} %get-tuple-element.50), channel_id=1, source_target_pairs={{1,0},{2,1},{3,2},{20,3},{5,4},{6,5},{7,6},{24,7},{9,8},{10,9},{11... | collective-permute-start | bytes 786440 | tf_op jit(solution)/shard_map/ppermute | solution.py:629
  201.4 5.3 %collective-permute-start.7 = (f32[8,256,128]{2,1,0:T(8,128)S(1)}, f32[8,256,128]{2,1,0:T(8,128)S(1)}, u32[]{:S(2)}, u32[]{:S(2)}) collective-permute-start(f32[8,256,128]{2,1,0:T(8,128)S(1)} %all_to_all.22.own_ref), channel_id=1, source_target_pairs={{0,1},{1,0},{2,3},{3,2},{4,5},{5,4},{6,7},{7,6},{8,9},{9,8},{10,11... | collective-permute-start | bytes 3145736 | tf_op jit(solution)/shard_map/ppermute | solution.py:613

commit v7 on v6

--- a/solution.py
+++ b/solution.py
@@ -605,8 +605,17 @@
 
 
 def gather_cores(copies):
-    groups = [list(range(core, NR, 2)) for core in range(2)]
-    return lax.all_to_all(copies, "rad", split_axis=0, concat_axis=0, axis_index_groups=groups, tiled=True)
+    groups = []
+    for tile in range(TILES):
+        for core in range(2):
+            group = []
+            for chip in range(CHIPS):
+                other = tile ^ 1 if chip % 4 == 3 else tile
+                group.append(other * NR + 2 * chip + core)
+            groups.append(group)
+    return lax.all_to_all(
+        copies, ("lat", "rad"), split_axis=0, concat_axis=0, axis_index_groups=groups, tiled=True
+    )
 
 
 def swap_cores(own):

time: 217 us -> 231 us (1.065)
  blocking collectives: 108 us -> 124 us
    all_to_all x2, blocking collectives: 57.1 us -> 72.5 us  [gather_cores(): lax.all_to_all(copies, ('lat', 'rad'), split_axis=0, concat_axis=0, axis_...]
where the time goes in v7:
time: 231 us; the launch traced here: 230 us
  blocking collectives  124 us (54%)
  waiting for transfers between devices  44.9 us (19%)
  Pallas kernels  29.3 us (13%)
  starting transfers between devices  29.2 us (13%)
    all_to_all x2, blocking collectives, gather_cores(): lax.all_to_all(copies, ('lat', 'rad'), split_axis=0, concat_axis=0, axis_...  72.5 us
    all_to_all x1, blocking collectives, gather(): lax.all_to_all(sent, axis, split_axis=0, concat_axis=0, axis_index_groups...  51.3 us
    pallas_call x8, Pallas kernels, call(): pl.pallas_call(kernel, out_shape=shapes, in_specs=[pl.BlockSpec(memory_sp...  29.3 us
    all_to_all x1, waiting for transfers between devices, gather(): lax.all_to_all(sent, axis, split_axis=0, concat_axis=0, axis_index_groups...  17.2 us
    ppermute x3, waiting for transfers between devices, radial(): lax.ppermute(values, ('lat', 'rad'), above)  15.5 us
    ppermute x3, starting transfers between devices, radial(): lax.ppermute(values, ('lat', 'rad'), below)  9.81 us
    all_to_all x1, starting transfers between devices, gather(): lax.all_to_all(sent, axis, split_axis=0, concat_axis=0, axis_index_groups...  8.72 us
    ppermute x2, waiting for transfers between devices, swap_cores(): return lax.ppermute(own, 'rad', [(layer, layer ^ 1) for layer in range(NR)])  7.23 us
  transfers between devices with their start and end apart: 9, of which 9 were waited for; matrix products, arithmetic and copies ran while one was open for 0% of the time, Pallas kernels for 1%

profile of v7, /device:TPU:1, one launch (start us, length us, event | category | flops | bytes accessed | tf_op | source)
XLA Modules:
  0.0 230.0 jit_solution(13373462821255673751)
XLA Ops:
  0.1 0.7 pad_maximum_fusion
  0.8 51.3 %all_to_all.20 = f32[8,24,128]{2,1,0:T(8,128)S(1)} all-to-all(f32[8,24,128]{2,1,0:T(8,128)S(1)} %broadcast_in_dim.6), channel_id=1, replica_groups={{0,128,256,384,512,640,768,896},{16,144,272,400,528,656,784,912},{32,16..., dimensions={0} | all-to-all | bytes 196608 | tf_op jit(solution)/shard_map/all_to_all | solution.py:597
  52.1 1.0 broadcast_in_dim.16
  53.1 8.7 %all-to-all-start.1 = ((f32[8,192,128]{2,1,0:T(8,128)}), f32[8,192,128]{2,1,0:T(8,128)S(1)}, u32[]{:S(2)}, u32[]{:S(2)}) async-start(f32[8,192,128]{2,1,0:T(8,128)} %broadcast_in_dim.16), calls=%async_computation.1 | async-start | bytes 1572864 | tf_op jit(solution)/shard_map/all_to_all | solution.py:597
  62.2 0.1 mul.35
  62.6 17.2 %all-to-all-done.1 = f32[8,192,128]{2,1,0:T(8,128)S(1)} async-done(((f32[8,192,128]{2,1,0:T(8,128)}), f32[8,192,128]{2,1,0:T(8,128)S(1)}, u32[]{:S(2)}, u32[]{:S(2)}) %all-to-all-start.1) | async-done | bytes 786464 | tf_op jit(solution)/shard_map/all_to_all | solution.py:597
  79.8 0.2 shard_map.64.pair_ref
  79.9 5.4 %collective-permute-start.1 = (f32[1024,128]{1,0:T(8,128)S(1)}, f32[1024,128]{1,0:T(8,128)S(1)}, u32[]{:S(2)}, u32[]{:S(2)}) collective-permute-start(f32[1024,128]{1,0:T(8,128)S(1)} %shard_map.64.pair_ref), channel_id=1, source_target_pairs={{0,1},{1,2},{2,3},{3,20},{4,5},{5,6},{6,7},{7,24},{8,9},{9,10},{10... | collective-permute-start | bytes 1572872 | tf_op jit(solution)/shard_map/ppermute | solution.py:638
  85.4 1.9 collective-permute-start
  87.4 1.3 shard_map.65
  88.8 2.7 %collective-permute-done.1.below_ref = f32[1024,128]{1,0:T(8,128)S(1)} collective-permute-done((f32[1024,128]{1,0:T(8,128)S(1)}, f32[1024,128]{1,0:T(8,128)S(1)}, u32[]{:S(2)}, u32[]{:S(2)}) %collective-permute-start.1) | collective-permute-done | bytes 524320 | tf_op jit(solution)/shard_map/ppermute | solution.py:638
  91.5 4.4 %collective-permute-done.above_ref = f32[1024,128]{1,0:T(8,128)S(1)} collective-permute-done((f32[1024,128]{1,0:T(8,128)S(1)}, f32[1024,128]{1,0:T(8,128)S(1)}, u32[]{:S(2)}, u32[]{:S(2)}) %collective-permute-start) | collective-permute-done | bytes 524320 | tf_op jit(solution)/shard_map/ppermute | solution.py:638
  95.9 1.1 shard_map.66
  96.9 1.9 collective-permute-start.3
  98.9 2.4 %collective-permute-start.2 = (f32[512,128]{1,0:T(8,128)S(1)}, f32[512,128]{1,0:T(8,128)S(1)}, u32[]{:S(2)}, u32[]{:S(2)}) collective-permute-start(f32[512,128]{1,0:T(8,128)S(1)} %get-tuple-element.40), channel_id=1, source_target_pairs={{1,0},{2,1},{3,2},{20,3},{5,4},{6,5},{7,6},{24,7},{9,8},{10,9},{11... | collective-permute-start | bytes 786440 | tf_op jit(solution)/shard_map/ppermute | solution.py:638
  101.3 0.9 collective-permute-done.3.below_ref.smoothed_below_ref
  102.2 6.7 %collective-permute-done.2.above_ref.smoothed_above_ref = f32[512,128]{1,0:T(8,128)S(1)} collective-permute-done((f32[512,128]{1,0:T(8,128)S(1)}, f32[512,128]{1,0:T(8,128)S(1)}, u32[]{:S(2)}, u32[]{:S(2)}) %collective-permute-start.2) | collective-permute-done | bytes 262176 | tf_op jit(solution)/shard_map/ppermute | solution.py:638
  108.9 1.6 shard_map.67
  110.4 51.7 %all_to_all.21.own_ref = f32[8,656,128]{2,1,0:T(8,128)S(1)} all-to-all(f32[8,656,128]{2,1,0:T(8,128)S(1)} %shard_map.67), channel_id=1, replica_groups={{0,2,4,22,8,10,12,30},{1,3,5,23,9,11,13,31},{16,18,20,6,24,26,28,14},{1..., dimensions={0} | all-to-all | bytes 5373952 | tf_op jit(solution)/shard_map/all_to_all | solution.py:616
  162.1 1.9 collective-permute-start.4
  164.0 5.0 %collective-permute-done.4.other_ref = f32[8,656,128]{2,1,0:T(8,128)S(1)} collective-permute-done((f32[8,656,128]{2,1,0:T(8,128)S(1)}, f32[8,656,128]{2,1,0:T(8,128)S(1)}, u32[]{:S(2)}, u32[]{:S(2)}) %collective-permute-start.4) | collective-permute-done | bytes 2687008 | tf_op jit(solution)/shard_map/ppermute | solution.py:622
  169.0 3.4 %shard_map.68 = (f32[2176,128]{1,0:T(8,128)S(1)}, f32[16,136,128]{2,1,0:T(8,128)S(1)}, f32[2048,128]{1,0:T(8,128)S(1)}, f32[2048,128]{1,0:T(8,128)S(1)}, f32[2048,128]{1,0:T(8,128)S(1)}) custom-call(s32[2]{0:T(128)S(1)} %pad_add_fusion.place_ref, f32[8,656,128]{2,1,0:T(8,128)S(1)} %all_to_all.21.own_ref, f32[8,656,128]{2,1,0:T(8,128)S(1)} %collective-permute-done.4.other_ref), custom_call_target="tpu_custom_call" | custom-call | flops 25165824 | bytes 25165824 | tf_op jit(solution)/shard_map/pallas_call | solution.py:521
  172.4 10.6 %shard_map.69 = (f32[1024,128]{1,0:T(8,128)S(1)}, f32[1024,128]{1,0:T(8,128)S(1)}, f32[1024,128]{1,0:T(8,128)S(1)}, f32[512,128]{1,0:T(8,128)S(1)}) custom-call(s32[2]{0:T(128)S(1)} %pad_add_fusion.place_ref, f32[8,656,128]{2,1,0:T(8,128)S(1)} %all_to_all.21.own_ref, f32[8,656,128]{2,1,0:T(8,128)S(1)} %collective-permute-done.4.other_ref, ...), custom_call_target="tpu_custom_call" | custom-call | flops 4194304 | bytes 4194304 | tf_op jit(solution)/shard_map/pallas_call | solution.py:521
  183.0 2.5 %collective-permute-start.6 = (f32[512,128]{1,0:T(8,128)S(1)}, f32[512,128]{1,0:T(8,128)S(1)}, u32[]{:S(2)}, u32[]{:S(2)}) collective-permute-start(f32[512,128]{1,0:T(8,128)S(1)} %get-tuple-element.50), channel_id=1, source_target_pairs={{0,1},{1,2},{2,3},{3,20},{4,5},{5,6},{6,7},{7,24},{8,9},{9,10},{10... | collective-permute-start | bytes 786440 | tf_op jit(solution)/shard_map/ppermute | solution.py:638
  185.5 1.9 collective-permute-start.5
  187.4 1.4 collective-permute-done.6.below_ref
  188.8 4.4 %collective-permute-done.5.above_ref = f32[512,128]{1,0:T(8,128)S(1)} collective-permute-done((f32[512,128]{1,0:T(8,128)S(1)}, f32[512,128]{1,0:T(8,128)S(1)}, u32[]{:S(2)}, u32[]{:S(2)}) %collective-permute-start.5) | collective-permute-done | bytes 262176 | tf_op jit(solution)/shard_map/ppermute | solution.py:638
  193.2 1.5 shard_map.70
  194.6 20.9 %all_to_all.22.own_ref = f32[8,256,128]{2,1,0:T(8,128)S(1)} all-to-all(f32[8,256,128]{2,1,0:T(8,128)S(1)} %shard_map.70), channel_id=1, replica_groups={{0,2,4,22,8,10,12,30},{1,3,5,23,9,11,13,31},{16,18,20,6,24,26,28,14},{1..., dimensions={0} | all-to-all | bytes 2097152 | tf_op jit(solution)/shard_map/all_to_all | solution.py:616
  215.5 2.5 %collective-permute-start.7 = (f32[8,256,128]{2,1,0:T(8,128)S(1)}, f32[8,256,128]{2,1,0:T(8,128)S(1)}, u32[]{:S(2)}, u32[]{:S(2)}) collective-permute-start(f32[8,256,128]{2,1,0:T(8,128)S(1)} %all_to_all.22.own_ref), channel_id=1, source_target_pairs={{0,1},{1,0},{2,3},{3,2},{4,5},{5,4},{6,7},{7,6},{8,9},{9,8},{10,11... | collective-permute-start | bytes 3145736 | tf_op jit(solution)/shard_map/ppermute | solution.py:622
  218.0 2.3 collective-permute-done.7.other_ref
  220.3 9.8 %shard_map.71 = f32[8,128]{1,0:T(8,128)} custom-call(s32[2]{0:T(128)S(1)} %pad_add_fusion.place_ref, f32[8,256,128]{2,1,0:T(8,128)S(1)} %all_to_all.22.own_ref, f32[8,256,128]{2,1,0:T(8,128)S(1)} %collective-permute-done.7.other_ref, f32[2176,128]{1,0:T(8,128)S(1)} %get-tuple-element.42.rows_ref, f32[16,136,128]{2,1,0:T(8,128)S(1)} %get-tuple-element.43.columns_ref, ...), custom_call_target="tpu_custom_call" | custom-call | flops 4194304 | bytes 4194304 | tf_op jit(solution)/shard_map/pallas_call | solution.py:521
  (21 shorter events, 0.9 us)
Async XLA Ops:
  0.0 61.8 %copy-start.1 = (s32[64,4]{0,1:T(4,128)S(1)}, s32[64,4]{0,1:T(4,128)}, u32[]{:S(2)}) copy-start(s32[64,4]{0,1:T(4,128)} %param.11) | copy-start | bytes 3076
  0.0 62.0 %copy-start.2 = (s32[64,4]{0,1:T(4,128)S(1)}, s32[64,4]{0,1:T(4,128)}, u32[]{:S(2)}) copy-start(s32[64,4]{0,1:T(4,128)} %param.10) | copy-start | bytes 3076
  0.0 62.3 %copy-start = (s32[64,4]{0,1:T(4,128)S(1)}, s32[64,4]{0,1:T(4,128)}, u32[]{:S(2)}) copy-start(s32[64,4]{0,1:T(4,128)} %param.9) | copy-start | bytes 3076
  53.1 26.7 %all-to-all-start.1 = ((f32[8,192,128]{2,1,0:T(8,128)}), f32[8,192,128]{2,1,0:T(8,128)S(1)}, u32[]{:S(2)}, u32[]{:S(2)}) async-start(f32[8,192,128]{2,1,0:T(8,128)} %broadcast_in_dim.16), calls=%async_computation.1 | async-start | bytes 1572864 | tf_op jit(solution)/shard_map/all_to_all | solution.py:597
  79.9 11.5 %collective-permute-start.1 = (f32[1024,128]{1,0:T(8,128)S(1)}, f32[1024,128]{1,0:T(8,128)S(1)}, u32[]{:S(2)}, u32[]{:S(2)}) collective-permute-start(f32[1024,128]{1,0:T(8,128)S(1)} %shard_map.64.pair_ref), channel_id=1, source_target_pairs={{0,1},{1,2},{2,3},{3,20},{4,5},{5,6},{6,7},{7,24},{8,9},{9,10},{10... | collective-permute-start | bytes 1572872 | tf_op jit(solution)/shard_map/ppermute | solution.py:638
  85.4 10.5 %collective-permute-start = (f32[1024,128]{1,0:T(8,128)S(1)}, f32[1024,128]{1,0:T(8,128)S(1)}, u32[]{:S(2)}, u32[]{:S(2)}) collective-permute-start(f32[1024,128]{1,0:T(8,128)S(1)} %shard_map.64.pair_ref), channel_id=1, source_target_pairs={{1,0},{2,1},{3,2},{20,3},{5,4},{6,5},{7,6},{24,7},{9,8},{10,9},{11... | collective-permute-start | bytes 1572872 | tf_op jit(solution)/shard_map/ppermute | solution.py:638
  96.9 5.2 %collective-permute-start.3 = (f32[512,128]{1,0:T(8,128)S(1)}, f32[512,128]{1,0:T(8,128)S(1)}, u32[]{:S(2)}, u32[]{:S(2)}) collective-permute-start(f32[512,128]{1,0:T(8,128)S(1)} %get-tuple-element.40), channel_id=1, source_target_pairs={{0,1},{1,2},{2,3},{3,20},{4,5},{5,6},{6,7},{7,24},{8,9},{9,10},{10... | collective-permute-start | bytes 786440 | tf_op jit(solution)/shard_map/ppermute | solution.py:638
  98.9 10.0 %collective-permute-start.2 = (f32[512,128]{1,0:T(8,128)S(1)}, f32[512,128]{1,0:T(8,128)S(1)}, u32[]{:S(2)}, u32[]{:S(2)}) collective-permute-start(f32[512,128]{1,0:T(8,128)S(1)} %get-tuple-element.40), channel_id=1, source_target_pairs={{1,0},{2,1},{3,2},{20,3},{5,4},{6,5},{7,6},{24,7},{9,8},{10,9},{11... | collective-permute-start | bytes 786440 | tf_op jit(solution)/shard_map/ppermute | solution.py:638
  162.1 6.9 %collective-permute-start.4 = (f32[8,656,128]{2,1,0:T(8,128)S(1)}, f32[8,656,128]{2,1,0:T(8,128)S(1)}, u32[]{:S(2)}, u32[]{:S(2)}) collective-permute-start(f32[8,656,128]{2,1,0:T(8,128)S(1)} %all_to_all.21.own_ref), channel_id=1, source_target_pairs={{0,1},{1,0},{2,3},{3,2},{4,5},{5,4},{6,7},{7,6},{8,9},{9,8},{10,11... | collective-permute-start | bytes 8060936 | tf_op jit(solution)/shard_map/ppermute | solution.py:622
  183.0 5.8 %collective-permute-start.6 = (f32[512,128]{1,0:T(8,128)S(1)}, f32[512,128]{1,0:T(8,128)S(1)}, u32[]{:S(2)}, u32[]{:S(2)}) collective-permute-start(f32[512,128]{1,0:T(8,128)S(1)} %get-tuple-element.50), channel_id=1, source_target_pairs={{0,1},{1,2},{2,3},{3,20},{4,5},{5,6},{6,7},{7,24},{8,9},{9,10},{10... | collective-permute-start | bytes 786440 | tf_op jit(solution)/shard_map/ppermute | solution.py:638
  185.5 7.7 %collective-permute-start.5 = (f32[512,128]{1,0:T(8,128)S(1)}, f32[512,128]{1,0:T(8,128)S(1)}, u32[]{:S(2)}, u32[]{:S(2)}) collective-permute-start(f32[512,128]{1,0:T(8,128)S(1)} %get-tuple-element.50), channel_id=1, source_target_pairs={{1,0},{2,1},{3,2},{20,3},{5,4},{6,5},{7,6},{24,7},{9,8},{10,9},{11... | collective-permute-start | bytes 786440 | tf_op jit(solution)/shard_map/ppermute | solution.py:638
  215.5 4.8 %collective-permute-start.7 = (f32[8,256,128]{2,1,0:T(8,128)S(1)}, f32[8,256,128]{2,1,0:T(8,128)S(1)}, u32[]{:S(2)}, u32[]{:S(2)}) collective-permute-start(f32[8,256,128]{2,1,0:T(8,128)S(1)} %all_to_all.22.own_ref), channel_id=1, source_target_pairs={{0,1},{1,0},{2,3},{3,2},{4,5},{5,4},{6,7},{7,6},{8,9},{9,8},{10,11... | collective-permute-start | bytes 3145736 | tf_op jit(solution)/shard_map/ppermute | solution.py:622
